TPU v7x, 512 devices: a whole 4x4x16 slice. The times are simulated.
512 devices in a mesh: pop: 64 (over y_lo, z, core), shard: 8 (over x, y_hi).
Axes of the slice: x: 4, y: 4 (y_hi: 2, y_lo: 2; y = y_hi * 2 + y_lo), z: 16, core: 2. Of those that a mesh axis runs over, the one named last changes fastest.
Arguments:
- hidden: bfloat16 [8192, 4096], P('pop'), may hold values from -6 to 6
- weight: bfloat16 [4096, 14336], P('pop', 'shard'), may hold values from -0.09375 to 0.09375
- left_factors: bfloat16 [512, 4096], P('pop'), may hold values from -6 to 6
- right_factors: bfloat16 [512, 14336], P('pop', 'shard'), may hold values from -6 to 6
- target: bfloat16 [8192, 14336], P('pop', 'shard'), may hold values from -6 to 6
Outputs:
- up_out: bfloat16 [8192, 14336], P('pop', 'shard')
- step: float32 [4096, 14336], P('pop', 'shard')
- fitness: float32 [512], P('pop')
All inputs are finite; a program needn't handle non-finite values.
Results may differ from a plain program's by a relative error of at most 0.001.
Values may be sent and summed in bfloat16 or wider, within the bound.
No kernel may reach another device: no remote copies, remote signals or barrier semaphores. Data moves between devices by JAX's collectives and lax.ppermute only.
A program may use at most 64 MiB of HBM per device.

v0:
```python
import math

import jax
import jax.numpy as jnp
from jax import lax
from jax.sharding import PartitionSpec as P

noise_scale = 0.5
spread_eps = 1e-05


def split_parts(values):
    high = values.astype(jnp.bfloat16)
    kept = lax.optimization_barrier(high)
    low = (values - kept.astype(jnp.float32)).astype(jnp.bfloat16)
    return (high, low)


def local(hidden, weight, left_factors, right_factors, target):
    local_members = left_factors.shape[0]
    row_count = hidden.shape[0]
    token_count = row_count // local_members
    feature_count = hidden.shape[1]
    local_cols = weight.shape[1]
    member_count = local_members * lax.axis_size("pop")
    base_out = jnp.dot(
        hidden,
        lax.all_gather(weight, "pop", axis=0, tiled=True),
        preferred_element_type=jnp.float32,
    )
    grouped = hidden.reshape(local_members, token_count, feature_count)
    projected = jnp.einsum(
        "mtd,md->mt", grouped, left_factors, preferred_element_type=jnp.float32
    ) / math.sqrt(feature_count)
    right_wide = right_factors.astype(jnp.float32)
    perturbed = (
        base_out.reshape(local_members, token_count, local_cols)
        + noise_scale * projected[:, :, None] * right_wide[:, None, :]
    )
    up_out = perturbed.astype(jnp.bfloat16).reshape(row_count, local_cols)
    directions = target.reshape(local_members, token_count, local_cols).astype(jnp.float32)
    partial_value = jnp.sum(jax.nn.silu(perturbed) * directions, axis=(1, 2))
    reward = lax.psum(partial_value, "shard")
    mean_reward = lax.psum(jnp.sum(reward), "pop") / member_count
    centered = reward - mean_reward
    spread = lax.psum(jnp.sum(centered * centered), "pop") / member_count
    fitness = (reward - mean_reward) / jnp.sqrt(spread + spread_eps)
    weighted = left_factors.astype(jnp.float32) * fitness[:, None]
    weighted_all = lax.all_to_all(weighted, "pop", split_axis=1, concat_axis=0, tiled=True)
    weighted_high, weighted_low = split_parts(weighted_all)
    contract = (((0,), (0,)), ((), ()))
    portion = lax.all_gather(right_factors, "pop", axis=0, tiled=True)
    upper = lax.dot_general(weighted_high, portion, contract, preferred_element_type=jnp.float32)
    lower = lax.dot_general(weighted_low, portion, contract, preferred_element_type=jnp.float32)
    summed = upper + lower
    step = summed / math.sqrt(member_count)
    return (up_out, step, fitness)


def solution(mesh):
    in_specs = (
        P("pop", None),
        P("pop", "shard"),
        P("pop", None),
        P("pop", "shard"),
        P("pop", "shard"),
    )
    out_specs = (P("pop", "shard"), P("pop", "shard"), P("pop"))
    return jax.shard_map(local, mesh=mesh, in_specs=in_specs, out_specs=out_specs, check_vma=False)
```

profile of v0, /device:TPU:1, one launch (start us, length us, event | category | flops | bytes accessed | tf_op | source)
XLA Modules:
  0.0 432.2 jit_solution(2508791868741130458)
XLA Ops:
  7.2 0.0 copy-start
  7.2 0.0 copy-start.4
  7.2 0.0 all-gather.3.cloned.1.call-start
  7.2 0.7 all-gather.3.cloned.1.call-update
  7.9 0.0 all-gather.5.cloned.1.call-start
  8.0 0.7 all-gather.5.cloned.1.call-update
  8.7 0.8 convert_element_type.23
  9.4 0.0 copy-done
  9.4 1.3 fusion.3
  10.8 0.1 mul.48
  10.8 0.1 bitcast_multiply_fusion
  11.0 0.0 copy-start.2
  11.0 142.6 %all-gather.3.cloned.1.call-done = bf16[4096,1792]{1,0:T(8,128)(2,1)} async-done(((bf16[64,1792]{1,0:T(8,128)(2,1)}), bf16[4096,1792]{1,0:T(8,128)(2,1)}) %all-gather.3.cloned.1.call-update) | async-done | bytes 14680080 | tf_op jit(solution)/shard_map/all_gather | solution.py:28
  153.6 0.0 copy-done.4
  153.6 8.3 %multiply_reduce_fusion = (f32[128]{0:T(128)S(1)}, bf16[128,1792]{1,0:T(8,128)(2,1)}) fusion(bf16[128,1792]{1,0:T(8,128)(2,1)S(1)} %copy-done.4, f32[128,1792]{1,0:T(8,128)S(1)} %bitcast_multiply_fusion, bf16[128,4096]{1,0:T(8,128)(2,1)S(1)} %copy-done, bf16[4096,1792]{1,0:T(8,128)(2,1)} %all-gather.3.cloned.1.call-done), kind=kOutput, calls=%fused_computation.4 | convolution fusion | flops 1881112448 | bytes 17564160 | tf_op jit(solution)/shard_map/dot_general | solution.py:26
  161.9 0.1 reduce_sum.35
  161.9 0.1 reduce_sum.36
  162.1 20.1 %psum.21 = f32[8]{0:T(128)S(1)} all-reduce(f32[8]{0:T(128)S(1)} %reduce_sum.36), channel_id=1, replica_groups=mesh['pop'=64,'shard'=8] {'shard'}, use_global_device_ids=true, to_apply=%region_2.3 | all-reduce | flops 8 | bytes 64 | tf_op jit(solution)/shard_map/psum | solution.py:43
  182.2 0.6 reduce_sum.37
  182.8 108.7 %psum.22 = f32[]{:T(128)} all-reduce(f32[]{:T(128)} %reduce_sum.37), channel_id=1, replica_groups=mesh['pop'=64,'shard'=8] {'pop'}, use_global_device_ids=true, to_apply=%region_4.5 | all-reduce | flops 1 | bytes 8 | tf_op jit(solution)/shard_map/psum | solution.py:44
  292.1 0.6 multiply_reduce_fusion.1
  292.7 105.3 %psum.23 = f32[]{:T(128)} all-reduce(f32[]{:T(128)} %multiply_reduce_fusion.1), channel_id=1, replica_groups=mesh['pop'=64,'shard'=8] {'pop'}, use_global_device_ids=true, to_apply=%region_6.7 | all-reduce | flops 1 | bytes 8 | tf_op jit(solution)/shard_map/psum | solution.py:46
  398.7 0.0 copy-done.2
  398.7 0.0 copy-start.3
  398.8 0.1 convert_multiply_fusion
  398.8 0.1 all_to_all.14
  398.9 0.2 copy.14
  399.1 0.2 reshape.28
  399.3 21.1 %all_to_all.19 = f32[64,1,512]{2,1,0:T(1,128)S(1)} all-to-all(f32[64,1,512]{2,1,0:T(1,128)S(1)} %reshape.28), channel_id=1, replica_groups=mesh['pop'=64,'shard'=8] {'pop'}, dimensions={0} | all-to-all | bytes 262144 | tf_op jit(solution)/shard_map/all_to_all | solution.py:49
  420.4 0.5 broadcast.14
  420.9 1.0 reduce.2
  421.9 0.1 reshape.29
  422.0 0.0 all-gather.5.cloned.1.call-done
  422.0 0.0 copy-start.1
  422.0 2.1 fusion.6
  424.1 0.0 copy-done.3
  424.1 0.0 copy-done.1
  424.2 1.2 fusion
  (3 shorter events, 0.0 us)
Async XLA Ops:
  7.2 2.3 copy-start
  7.2 146.4 %copy-start.4 = (bf16[128,1792]{1,0:T(8,128)(2,1)S(1)}, bf16[128,1792]{1,0:T(8,128)(2,1)}, u32[]{:S(2)}) copy-start(bf16[128,1792]{1,0:T(8,128)(2,1)} %param.9) | copy-start | bytes 1376260
  7.2 146.4 %all-gather.3.cloned.1.call-start = ((), (), s32[]{:S(2)}) async-start(), calls=%async_computation.1 | async-start | bytes 14909440 | tf_op jit(solution)/shard_map/all_gather | solution.py:28
  7.9 414.1 %all-gather.5.cloned.1.call-start = ((), (), s32[]{:S(2)}) async-start(), calls=%async_computation.2 | async-start | bytes 1863680 | tf_op jit(solution)/shard_map/all_gather | solution.py:52
  11.0 387.7 %copy-start.2 = (bf16[8,4096]{1,0:T(8,128)(2,1)S(1)}, bf16[8,4096]{1,0:T(8,128)(2,1)}, u32[]{:S(2)}) copy-start(bf16[8,4096]{1,0:T(8,128)(2,1)} %param.7) | copy-start | bytes 196612
  398.7 25.4 %copy-start.3 = (f32[8]{0:T(128)}, f32[8]{0:T(128)S(1)}, u32[]{:S(2)}) copy-start(f32[8]{0:T(128)S(1)} %subtract_divide_fusion) | copy-start | bytes 100
  422.0 2.1 copy-start.1
Sparse Core Ops, SparseCore 0:
  10.2 143.3 all-gather.2
  155.7 118.4 all-gather.4
where the time goes:
time: 433 us; the launch traced here: 432 us
  blocking collectives  255 us (59%)
  waiting for transfers between devices  144 us (33%)
  between operations  15.5 us (4%)
  matrix products  12.9 us (3%)
    all_gather x1, waiting for transfers between devices, local(): lax.all_gather(weight, 'pop', axis=0, tiled=True)  143 us
    psum x1, blocking collectives, local(): mean_reward = lax.psum(jnp.sum(reward), 'pop') / member_count  109 us
    psum x1, blocking collectives, local(): spread = lax.psum(jnp.sum(centered * centered), 'pop') / member_count  105 us
    all_to_all x1, blocking collectives, local(): lax.all_to_all(weighted, 'pop', split_axis=1, concat_axis=0, tiled=True)  21.1 us
    psum x1, blocking collectives, local(): reward = lax.psum(partial_value, 'shard')  20.1 us
  transfers between devices with their start and end apart: 2, of which 1 were waited for; matrix products, arithmetic and copies ran while one was open for 3% of the time, Pallas kernels for 0%

commit v1 on v0

v1 whole, which is shorter than its diff:
```python
import math

import jax
import jax.numpy as jnp
from jax import lax
from jax.experimental import pallas as pl
from jax.experimental.pallas import tpu as pltpu
from jax.sharding import Mesh, PartitionSpec as P

noise_scale = 0.5
spread_eps = 1e-05
AXES = ("ylo", "z", "core", "x", "yhi")
SIZES = (2, 16, 2, 4, 2)
SWAP = [(0, 1), (1, 0)]


def project_kernel(gathered, hidden, target, right, projected, up, reward, total):
    i = pl.program_id(0)

    @pl.when(i == 0)
    def _():
        total[...] = jnp.zeros_like(total)

    slabs, _, cols = gathered.shape
    block = gathered[:, :128, :].reshape(slabs * 128, cols)
    total[...] += jnp.dot(hidden[...], block, preferred_element_type=jnp.float32)

    @pl.when(i == pl.num_programs(0) - 1)
    def _():
        rows = total.shape[0]
        members = right.shape[0]
        tokens = rows // members
        base = total[...].reshape(members, tokens, cols)
        factor = right[...].astype(jnp.float32)
        value = base + projected[...].reshape(members, tokens, 1) * factor[:, None, :]
        up[...] = value.reshape(rows, cols).astype(jnp.bfloat16)
        aim = target[...].astype(jnp.float32).reshape(members, tokens, cols)
        gain = value / (1.0 + jnp.exp(-value)) * aim
        summed = jnp.sum(jnp.sum(gain, axis=1), axis=-1, keepdims=True)
        reward[...] = jnp.broadcast_to(summed, reward.shape)


def project(gathered, hidden, target, right, projected):
    blocks, depth, cols = gathered.shape
    rows = hidden.shape[0]
    members = right.shape[0]
    slabs = 4
    whole = lambda *shape: pl.BlockSpec(shape, lambda i: (0,) * len(shape))
    return pl.pallas_call(
        project_kernel,
        grid=(blocks // slabs,),
        in_specs=[
            pl.BlockSpec((slabs, depth, cols), lambda i: (i, 0, 0)),
            pl.BlockSpec((rows, slabs * 128), lambda i: (0, i)),
            whole(rows, cols),
            whole(members, cols),
            whole(rows, 1),
        ],
        out_specs=[whole(rows, cols), whole(members, 128)],
        out_shape=[
            jax.ShapeDtypeStruct((rows, cols), jnp.bfloat16),
            jax.ShapeDtypeStruct((members, 128), jnp.float32),
        ],
        scratch_shapes=[pltpu.VMEM((rows, cols), jnp.float32)],
        compiler_params=pltpu.CompilerParams(vmem_limit_bytes=40 * 1024 * 1024),
        cost_estimate=pl.CostEstimate(
            flops=2 * rows * blocks * 128 * cols,
            bytes_accessed=blocks * depth * cols * 2,
            transcendentals=rows * cols,
        ),
    )(gathered, hidden, target, right, projected)


def step_kernel(left, fitness, right, out):
    weighted = left[...].astype(jnp.float32) * fitness[...]
    high = weighted.astype(jnp.bfloat16)
    low = (weighted - high.astype(jnp.float32)).astype(jnp.bfloat16)
    both = jnp.concatenate([high, low], axis=0)
    product = jnp.dot(both, right[...], preferred_element_type=jnp.float32)
    rows = left.shape[0]
    out[...] = (product[:rows] + product[rows:]) * (1.0 / math.sqrt(left.shape[1]))


def step_product(left, fitness, right):
    rows, members = left.shape
    cols = right.shape[1]
    width = 256
    return pl.pallas_call(
        step_kernel,
        grid=(cols // width,),
        in_specs=[
            pl.BlockSpec((rows, members), lambda j: (0, 0)),
            pl.BlockSpec((1, members), lambda j: (0, 0)),
            pl.BlockSpec((members, width), lambda j: (0, j)),
        ],
        out_specs=pl.BlockSpec((rows, width), lambda j: (0, j)),
        out_shape=jax.ShapeDtypeStruct((rows, cols), jnp.float32),
        compiler_params=pltpu.CompilerParams(vmem_limit_bytes=40 * 1024 * 1024),
        cost_estimate=pl.CostEstimate(
            flops=4 * rows * members * cols,
            bytes_accessed=members * cols * 2 + rows * cols * 4,
            transcendentals=0,
        ),
    )(left, fitness, right)


def local(hidden, weight, left_factors, right_factors, target):
    members, features = left_factors.shape
    rows = hidden.shape[0]
    tokens = rows // members
    depth, cols = weight.shape
    half = cols // 2
    ylo = lax.axis_index("ylo")
    z = lax.axis_index("z")
    core = lax.axis_index("core")

    def own(a):
        return lax.dynamic_slice_in_dim(a, ylo * half, half, axis=1)

    def other(a):
        return lax.dynamic_slice_in_dim(a, (1 - ylo) * half, half, axis=1)

    slab = jnp.concatenate([weight, right_factors], axis=0)
    slab_own = own(slab)
    slab_recv = lax.ppermute(other(slab), "ylo", SWAP)
    right_local = jnp.concatenate([slab_own[depth:], slab_recv[depth:]], axis=0)
    packed = jnp.concatenate([slab_own[:depth], slab_recv[:depth], right_local], axis=0)
    gathered = lax.all_gather(packed, ("z", "core"), axis=0, tiled=False)

    after, hidden_b, left_b, target_b = lax.optimization_barrier(
        (packed, hidden, left_factors, target)
    )
    rows_recv = lax.ppermute(hidden_b, "ylo", SWAP)
    target_recv = lax.ppermute(other(target_b), "ylo", SWAP)
    projected_own = (
        jnp.einsum(
            "mtd,md->mt",
            hidden_b.reshape(members, tokens, features),
            left_b,
            preferred_element_type=jnp.float32,
        ).reshape(rows, 1)
        * (noise_scale / math.sqrt(features))
    )
    projected_recv = lax.ppermute(projected_own, "ylo", SWAP)
    projected = jnp.concatenate([projected_own, projected_recv], axis=0)
    target_all = jnp.concatenate([own(target_b), target_recv], axis=0)
    hidden_all = jnp.concatenate([hidden_b, rows_recv], axis=0)
    spread_rows = hidden_all.reshape(2 * rows, 2, features // (2 * depth), depth)
    spread_rows = jnp.where(ylo == 0, spread_rows, spread_rows[:, ::-1])
    hidden_all = spread_rows.transpose(0, 2, 1, 3).reshape(2 * rows, features)

    left_split = left_b.reshape(members, features // depth, depth).transpose(1, 0, 2)
    left_all = lax.all_to_all(left_split, ("ylo", "z", "core"), 0, 0, tiled=True)
    left_all = left_all.reshape(2, features // (2 * depth), members, depth)
    left_all = jnp.where(ylo == 0, left_all, left_all[::-1])
    left_all = left_all.transpose(3, 1, 0, 2).reshape(depth, -1)

    up, reward_rows = project(gathered, hidden_all, target_all, right_local, projected)

    up_recv = lax.ppermute(up[rows:], "ylo", SWAP)
    up_own = up[:rows]
    up_out = jnp.where(
        ylo == 0,
        jnp.concatenate([up_own, up_recv], axis=1),
        jnp.concatenate([up_recv, up_own], axis=1),
    )
    portion = gathered[:, 2 * depth :]
    portion_recv = lax.ppermute(
        jnp.concatenate([portion[:, members:], portion[:, :members]], axis=1), "ylo", SWAP
    )
    portion = portion.reshape(-1, half)
    portion_recv = portion_recv.reshape(-1, half)
    right_all = jnp.where(
        ylo == 0,
        jnp.concatenate([portion, portion_recv], axis=1),
        jnp.concatenate([portion_recv, portion], axis=1),
    )

    part = reward_rows[:, 0].reshape(2, members)
    part = jnp.where(ylo == 0, part, part[::-1]).reshape(1, 2 * members)
    near = lax.all_to_all(
        jnp.broadcast_to(part, (32, 2 * members)), ("ylo", "core", "x", "yhi"), 0, 0, tiled=True
    )
    near = near.reshape(2, 2, 8, 2 * members).sum(axis=(0, 2)).reshape(1, 4 * members)
    reward = lax.all_to_all(jnp.broadcast_to(near, (16, 4 * members)), "z", 0, 0, tiled=True)
    reward = reward.reshape(-1)
    count = reward.shape[0]
    centered = reward - jnp.sum(reward) / count
    spread = jnp.sum(centered * centered) / count
    fitness_all = (centered / jnp.sqrt(spread + spread_eps)).reshape(16, 2, 2, members)
    fitness = lax.dynamic_slice(fitness_all, (z, core, ylo, 0), (1, 1, 1, members)).reshape(members)
    fitness_order = jnp.where(ylo == 0, fitness_all, fitness_all[:, :, ::-1]).reshape(1, count)

    step = step_product(left_all, fitness_order, right_all)
    return (up_out, step, fitness)


def solution(mesh):
    fine = Mesh(mesh.devices.reshape(SIZES), AXES)
    pop = ("ylo", "z", "core")
    shard = ("x", "yhi")
    in_specs = (P(pop, None), P(pop, shard), P(pop, None), P(pop, shard), P(pop, shard))
    out_specs = (P(pop, shard), P(pop, shard), P(pop))
    return jax.shard_map(local, mesh=fine, in_specs=in_specs, out_specs=out_specs, check_vma=False)
```

time: 433 us -> 166 us (0.38)
  blocking collectives: 255 us -> 0 us
  waiting for transfers between devices: 144 us -> 63 us
  starting transfers between devices: 0.08 us -> 50.5 us
  local copies, waits for them, and re-layouts: 1.25 us -> 21.1 us
  matrix products: 12.9 us -> 0.48 us
  Pallas kernels: 0 us -> 7.84 us
    psum x3 -> x0, blocking collectives: 234 us -> none  [the longest x1 109 us: local(): mean_reward = lax.psum(jnp.sum(reward), 'pop') / member_count]
    all_gather x2 -> x1, waiting for transfers between devices: 143 us -> 37.2 us  [local(): gathered = lax.all_gather(packed, ('z', 'core'), axis=0, tiled=False)]
    all_to_all x0 -> x3, starting transfers between devices: none -> 32.3 us  [the longest x1 18.6 us: local(): lax.all_to_all(left_split, ('ylo', 'z', 'core'), 0, 0, tiled=True)]
    all_to_all x0 -> x3, waiting for transfers between devices: none -> 23.5 us  [the longest x1 13.6 us: local(): lax.all_to_all(left_split, ('ylo', 'z', 'core'), 0, 0, tiled=True)]
    all_to_all x1 -> x0, blocking collectives: 21.1 us -> none  [local(): lax.all_to_all(weighted, 'pop', split_axis=1, concat_axis=0, tiled=True)]
    ppermute x0 -> x6, starting transfers between devices: none -> 18.2 us  [the longest x1 4.03 us: local(): slab_recv = lax.ppermute(other(slab), 'ylo', SWAP)]
    dot_general x4 -> x1, matrix products: 12.9 us -> 0.48 us  [local(): jnp.einsum('mtd,md->mt', hidden_b.reshape(members, tokens, features), lef...]
    pallas_call x0 -> x2, Pallas kernels: none -> 7.84 us  [the longest x1 4.45 us: project(): pl.pallas_call(project_kernel, grid=(blocks // slabs,), in_specs=[pl.Bloc...]
  transfers between devices with their start and end apart: 2 -> 10, of which waited for: 1 -> 5; matrix products, arithmetic and copies ran while one was open for 3% -> 12% of each run, Pallas kernels for 0% -> 0%
where the time goes in v1:
time: 166 us
  waiting for transfers between devices  63 us (38%)
  starting transfers between devices  50.5 us (30%)
  local copies, waits for them, and re-layouts  21.1 us (13%)
  between operations  15.7 us (9%)
  Pallas kernels  7.84 us (5%)
  other arithmetic  7 us (4%)
    all_gather x1, waiting for transfers between devices, local(): gathered = lax.all_gather(packed, ('z', 'core'), axis=0, tiled=False)  37.2 us
    all_to_all x1, starting transfers between devices, local(): lax.all_to_all(left_split, ('ylo', 'z', 'core'), 0, 0, tiled=True)  18.6 us
    all_to_all x1, waiting for transfers between devices, local(): lax.all_to_all(left_split, ('ylo', 'z', 'core'), 0, 0, tiled=True)  13.6 us
    all_to_all x1, waiting for transfers between devices, local(): lax.all_to_all(jnp.broadcast_to(near, (16, 4 * members)), 'z', 0, 0, tile...  7.71 us
    all_to_all x1, starting transfers between devices, local(): lax.all_to_all(jnp.broadcast_to(near, (16, 4 * members)), 'z', 0, 0, tile...  6.92 us
    all_to_all x1, starting transfers between devices, local(): lax.all_to_all(jnp.broadcast_to(part, (32, 2 * members)), ('ylo', 'core',...  6.85 us
    unnamed x9, local copies, waits for them, and re-layouts  5.3 us
    pallas_call x1, Pallas kernels, project(): pl.pallas_call(project_kernel, grid=(blocks // slabs,), in_specs=[pl.Bloc...  4.45 us
  transfers between devices with their start and end apart: 10, of which 5 were waited for; matrix products, arithmetic and copies ran while one was open for 12% of the time, Pallas kernels for 0%

profile of v1, /device:TPU:1, one launch (start us, length us, event | category | flops | bytes accessed | tf_op | source)
XLA Modules:
  0.0 165.6 jit_solution(10158556024407795815)
XLA Ops:
  7.2 1.0 constant_dynamic-update-slice_fusion.1
  8.3 0.8 constant_dynamic-update-slice_fusion
  9.0 4.0 %collective-permute-start = (bf16[72,896]{1,0:T(8,128)(2,1)S(1)}, bf16[72,896]{1,0:T(8,128)(2,1)S(1)}, u32[]{:S(2)}, u32[]{:S(2)}) collective-permute-start(bf16[72,896]{1,0:T(8,128)(2,1)S(1)} %constant_dynamic-slice_fusion.3), channel_id=1, source_target_pairs={{0,256},{256,0},{1,257},{257,1},{2,258},{258,2},{3,259},{259,3},{4... | collective-permute-start | bytes 387080 | tf_op jit(solution)/shard_map/ppermute | solution.py:125
  13.1 2.3 %collective-permute-done = bf16[72,896]{1,0:T(8,128)(2,1)S(1)} collective-permute-done((bf16[72,896]{1,0:T(8,128)(2,1)S(1)}, bf16[72,896]{1,0:T(8,128)(2,1)S(1)}, u32[]{:S(2)}, u32[]{:S(2)}) %collective-permute-start) | collective-permute-done | bytes 129056 | tf_op jit(solution)/shard_map/ppermute | solution.py:125
  15.4 0.7 pad_maximum_fusion.3
  16.2 0.7 copy.52
  16.8 3.4 %collective-permute-start.1 = (bf16[128,4096]{0,1:T(8,128)(2,1)S(1)}, bf16[128,4096]{0,1:T(8,128)(2,1)S(1)}, u32[]{:S(2)}, u32[]{:S(2)}) collective-permute-start(bf16[128,4096]{0,1:T(8,128)(2,1)S(1)} %copy.52), channel_id=1, source_target_pairs={{0,256},{256,0},{1,257},{257,1},{2,258},{258,2},{3,259},{259,3},{4... | collective-permute-start | bytes 3145736 | tf_op jit(solution)/shard_map/ppermute | solution.py:133
  20.2 1.8 %constant_dynamic-slice_fusion.2 = (bf16[128,896]{1,0:T(8,128)(2,1)S(1)}, bf16[128,896]{1,0:T(8,128)(2,1)}) fusion(bf16[128,1792]{1,0:T(8,128)(2,1)} %param.9, s32[]{:T(128)S(6)} %select_n.66, s32[]{:T(128)S(6)} %select_n.67), kind=kLoop, calls=%fused_computation.23 | loop fusion | bytes 917512 | tf_op jit(solution)/shard_map/dynamic_slice | solution.py:118
  22.0 1.9 %collective-permute-start.2 = (bf16[128,896]{1,0:T(8,128)(2,1)}, bf16[128,896]{1,0:T(8,128)(2,1)}, u32[]{:S(2)}, u32[]{:S(2)}) collective-permute-start(bf16[128,896]{1,0:T(8,128)(2,1)} %get-tuple-element.18), channel_id=1, source_target_pairs={{0,256},{256,0},{1,257},{257,1},{2,258},{258,2},{3,259},{259,3},{4... | collective-permute-start | bytes 688136 | tf_op jit(solution)/shard_map/ppermute | solution.py:134
  23.9 0.5 fusion.2
  24.4 0.2 reshape.85
  24.7 3.4 %collective-permute-start.3 = (f32[128,1]{0,1:T(1,128)S(1)}, f32[128,1]{0,1:T(1,128)S(1)}, u32[]{:S(2)}, u32[]{:S(2)}) collective-permute-start(f32[128,1]{0,1:T(1,128)S(1)} %mul.34), channel_id=1, source_target_pairs={{0,256},{256,0},{1,257},{257,1},{2,258},{258,2},{3,259},{259,3},{4... | collective-permute-start | bytes 1544 | tf_op jit(solution)/shard_map/ppermute | solution.py:144
  28.1 0.1 copy.56
  28.2 0.8 reshape.99
  28.9 18.6 %all-to-all-start = ((bf16[64,2,256]{2,1,0:T(2,128)(2,1)}), bf16[64,2,256]{2,1,0:T(2,128)(2,1)S(1)}, u32[]{:S(2)}, u32[]{:S(2)}) async-start(bf16[64,2,256]{2,1,0:T(2,128)(2,1)} %reshape.99), calls=%async_computation | async-start | bytes 131072 | tf_op jit(solution)/shard_map/all_to_all | solution.py:153
  47.5 0.1 copy.55.projected
  47.7 1.0 pad_maximum_fusion.2.target
  48.7 13.6 %all-to-all-done = bf16[64,2,256]{2,1,0:T(2,128)(2,1)S(1)} async-done(((bf16[64,2,256]{2,1,0:T(2,128)(2,1)}), bf16[64,2,256]{2,1,0:T(2,128)(2,1)S(1)}, u32[]{:S(2)}, u32[]{:S(2)}) %all-to-all-start) | async-done | bytes 65568 | tf_op jit(solution)/shard_map/all_to_all | solution.py:153
  62.2 0.1 reshape.100
  62.4 0.2 pad_maximum_fusion
  62.6 0.6 fusion
  63.2 1.5 copy.53
  64.8 2.9 %copy.54.hidden = bf16[256,4096]{1,0:T(8,128)(2,1)S(1)} copy(bf16[256,4096]{0,1:T(8,128)(2,1)} %bitcast.23) | data formatting | bytes 4194304 | tf_op jit(solution)/shard_map/reshape | solution.py:150
  67.7 37.2 %all-gather.3.cloned.1.call-done = bf16[4608,896]{1,0:T(8,128)(2,1)} async-done(((bf16[144,896]{1,0:T(8,128)(2,1)}), bf16[4608,896]{1,0:T(8,128)(2,1)}) %all-gather.3.cloned.1.call-update) | async-done | bytes 8257552 | tf_op jit(solution)/shard_map/all_gather | solution.py:128
  105.0 2.1 %fusion.4 = (bf16[32,8,896]{2,1,0:T(8,128)(2,1)}, bf16[32,8,896]{2,1,0:T(8,128)(2,1)}) fusion(bf16[32,144,896]{2,1,0:T(8,128)(2,1)} %bitcast.19), kind=kLoop, calls=%fused_computation.27 | loop fusion | bytes 1835008 | tf_op jit(solution)/shard_map/slice | solution.py:169
  107.1 3.3 %copy-done = bf16[4608,896]{1,0:T(8,128)(2,1)S(1)} copy-done((bf16[4608,896]{1,0:T(8,128)(2,1)S(1)}, bf16[4608,896]{1,0:T(8,128)(2,1)}, u32[]{:S(2)}) %copy-start) | copy-done | bytes 8257560
  110.4 4.5 %shard_map.76 = (bf16[256,896]{1,0:T(8,128)(2,1)S(1)}, f32[16,128]{1,0:T(8,128)S(1)}) custom-call(bf16[32,144,896]{2,1,0:T(8,128)(2,1)S(1)} %bitcast.21, bf16[256,4096]{1,0:T(8,128)(2,1)S(1)} %copy.54.hidden, bf16[256,896]{1,0:T(8,128)(2,1)S(1)} %pad_maximum_fusion.2.target, bf16[16,896]{1,0:T(8,128)(2,1)S(1)} %pad_maximum_fusion.4.right, ...), custom_call_target="tpu_custom_call" | custom-call | flops 1879048192 | bytes 8257536 | tf_op jit(solution)/shard_map/pallas_call | solution.py:49
  114.9 0.1 slice_reduce_fusion
  115.2 0.6 broadcast_in_dim.15
  115.8 6.9 %all-to-all-start.1 = ((f32[32,1,16]{2,1,0:T(1,128)}), f32[32,1,16]{2,1,0:T(1,128)S(1)}, u32[]{:S(2)}, u32[]{:S(2)}) async-start(f32[32,1,16]{2,1,0:T(1,128)} %broadcast_in_dim.15), calls=%async_computation.1 | async-start | bytes 32768 | tf_op jit(solution)/shard_map/all_to_all | solution.py:181
  122.7 1.2 pad_maximum_fusion.1
  123.9 3.3 %collective-permute-start.5 = (bf16[32,16,896]{2,1,0:T(8,128)(2,1)S(1)}, bf16[32,16,896]{2,1,0:T(8,128)(2,1)S(1)}, u32[]{:S(2)}, u32[]{:S(2)}) collective-permute-start(bf16[32,16,896]{2,1,0:T(8,128)(2,1)S(1)} %pad_maximum_fusion.1), channel_id=1, source_target_pairs={{0,256},{256,0},{1,257},{257,1},{2,258},{258,2},{3,259},{259,3},{4... | collective-permute-start | bytes 2752520 | tf_op jit(solution)/shard_map/ppermute | solution.py:168
  127.3 0.1 copy.60.left
  127.4 2.2 %all-to-all-done.1 = f32[32,1,16]{2,1,0:T(1,128)S(1)} async-done(((f32[32,1,16]{2,1,0:T(1,128)}), f32[32,1,16]{2,1,0:T(1,128)S(1)}, u32[]{:S(2)}, u32[]{:S(2)}) %all-to-all-start.1) | async-done | bytes 2080 | tf_op jit(solution)/shard_map/all_to_all | solution.py:181
  129.8 0.6 broadcast_in_dim.17
  130.4 6.9 %all-to-all-start.2 = ((f32[16,1,32]{2,1,0:T(1,128)}), f32[16,1,32]{2,1,0:T(1,128)S(1)}, u32[]{:S(2)}, u32[]{:S(2)}) async-start(f32[16,1,32]{2,1,0:T(1,128)} %broadcast_in_dim.17), calls=%async_computation.2 | async-start | bytes 16384 | tf_op jit(solution)/shard_map/all_to_all | solution.py:185
  137.3 1.3 slice.44
  138.6 2.2 %collective-permute-start.4 = (bf16[128,896]{1,0:T(8,128)(2,1)S(1)}, bf16[128,896]{1,0:T(8,128)(2,1)S(1)}, u32[]{:S(2)}, u32[]{:S(2)}) collective-permute-start(bf16[128,896]{1,0:T(8,128)(2,1)S(1)} %get-tuple-element.16), channel_id=1, source_target_pairs={{0,256},{256,0},{1,257},{257,1},{2,258},{258,2},{3,259},{259,3},{4... | collective-permute-start | bytes 688136 | tf_op jit(solution)/shard_map/ppermute | solution.py:160
  140.8 7.7 %all-to-all-done.2 = f32[16,1,32]{2,1,0:T(1,128)S(1)} async-done(((f32[16,1,32]{2,1,0:T(1,128)}), f32[16,1,32]{2,1,0:T(1,128)S(1)}, u32[]{:S(2)}, u32[]{:S(2)}) %all-to-all-start.2) | async-done | bytes 2080 | tf_op jit(solution)/shard_map/all_to_all | solution.py:185
  148.5 0.6 reduce_sum.28
  149.8 0.6 multiply_reduce_fusion
  151.2 0.6 subtract_divide_fusion
  151.8 0.8 copy.59
  152.6 0.1 reshape.90.fitness
  152.7 1.4 dynamic-slice_reduce_fusion
  154.1 0.9 maximum_select_fusion.1
  155.0 0.4 maximum_select_fusion.right
  155.4 3.4 %shard_map.77 = f32[64,1792]{1,0:T(8,128)} custom-call(bf16[64,512]{1,0:T(8,128)(2,1)S(1)} %copy.60.left, f32[1,512]{1,0:T(1,128)S(1)} %reshape.90.fitness, bf16[512,1792]{1,0:T(8,128)(2,1)S(1)} %maximum_select_fusion.right), custom_call_target="tpu_custom_call" | custom-call | flops 234881024 | bytes 2293760 | tf_op jit(solution)/shard_map/pallas_call | solution.py:88
  (31 shorter events, 0.7 us)
Async XLA Ops:
  7.2 9.0 %copy-start.1 = (bf16[128,4096]{1,0:T(8,128)(2,1)S(1)}, bf16[128,4096]{1,0:T(8,128)(2,1)}, u32[]{:S(2)}) copy-start(bf16[128,4096]{1,0:T(8,128)(2,1)} %param.5) | copy-start | bytes 3145732
  7.2 97.8 %all-gather.3.cloned.1.call-start = ((), (), s32[]{:S(2)}) async-start(), calls=%async_computation.3 | async-start | bytes 8515584 | tf_op jit(solution)/shard_map/all_gather | solution.py:128
  9.0 6.4 %collective-permute-start = (bf16[72,896]{1,0:T(8,128)(2,1)S(1)}, bf16[72,896]{1,0:T(8,128)(2,1)S(1)}, u32[]{:S(2)}, u32[]{:S(2)}) collective-permute-start(bf16[72,896]{1,0:T(8,128)(2,1)S(1)} %constant_dynamic-slice_fusion.3), channel_id=1, source_target_pairs={{0,256},{256,0},{1,257},{257,1},{2,258},{258,2},{3,259},{259,3},{4... | collective-permute-start | bytes 387080 | tf_op jit(solution)/shard_map/ppermute | solution.py:125
  13.1 10.8 %copy-start.2 = (bf16[8,4096]{1,0:T(8,128)(2,1)S(1)}, bf16[8,4096]{1,0:T(8,128)(2,1)}, u32[]{:S(2)}) copy-start(bf16[8,4096]{1,0:T(8,128)(2,1)} %param.7) | copy-start | bytes 196612
  16.8 45.5 %collective-permute-start.1 = (bf16[128,4096]{0,1:T(8,128)(2,1)S(1)}, bf16[128,4096]{0,1:T(8,128)(2,1)S(1)}, u32[]{:S(2)}, u32[]{:S(2)}) collective-permute-start(bf16[128,4096]{0,1:T(8,128)(2,1)S(1)} %copy.52), channel_id=1, source_target_pairs={{0,256},{256,0},{1,257},{257,1},{2,258},{258,2},{3,259},{259,3},{4... | collective-permute-start | bytes 3145736 | tf_op jit(solution)/shard_map/ppermute | solution.py:133
  22.0 25.7 %collective-permute-start.2 = (bf16[128,896]{1,0:T(8,128)(2,1)}, bf16[128,896]{1,0:T(8,128)(2,1)}, u32[]{:S(2)}, u32[]{:S(2)}) collective-permute-start(bf16[128,896]{1,0:T(8,128)(2,1)} %get-tuple-element.18), channel_id=1, source_target_pairs={{0,256},{256,0},{1,257},{257,1},{2,258},{258,2},{3,259},{259,3},{4... | collective-permute-start | bytes 688136 | tf_op jit(solution)/shard_map/ppermute | solution.py:134
  24.7 22.8 %collective-permute-start.3 = (f32[128,1]{0,1:T(1,128)S(1)}, f32[128,1]{0,1:T(1,128)S(1)}, u32[]{:S(2)}, u32[]{:S(2)}) collective-permute-start(f32[128,1]{0,1:T(1,128)S(1)} %mul.34), channel_id=1, source_target_pairs={{0,256},{256,0},{1,257},{257,1},{2,258},{258,2},{3,259},{259,3},{4... | collective-permute-start | bytes 1544 | tf_op jit(solution)/shard_map/ppermute | solution.py:144
  28.9 33.3 %all-to-all-start = ((bf16[64,2,256]{2,1,0:T(2,128)(2,1)}), bf16[64,2,256]{2,1,0:T(2,128)(2,1)S(1)}, u32[]{:S(2)}, u32[]{:S(2)}) async-start(bf16[64,2,256]{2,1,0:T(2,128)(2,1)} %reshape.99), calls=%async_computation | async-start | bytes 131072 | tf_op jit(solution)/shard_map/all_to_all | solution.py:153
  107.1 3.3 %copy-start = (bf16[4608,896]{1,0:T(8,128)(2,1)S(1)}, bf16[4608,896]{1,0:T(8,128)(2,1)}, u32[]{:S(2)}) copy-start(bf16[4608,896]{1,0:T(8,128)(2,1)} %all-gather.3.cloned.1.call-done) | copy-start | bytes 24772612
  115.8 13.8 %all-to-all-start.1 = ((f32[32,1,16]{2,1,0:T(1,128)}), f32[32,1,16]{2,1,0:T(1,128)S(1)}, u32[]{:S(2)}, u32[]{:S(2)}) async-start(f32[32,1,16]{2,1,0:T(1,128)} %broadcast_in_dim.15), calls=%async_computation.1 | async-start | bytes 32768 | tf_op jit(solution)/shard_map/all_to_all | solution.py:181
  123.9 31.0 %collective-permute-start.5 = (bf16[32,16,896]{2,1,0:T(8,128)(2,1)S(1)}, bf16[32,16,896]{2,1,0:T(8,128)(2,1)S(1)}, u32[]{:S(2)}, u32[]{:S(2)}) collective-permute-start(bf16[32,16,896]{2,1,0:T(8,128)(2,1)S(1)} %pad_maximum_fusion.1), channel_id=1, source_target_pairs={{0,256},{256,0},{1,257},{257,1},{2,258},{258,2},{3,259},{259,3},{4... | collective-permute-start | bytes 2752520 | tf_op jit(solution)/shard_map/ppermute | solution.py:168
  130.4 18.2 %all-to-all-start.2 = ((f32[16,1,32]{2,1,0:T(1,128)}), f32[16,1,32]{2,1,0:T(1,128)S(1)}, u32[]{:S(2)}, u32[]{:S(2)}) async-start(f32[16,1,32]{2,1,0:T(1,128)} %broadcast_in_dim.17), calls=%async_computation.2 | async-start | bytes 16384 | tf_op jit(solution)/shard_map/all_to_all | solution.py:185
  138.6 15.5 %collective-permute-start.4 = (bf16[128,896]{1,0:T(8,128)(2,1)S(1)}, bf16[128,896]{1,0:T(8,128)(2,1)S(1)}, u32[]{:S(2)}, u32[]{:S(2)}) collective-permute-start(bf16[128,896]{1,0:T(8,128)(2,1)S(1)} %get-tuple-element.16), channel_id=1, source_target_pairs={{0,256},{256,0},{1,257},{257,1},{2,258},{258,2},{3,259},{259,3},{4... | collective-permute-start | bytes 688136 | tf_op jit(solution)/shard_map/ppermute | solution.py:160
Sparse Core Ops, SparseCore 0:
  16.3 88.6 all-gather.2

commit v2 on v1

v2 whole, which is shorter than its diff:
```python
import math

import jax
import jax.numpy as jnp
from jax import lax
from jax.experimental import pallas as pl
from jax.experimental.pallas import tpu as pltpu
from jax.sharding import Mesh, PartitionSpec as P

noise_scale = 0.5
spread_eps = 1e-05
AXES = ("ylo", "z", "core", "x", "yhi")
SIZES = (2, 16, 2, 4, 2)
SWAP = [(0, 1), (1, 0)]


def project_kernel(gathered, hidden, target, right, projected, up, reward, total):
    i = pl.program_id(0)
    slabs, _, cols = gathered.shape
    block = gathered[:, :128, :].reshape(slabs * 128, cols)
    part = jnp.dot(hidden[...], block, preferred_element_type=jnp.float32)

    @pl.when(i == 0)
    def _():
        total[...] = part

    @pl.when(i > 0)
    def _():
        total[...] += part

    @pl.when(i == pl.num_programs(0) - 1)
    def _():
        rows = total.shape[0]
        members = right.shape[0]
        tokens = rows // members
        base = total[...].reshape(members, tokens, cols)
        factor = right[...].astype(jnp.float32)
        value = base + projected[...].reshape(members, tokens, 1) * factor[:, None, :]
        up[...] = value.reshape(rows, cols).astype(jnp.bfloat16)
        aim = target[...].astype(jnp.float32).reshape(members, tokens, cols)
        gain = value * (0.5 + 0.5 * jnp.tanh(0.5 * value)) * aim
        summed = jnp.sum(jnp.sum(gain, axis=1), axis=-1, keepdims=True)
        peers = reward.shape[0]
        lanes = reward.shape[-1]
        spot = lax.broadcasted_iota(jnp.int32, (members, lanes), 0) == lax.broadcasted_iota(
            jnp.int32, (members, lanes), 1
        )
        line = jnp.sum(jnp.where(spot, summed, 0.0), axis=0, keepdims=True)
        reward[...] = jnp.broadcast_to(line[None], reward.shape)


def project(gathered, hidden, target, right, projected, peers):
    blocks, depth, cols = gathered.shape
    rows = hidden.shape[0]
    members = right.shape[0]
    slabs = 4
    whole = lambda *shape: pl.BlockSpec(shape, lambda i: (0,) * len(shape))
    return pl.pallas_call(
        project_kernel,
        grid=(blocks // slabs,),
        in_specs=[
            pl.BlockSpec((slabs, depth, cols), lambda i: (i, 0, 0)),
            pl.BlockSpec((rows, slabs * 128), lambda i: (0, i)),
            whole(rows, cols),
            whole(members, cols),
            whole(rows, 1),
        ],
        out_specs=[whole(rows, cols), whole(peers, 1, members)],
        out_shape=[
            jax.ShapeDtypeStruct((rows, cols), jnp.bfloat16),
            jax.ShapeDtypeStruct((peers, 1, members), jnp.float32),
        ],
        scratch_shapes=[pltpu.VMEM((rows, cols), jnp.float32)],
        compiler_params=pltpu.CompilerParams(vmem_limit_bytes=60 * 1024 * 1024),
        cost_estimate=pl.CostEstimate(
            flops=2 * rows * blocks * 128 * cols,
            bytes_accessed=blocks * depth * cols * 2,
            transcendentals=rows * cols,
        ),
    )(gathered, hidden, target, right, projected)


def step_kernel(place, reward, left, right_own, right_other, out, fitness, both):
    h = pl.program_id(0)
    members, depth = left.shape
    blocks, lanes = reward.shape[0], reward.shape[2]

    @pl.when(h == 0)
    def _():
        value = reward[...].reshape(blocks, lanes)
        total = jnp.sum(jnp.sum(value, axis=0, keepdims=True), axis=1, keepdims=True)
        centered = value - total * (1.0 / members)
        squares = jnp.sum(jnp.sum(centered * centered, axis=0, keepdims=True), axis=1, keepdims=True)
        score = centered / jnp.sqrt(squares * (1.0 / members) + spread_eps)
        shape = (blocks, lanes, lanes)
        spot = lax.broadcasted_iota(jnp.int32, shape, 1) == lax.broadcasted_iota(jnp.int32, shape, 2)
        column = jnp.sum(jnp.where(spot, score[:, None, :], 0.0), axis=-1, keepdims=True)
        column = column.reshape(members, 1)
        own = fitness.shape[1]
        pick = (members, own)
        mine = lax.broadcasted_iota(jnp.int32, pick, 0) == (
            lax.broadcasted_iota(jnp.int32, pick, 1) + place[1]
        )
        fitness[...] = jnp.sum(jnp.where(mine, column, 0.0), axis=0, keepdims=True)
        weighted = left[...].astype(jnp.float32) * column
        high = weighted.astype(jnp.bfloat16)
        low = (weighted - high.astype(jnp.float32)).astype(jnp.bfloat16)
        both[...] = jnp.concatenate([high, low], axis=1)

    def multiply(right):
        product = lax.dot_general(
            both[...],
            right[...].reshape(members, right.shape[-1]),
            (((0,), (0,)), ((), ())),
            preferred_element_type=jnp.float32,
        )
        out[...] = (product[:depth] + product[depth:]) * (1.0 / math.sqrt(members))

    @pl.when(h == 0)
    def _():
        multiply(right_own)

    @pl.when(h == 1)
    def _():
        multiply(right_other)


def step_product(place, reward, left, gathered, right_other, own):
    members, depth = left.shape
    blocks, rows, half = gathered.shape
    count = right_other.shape[1]
    return pl.pallas_call(
        step_kernel,
        grid_spec=pltpu.PrefetchScalarGridSpec(
            num_scalar_prefetch=1,
            grid=(2,),
            in_specs=[
                pl.BlockSpec(reward.shape, lambda h, p: (0, 0, 0)),
                pl.BlockSpec((members, depth), lambda h, p: (0, 0)),
                pl.BlockSpec((blocks, count, half), lambda h, p: (0, rows // count - 1, 0)),
                pl.BlockSpec((blocks, count, half), lambda h, p: (0, 0, 0)),
            ],
            out_specs=[
                pl.BlockSpec((depth, half), lambda h, p: (0, (p[0] + h) % 2)),
                pl.BlockSpec((1, own), lambda h, p: (0, 0)),
            ],
            scratch_shapes=[pltpu.VMEM((members, 2 * depth), jnp.bfloat16)],
        ),
        out_shape=[
            jax.ShapeDtypeStruct((depth, 2 * half), jnp.float32),
            jax.ShapeDtypeStruct((1, own), jnp.float32),
        ],
        compiler_params=pltpu.CompilerParams(vmem_limit_bytes=60 * 1024 * 1024),
        cost_estimate=pl.CostEstimate(
            flops=8 * depth * members * half,
            bytes_accessed=members * half * 4 + depth * half * 8,
            transcendentals=0,
        ),
    )(place, reward, left, gathered, right_other)


def local(hidden, weight, left_factors, right_factors, target):
    members, features = left_factors.shape
    rows = hidden.shape[0]
    tokens = rows // members
    depth, cols = weight.shape
    half = cols // 2
    ylo = lax.axis_index("ylo")
    z = lax.axis_index("z")
    core = lax.axis_index("core")
    low = ylo == 0

    def own(a):
        return jnp.where(low, a[:, :half], a[:, half:])

    def other(a):
        return jnp.where(low, a[:, half:], a[:, :half])

    def order(a, b, axis=0):
        return jnp.where(
            low, jnp.concatenate([a, b], axis=axis), jnp.concatenate([b, a], axis=axis)
        )

    mine, sent = own(right_factors), other(right_factors)
    slab_recv = lax.ppermute(
        jnp.concatenate([other(weight), sent, mine], axis=0), "ylo", SWAP
    )
    theirs, theirs_far = slab_recv[depth : depth + members], slab_recv[depth + members :]
    right_local = order(mine, theirs)
    packed = jnp.concatenate([order(own(weight), slab_recv[:depth]), right_local], axis=0)
    gathered = lax.all_gather(packed, ("z", "core"), axis=0, tiled=False)

    after, hidden_b, left_b, target_b, sent, theirs_far = lax.optimization_barrier(
        (packed, hidden, left_factors, target, sent, theirs_far)
    )
    rows_recv = lax.ppermute(hidden_b, "ylo", SWAP)
    target_recv = lax.ppermute(other(target_b), "ylo", SWAP)
    projected_own = (
        jnp.einsum(
            "mtd,md->mt",
            hidden_b.reshape(members, tokens, features),
            left_b,
            preferred_element_type=jnp.float32,
        ).reshape(rows, 1)
        * (noise_scale / math.sqrt(features))
    )
    projected_recv = lax.ppermute(projected_own, "ylo", SWAP)
    projected = order(projected_own, projected_recv)
    target_all = order(own(target_b), target_recv)
    hidden_all = order(hidden_b, rows_recv)
    spread_rows = hidden_all.reshape(2 * rows, 2, features // (2 * depth), depth)
    hidden_all = spread_rows.transpose(0, 2, 1, 3).reshape(2 * rows, features)

    left_split = left_b.reshape(members, features // depth, depth).transpose(1, 0, 2)
    left_all = lax.all_to_all(left_split, ("ylo", "z", "core"), 0, 0, tiled=True)
    left_all = left_all.reshape(2, features // (2 * depth), members, depth)
    left_all = left_all.transpose(1, 0, 2, 3).reshape(-1, depth)
    far = order(sent, theirs_far)
    right_other = lax.all_gather(far, ("z", "core"), axis=0, tiled=False)

    hidden_all, left_all, right_other = lax.optimization_barrier((hidden_all, left_all, right_other))
    up, part = project(gathered, hidden_all, target_all, right_local, projected, 32)

    near = lax.all_to_all(part, ("ylo", "core", "x", "yhi"), 0, 0, tiled=True)
    near = near.reshape(2, 2, 8, 2 * members).sum(axis=(0, 2))
    near = near.reshape(1, 1, 4 * members)
    reward = lax.all_to_all(jnp.broadcast_to(near, (16, 1, 4 * members)), "z", 0, 0, tiled=True)

    up_recv = lax.ppermute(jnp.where(low, up[rows:], up[:rows]), "ylo", SWAP)
    up_out = order(jnp.where(low, up[:rows], up[rows:]), up_recv, axis=1)

    place = jnp.stack([ylo, z * 4 * members + core * 2 * members + ylo * members]).astype(jnp.int32)
    step, fitness = step_product(place, reward, left_all, gathered, right_other, members)
    return (up_out, step, fitness.reshape(members))


def solution(mesh):
    fine = Mesh(mesh.devices.reshape(SIZES), AXES)
    pop = ("ylo", "z", "core")
    shard = ("x", "yhi")
    in_specs = (P(pop, None), P(pop, shard), P(pop, None), P(pop, shard), P(pop, shard))
    out_specs = (P(pop, shard), P(pop, shard), P(pop))
    return jax.shard_map(local, mesh=fine, in_specs=in_specs, out_specs=out_specs, check_vma=False)
```

time: 166 us -> 166 us (level)
  blocking collectives: 0 us -> 38.1 us
  waiting for transfers between devices: 63 us -> 35.7 us
  local copies, waits for them, and re-layouts: 21.1 us -> 7.3 us
  Pallas kernels: 7.84 us -> 13.7 us
  starting transfers between devices: 50.5 us -> 47.1 us
  other arithmetic: 7 us -> 8.83 us
    all_gather x0 -> x1, blocking collectives: none -> 38.1 us  [local(): right_other = lax.all_gather(far, ('z', 'core'), axis=0, tiled=False)]
    all_gather x1, waiting for transfers between devices: 37.2 us -> 9.77 us  [local(): gathered = lax.all_gather(packed, ('z', 'core'), axis=0, tiled=False)]
    all_to_all x1, waiting for transfers between devices: 13.6 us -> 0.01 us  [local(): lax.all_to_all(left_split, ('ylo', 'z', 'core'), 0, 0, tiled=True)]
    all_to_all x2, waiting for transfers between devices: 9.93 us -> 17.5 us  [the longest x1 10.6 us: local(): lax.all_to_all(jnp.broadcast_to(near, (16, 1, 4 * members)), 'z', 0, 0, t...]
    ppermute x1, waiting for transfers between devices: 0.01 us -> 5.87 us  [local(): target_recv = lax.ppermute(other(target_b), 'ylo', SWAP)]
    select_n x3 -> x10, other arithmetic: 1.31 us -> 6.45 us  [the longest x6 2.47 us: order(): jnp.where(low, jnp.concatenate([a, b], axis=axis), jnp.concatenate([b, a]...]
    pallas_call x1, Pallas kernels: 4.45 us -> 9.59 us  [project(): pl.pallas_call(project_kernel, grid=(blocks // slabs,), in_specs=[pl.Bloc...]
    unnamed x9 -> x10, local copies, waits for them, and re-layouts: 5.3 us -> 1.52 us
  transfers between devices with their start and end apart: 10 -> 9, of which waited for: 5 -> 5; matrix products, arithmetic and copies ran while one was open for 12% -> 7% of each run, Pallas kernels for 0% -> 2%
where the time goes in v2:
time: 166 us; the launch traced here: 165 us
  starting transfers between devices  47.1 us (28%)
  blocking collectives  38.1 us (23%)
  waiting for transfers between devices  35.7 us (22%)
  between operations  14.3 us (9%)
  Pallas kernels  13.7 us (8%)
  other arithmetic  8.83 us (5%)
  local copies, waits for them, and re-layouts  7.3 us (4%)
    all_gather x1, blocking collectives, local(): right_other = lax.all_gather(far, ('z', 'core'), axis=0, tiled=False)  38.1 us
    all_to_all x1, starting transfers between devices, local(): lax.all_to_all(left_split, ('ylo', 'z', 'core'), 0, 0, tiled=True)  18.1 us
    all_to_all x1, waiting for transfers between devices, local(): lax.all_to_all(jnp.broadcast_to(near, (16, 1, 4 * members)), 'z', 0, 0, t...  10.6 us
    all_gather x1, waiting for transfers between devices, local(): gathered = lax.all_gather(packed, ('z', 'core'), axis=0, tiled=False)  9.77 us
    pallas_call x1, Pallas kernels, project(): pl.pallas_call(project_kernel, grid=(blocks // slabs,), in_specs=[pl.Bloc...  9.59 us
    all_to_all x1, waiting for transfers between devices, local(): near = lax.all_to_all(part, ('ylo', 'core', 'x', 'yhi'), 0, 0, tiled=True)  6.92 us
    all_to_all x1, starting transfers between devices, local(): near = lax.all_to_all(part, ('ylo', 'core', 'x', 'yhi'), 0, 0, tiled=True)  6.9 us
    all_to_all x1, starting transfers between devices, local(): lax.all_to_all(jnp.broadcast_to(near, (16, 1, 4 * members)), 'z', 0, 0, t...  6.03 us
  transfers between devices with their start and end apart: 9, of which 5 were waited for; matrix products, arithmetic and copies ran while one was open for 7% of the time, Pallas kernels for 2%

profile of v2, /device:TPU:1, one launch (start us, length us, event | category | flops | bytes accessed | tf_op | source)
XLA Modules:
  0.0 165.5 jit_solution(9938447807904186101)
XLA Ops:
  7.2 0.0 all-gather.3.cloned.1.call-start
  7.2 0.8 broadcast_select_fusion.8
  8.0 1.0 broadcast_select_fusion.5
  9.0 0.0 copy-start.2
  9.1 4.0 %collective-permute-start = (bf16[80,896]{1,0:T(8,128)(2,1)S(1)}, bf16[80,896]{1,0:T(8,128)(2,1)S(1)}, u32[]{:S(2)}, u32[]{:S(2)}) collective-permute-start(bf16[80,896]{1,0:T(8,128)(2,1)S(1)} %pad_maximum_fusion.1), channel_id=1, source_target_pairs={{0,256},{256,0},{1,257},{257,1},{2,258},{258,2},{3,259},{259,3},{4... | collective-permute-start | bytes 430088 | tf_op jit(solution)/shard_map/ppermute | solution.py:185
  13.1 2.5 %collective-permute-done = bf16[80,896]{1,0:T(8,128)(2,1)S(1)} collective-permute-done((bf16[80,896]{1,0:T(8,128)(2,1)S(1)}, bf16[80,896]{1,0:T(8,128)(2,1)S(1)}, u32[]{:S(2)}, u32[]{:S(2)}) %collective-permute-start) | collective-permute-done | bytes 143392 | tf_op jit(solution)/shard_map/ppermute | solution.py:185
  15.7 0.7 pad_maximum_fusion
  16.4 0.0 all-gather.3.cloned.1.call-update
  16.4 0.7 copy.32
  17.1 3.4 %collective-permute-start.1 = (bf16[128,4096]{0,1:T(8,128)(2,1)S(1)}, bf16[128,4096]{0,1:T(8,128)(2,1)S(1)}, u32[]{:S(2)}, u32[]{:S(2)}) collective-permute-start(bf16[128,4096]{0,1:T(8,128)(2,1)S(1)} %copy.32), channel_id=1, source_target_pairs={{0,256},{256,0},{1,257},{257,1},{2,258},{258,2},{3,259},{259,3},{4... | collective-permute-start | bytes 3145736 | tf_op jit(solution)/shard_map/ppermute | solution.py:196
  20.5 0.2 reshape.165
  20.7 0.1 copy.35
  20.8 0.8 reshape.174
  21.5 18.1 %all-to-all-start = ((bf16[64,2,256]{2,1,0:T(2,128)(2,1)}), bf16[64,2,256]{2,1,0:T(2,128)(2,1)S(1)}, u32[]{:S(2)}, u32[]{:S(2)}) async-start(bf16[64,2,256]{2,1,0:T(2,128)(2,1)} %reshape.174), calls=%async_computation | async-start | bytes 131072 | tf_op jit(solution)/shard_map/all_to_all | solution.py:215
  39.7 0.5 fusion.1
  40.2 0.1 concatenate.106
  40.3 3.4 %collective-permute-start.3 = (f32[128,1]{0,1:T(1,128)S(1)}, f32[128,1]{0,1:T(1,128)S(1)}, u32[]{:S(2)}, u32[]{:S(2)}) collective-permute-start(f32[128,1]{0,1:T(1,128)S(1)} %concatenate.106), channel_id=1, source_target_pairs={{0,256},{256,0},{1,257},{257,1},{2,258},{258,2},{3,259},{259,3},{4... | collective-permute-start | bytes 1544 | tf_op jit(solution)/shard_map/ppermute | solution.py:207
  43.7 38.1 %all_gather.12.right_other = bf16[32,16,896]{2,1,0:T(8,128)(2,1)} all-gather(bf16[1,16,896]{2,1,0:T(8,128)(2,1)S(1)} %maximum_select_fusion.5), channel_id=1, replica_groups=mesh['ylo'=2,'z'=16,'core'=2,'x'=4,'yhi'=2] {'z','core'}, dimensions={0}, use_global_device_ids=true | all-gather | bytes 946176 | tf_op jit(solution)/shard_map/all_gather | solution.py:219
  81.8 1.1 broadcast_select_fusion.3
  82.9 2.1 %collective-permute-start.2 = (bf16[128,896]{1,0:T(8,128)(2,1)S(1)}, bf16[128,896]{1,0:T(8,128)(2,1)S(1)}, u32[]{:S(2)}, u32[]{:S(2)}) collective-permute-start(bf16[128,896]{1,0:T(8,128)(2,1)S(1)} %get-tuple-element.30), channel_id=1, source_target_pairs={{0,256},{256,0},{1,257},{257,1},{2,258},{258,2},{3,259},{259,3},{4... | collective-permute-start | bytes 688136 | tf_op jit(solution)/shard_map/ppermute | solution.py:197
  85.0 0.0 collective-permute-done.3
  85.0 0.1 copy.37
  85.2 0.1 copy.38
  85.3 0.7 broadcast_select_fusion.6.projected
  86.0 5.9 %collective-permute-done.2 = bf16[128,896]{1,0:T(8,128)(2,1)S(1)} collective-permute-done((bf16[128,896]{1,0:T(8,128)(2,1)S(1)}, bf16[128,896]{1,0:T(8,128)(2,1)S(1)}, u32[]{:S(2)}, u32[]{:S(2)}) %collective-permute-start.2) | collective-permute-done | bytes 229408 | tf_op jit(solution)/shard_map/ppermute | solution.py:197
  91.9 0.9 maximum_select_fusion.1.target
  92.7 0.0 all-to-all-done
  92.7 0.1 reshape.175
  92.9 0.7 copy.36
  93.5 0.0 collective-permute-done.1
  93.5 1.0 fusion
  94.6 0.2 copy.34
  94.8 2.9 %copy.39.hidden = bf16[256,4096]{1,0:T(8,128)(2,1)} copy(bf16[256,4096]{0,1:T(8,128)(2,1)S(1)} %bitcast.24) | data formatting | bytes 4194304 | tf_op jit(solution)/shard_map/optimization_barrier | solution.py:221
  97.7 9.8 %all-gather.3.cloned.1.call-done = bf16[4608,896]{1,0:T(8,128)(2,1)} async-done(((bf16[144,896]{1,0:T(8,128)(2,1)}), bf16[4608,896]{1,0:T(8,128)(2,1)}) %all-gather.3.cloned.1.call-update) | async-done | bytes 8257552 | tf_op jit(solution)/shard_map/all_gather | solution.py:191
  107.4 9.6 %shard_map.76 = (bf16[256,896]{1,0:T(8,128)(2,1)}, f32[32,1,16]{2,1,0:T(1,128)}) custom-call(bf16[32,144,896]{2,1,0:T(8,128)(2,1)} %bitcast.22, bf16[256,4096]{1,0:T(8,128)(2,1)} %copy.39.hidden, bf16[256,896]{1,0:T(8,128)(2,1)} %maximum_select_fusion.1.target, bf16[16,896]{1,0:T(8,128)(2,1)} %copy-done.1, f32[256,1]{1,0:T(8,128)} %broadcast_select_fusion.6.projected), custom_call_target="tpu_custom_call" | custom-call | flops 1879048192 | bytes 8257536 | tf_op jit(solution)/shard_map/pallas_call | solution.py:58
  117.0 1.1 broadcast_select_fusion.1
  118.1 3.1 %collective-permute-start.4 = (bf16[128,896]{1,0:T(8,128)(2,1)S(1)}, bf16[128,896]{1,0:T(8,128)(2,1)S(1)}, u32[]{:S(2)}, u32[]{:S(2)}) collective-permute-start(bf16[128,896]{1,0:T(8,128)(2,1)S(1)} %get-tuple-element.28), channel_id=1, source_target_pairs={{0,256},{256,0},{1,257},{257,1},{2,258},{258,2},{3,259},{259,3},{4... | collective-permute-start | bytes 688136 | tf_op jit(solution)/shard_map/ppermute | solution.py:229
  121.3 6.9 %all-to-all-start.1 = ((f32[32,1,16]{2,1,0:T(1,128)}), f32[32,1,16]{2,1,0:T(1,128)S(1)}, u32[]{:S(2)}, u32[]{:S(2)}) async-start(f32[32,1,16]{2,1,0:T(1,128)} %get-tuple-element.22), calls=%async_computation.1 | async-start | bytes 32768 | tf_op jit(solution)/shard_map/all_to_all | solution.py:224
  128.2 6.9 %all-to-all-done.1 = f32[32,1,16]{2,1,0:T(1,128)S(1)} async-done(((f32[32,1,16]{2,1,0:T(1,128)}), f32[32,1,16]{2,1,0:T(1,128)S(1)}, u32[]{:S(2)}, u32[]{:S(2)}) %all-to-all-start.1) | async-done | bytes 2080 | tf_op jit(solution)/shard_map/all_to_all | solution.py:224
  135.1 0.1 broadcast_in_dim.7
  135.2 0.6 broadcast_in_dim.8
  135.8 6.0 %all-to-all-start.2 = ((f32[16,1,32]{2,1,0:T(1,128)}), f32[16,1,32]{2,1,0:T(1,128)S(1)}, u32[]{:S(2)}, u32[]{:S(2)}) async-start(f32[16,1,32]{2,1,0:T(1,128)} %broadcast_in_dim.8), calls=%async_computation.2 | async-start | bytes 16384 | tf_op jit(solution)/shard_map/all_to_all | solution.py:227
  141.9 0.6 pad_add_fusion.place
  142.5 10.6 %all-to-all-done.2.reward = f32[16,1,32]{2,1,0:T(1,128)S(1)} async-done(((f32[16,1,32]{2,1,0:T(1,128)}), f32[16,1,32]{2,1,0:T(1,128)S(1)}, u32[]{:S(2)}, u32[]{:S(2)}) %all-to-all-start.2) | async-done | bytes 2080 | tf_op jit(solution)/shard_map/all_to_all | solution.py:227
  153.1 0.6 copy-done.3
  153.7 4.1 %shard_map.77 = (f32[64,1792]{1,0:T(8,128)}, f32[1,8]{1,0:T(1,128)}) custom-call(s32[2]{0:T(128)} %pad_add_fusion.place, f32[16,1,32]{2,1,0:T(1,128)} %copy-done.3, bf16[512,64]{1,0:T(8,128)(2,1)} %bitcast.28, bf16[32,144,896]{2,1,0:T(8,128)(2,1)} %bitcast.23, bf16[32,16,896]{2,1,0:T(8,128)(2,1)} %all_gather.12.right_other), custom_call_target="tpu_custom_call" | custom-call | flops 234881024 | bytes 2293760 | tf_op jit(solution)/shard_map/pallas_call | solution.py:132
  157.8 0.0 collective-permute-done.4
  157.8 0.9 maximum_select_fusion.2
  (15 shorter events, 0.1 us)
Async XLA Ops:
  7.2 9.3 %copy-start = (bf16[128,4096]{1,0:T(8,128)(2,1)S(1)}, bf16[128,4096]{1,0:T(8,128)(2,1)}, u32[]{:S(2)}) copy-start(bf16[128,4096]{1,0:T(8,128)(2,1)} %param.5) | copy-start | bytes 3145732
  7.2 100.3 %all-gather.3.cloned.1.call-start = ((), (), s32[]{:S(2)}) async-start(), calls=%async_computation.3 | async-start | bytes 8515584 | tf_op jit(solution)/shard_map/all_gather | solution.py:191
  9.0 11.4 %copy-start.2 = (bf16[8,4096]{1,0:T(8,128)(2,1)S(1)}, bf16[8,4096]{1,0:T(8,128)(2,1)}, u32[]{:S(2)}) copy-start(bf16[8,4096]{1,0:T(8,128)(2,1)} %param.7) | copy-start | bytes 196612
  9.1 6.5 %collective-permute-start = (bf16[80,896]{1,0:T(8,128)(2,1)S(1)}, bf16[80,896]{1,0:T(8,128)(2,1)S(1)}, u32[]{:S(2)}, u32[]{:S(2)}) collective-permute-start(bf16[80,896]{1,0:T(8,128)(2,1)S(1)} %pad_maximum_fusion.1), channel_id=1, source_target_pairs={{0,256},{256,0},{1,257},{257,1},{2,258},{258,2},{3,259},{259,3},{4... | collective-permute-start | bytes 430088 | tf_op jit(solution)/shard_map/ppermute | solution.py:185
  15.6 5.9 %copy-start.1 = (bf16[16,896]{1,0:T(8,128)(2,1)}, bf16[16,896]{1,0:T(8,128)(2,1)S(1)}, u32[]{:S(2)}) copy-start(bf16[16,896]{1,0:T(8,128)(2,1)S(1)} %maximum_select_fusion.4.right) | copy-start | bytes 86020
  17.1 76.4 %collective-permute-start.1 = (bf16[128,4096]{0,1:T(8,128)(2,1)S(1)}, bf16[128,4096]{0,1:T(8,128)(2,1)S(1)}, u32[]{:S(2)}, u32[]{:S(2)}) collective-permute-start(bf16[128,4096]{0,1:T(8,128)(2,1)S(1)} %copy.32), channel_id=1, source_target_pairs={{0,256},{256,0},{1,257},{257,1},{2,258},{258,2},{3,259},{259,3},{4... | collective-permute-start | bytes 3145736 | tf_op jit(solution)/shard_map/ppermute | solution.py:196
  21.5 71.2 %all-to-all-start = ((bf16[64,2,256]{2,1,0:T(2,128)(2,1)}), bf16[64,2,256]{2,1,0:T(2,128)(2,1)S(1)}, u32[]{:S(2)}, u32[]{:S(2)}) async-start(bf16[64,2,256]{2,1,0:T(2,128)(2,1)} %reshape.174), calls=%async_computation | async-start | bytes 131072 | tf_op jit(solution)/shard_map/all_to_all | solution.py:215
  40.3 44.7 %collective-permute-start.3 = (f32[128,1]{0,1:T(1,128)S(1)}, f32[128,1]{0,1:T(1,128)S(1)}, u32[]{:S(2)}, u32[]{:S(2)}) collective-permute-start(f32[128,1]{0,1:T(1,128)S(1)} %concatenate.106), channel_id=1, source_target_pairs={{0,256},{256,0},{1,257},{257,1},{2,258},{258,2},{3,259},{259,3},{4... | collective-permute-start | bytes 1544 | tf_op jit(solution)/shard_map/ppermute | solution.py:207
  82.9 8.9 %collective-permute-start.2 = (bf16[128,896]{1,0:T(8,128)(2,1)S(1)}, bf16[128,896]{1,0:T(8,128)(2,1)S(1)}, u32[]{:S(2)}, u32[]{:S(2)}) collective-permute-start(bf16[128,896]{1,0:T(8,128)(2,1)S(1)} %get-tuple-element.30), channel_id=1, source_target_pairs={{0,256},{256,0},{1,257},{257,1},{2,258},{258,2},{3,259},{259,3},{4... | collective-permute-start | bytes 688136 | tf_op jit(solution)/shard_map/ppermute | solution.py:197
  118.1 39.6 %collective-permute-start.4 = (bf16[128,896]{1,0:T(8,128)(2,1)S(1)}, bf16[128,896]{1,0:T(8,128)(2,1)S(1)}, u32[]{:S(2)}, u32[]{:S(2)}) collective-permute-start(bf16[128,896]{1,0:T(8,128)(2,1)S(1)} %get-tuple-element.28), channel_id=1, source_target_pairs={{0,256},{256,0},{1,257},{257,1},{2,258},{258,2},{3,259},{259,3},{4... | collective-permute-start | bytes 688136 | tf_op jit(solution)/shard_map/ppermute | solution.py:229
  121.3 13.8 %all-to-all-start.1 = ((f32[32,1,16]{2,1,0:T(1,128)}), f32[32,1,16]{2,1,0:T(1,128)S(1)}, u32[]{:S(2)}, u32[]{:S(2)}) async-start(f32[32,1,16]{2,1,0:T(1,128)} %get-tuple-element.22), calls=%async_computation.1 | async-start | bytes 32768 | tf_op jit(solution)/shard_map/all_to_all | solution.py:224
  135.8 17.3 %all-to-all-start.2 = ((f32[16,1,32]{2,1,0:T(1,128)}), f32[16,1,32]{2,1,0:T(1,128)S(1)}, u32[]{:S(2)}, u32[]{:S(2)}) async-start(f32[16,1,32]{2,1,0:T(1,128)} %broadcast_in_dim.8), calls=%async_computation.2 | async-start | bytes 16384 | tf_op jit(solution)/shard_map/all_to_all | solution.py:227
  153.1 0.6 copy-start.3
Sparse Core Ops, SparseCore 0:
  16.5 90.8 all-gather.2

commit v3 on v2

v3 whole, which is shorter than its diff:
```python
import math

import jax
import jax.numpy as jnp
from jax import lax
from jax.experimental import pallas as pl
from jax.experimental.pallas import tpu as pltpu
from jax.sharding import Mesh, PartitionSpec as P

noise_scale = 0.5
spread_eps = 1e-05
AXES = ("ylo", "z", "core", "x", "yhi")
SIZES = (2, 16, 2, 4, 2)
SWAP = [(0, 1), (1, 0)]


def project_kernel(
    place, gathered, hidden, target, right, projected, keep, send, reward, portion, total, held, sems
):
    chunks, slabs, width, cols = held.shape
    copies = []
    for i in range(chunks):
        copy = pltpu.make_async_copy(
            gathered.at[pl.ds(i * slabs, slabs), pl.ds(0, width), :], held.at[i], sems.at[i]
        )
        copy.start()
        copies.append(copy)
    last = pltpu.make_async_copy(
        gathered.at[:, pl.ds(width, portion.shape[1]), :], portion, sems.at[chunks]
    )
    last.start()
    span = slabs * width
    for i in range(chunks):
        copies[i].wait()
        part = jnp.dot(
            hidden[:, i * span : (i + 1) * span],
            held[i].reshape(span, cols),
            preferred_element_type=jnp.float32,
        )
        if i == 0:
            total[...] = part
        else:
            total[...] += part
    rows = total.shape[0]
    members = right.shape[0]
    tokens = rows // members
    base = total[...].reshape(members, tokens, cols)
    factor = right[...].astype(jnp.float32)
    value = base + projected[...].reshape(members, tokens, 1) * factor[:, None, :]
    up = value.reshape(rows, cols).astype(jnp.bfloat16)
    keep[...] = up[: rows // 2]
    send[...] = up[rows // 2 :]
    aim = target[...].astype(jnp.float32).reshape(members, tokens, cols)
    gain = value * (0.5 + 0.5 * jnp.tanh(0.5 * value)) * aim
    summed = jnp.sum(jnp.sum(gain, axis=1), axis=-1, keepdims=True)
    shape = (members, reward.shape[-1])
    row = lax.broadcasted_iota(jnp.int32, shape, 0) + place[0] * (members // 2)
    row = jnp.where(row < members, row, row - members)
    spot = row == lax.broadcasted_iota(jnp.int32, shape, 1)
    line = jnp.sum(jnp.where(spot, summed, 0.0), axis=0, keepdims=True)
    reward[...] = jnp.broadcast_to(line[None], reward.shape)
    last.wait()


VMEM = pl.BlockSpec(memory_space=pltpu.VMEM)
SMEM = pl.BlockSpec(memory_space=pltpu.SMEM)
ANY = pl.BlockSpec(memory_space=pl.ANY)


def project(place, gathered, hidden, target, right, projected, peers):
    blocks, depth, cols = gathered.shape
    rows, features = hidden.shape
    members = right.shape[0]
    slabs = 4
    width = features // blocks
    return pl.pallas_call(
        project_kernel,
        in_specs=[SMEM, ANY, VMEM, VMEM, VMEM, VMEM],
        out_specs=[VMEM, VMEM, VMEM, VMEM],
        out_shape=[
            jax.ShapeDtypeStruct((rows // 2, cols), jnp.bfloat16),
            jax.ShapeDtypeStruct((rows // 2, cols), jnp.bfloat16),
            jax.ShapeDtypeStruct((peers, 1, members), jnp.float32),
            jax.ShapeDtypeStruct((blocks, depth - width, cols), jnp.bfloat16),
        ],
        scratch_shapes=[
            pltpu.VMEM((rows, cols), jnp.float32),
            pltpu.VMEM((blocks // slabs, slabs, width, cols), jnp.bfloat16),
            pltpu.SemaphoreType.DMA((blocks // slabs + 1,)),
        ],
        compiler_params=pltpu.CompilerParams(vmem_limit_bytes=53 * 1024 * 1024),
        cost_estimate=pl.CostEstimate(
            flops=2 * rows * features * cols,
            bytes_accessed=features * cols * 2,
            transcendentals=rows * cols,
        ),
    )(place, gathered, hidden, target, right, projected)


def step_kernel(place, reward, left, right_own, right_other, keep, recv, out, up, fitness):
    members, depth = left.shape
    blocks, _, lanes = reward.shape
    half = right_own.shape[2]
    own_at = pl.multiple_of(place[0] * half, 128)
    other_at = pl.multiple_of((1 - place[0]) * half, 128)
    up[:, pl.ds(own_at, half)] = keep[...]
    up[:, pl.ds(other_at, half)] = recv[...]
    value = reward[...].reshape(blocks, lanes)
    total = jnp.sum(jnp.sum(value, axis=0, keepdims=True), axis=1, keepdims=True)
    centered = value - total * (1.0 / members)
    squares = jnp.sum(jnp.sum(centered * centered, axis=0, keepdims=True), axis=1, keepdims=True)
    score = centered / jnp.sqrt(squares * (1.0 / members) + spread_eps)
    shape = (blocks, lanes, lanes)
    spot = lax.broadcasted_iota(jnp.int32, shape, 1) == lax.broadcasted_iota(jnp.int32, shape, 2)
    column = jnp.sum(jnp.where(spot, score[:, None, :], 0.0), axis=-1, keepdims=True)
    column = column.reshape(members, 1)
    pick = (members, fitness.shape[1])
    mine = lax.broadcasted_iota(jnp.int32, pick, 0) == (
        lax.broadcasted_iota(jnp.int32, pick, 1) + place[1]
    )
    fitness[...] = jnp.sum(jnp.where(mine, column, 0.0), axis=0, keepdims=True)
    weighted = left[...].astype(jnp.float32) * column
    high = weighted.astype(jnp.bfloat16)
    low = (weighted - high.astype(jnp.float32)).astype(jnp.bfloat16)
    both = jnp.concatenate([high, low], axis=1)

    def multiply(right, at):
        product = lax.dot_general(
            both,
            right.reshape(members, half),
            (((0,), (0,)), ((), ())),
            preferred_element_type=jnp.float32,
        )
        out[:, pl.ds(at, half)] = (product[:depth] + product[depth:]) * (1.0 / math.sqrt(members))

    multiply(right_other[...], other_at)
    multiply(right_own[...], own_at)


def step_product(place, reward, left, right_own, right_other, keep, recv, own):
    members, depth = left.shape
    half = right_other.shape[2]
    return pl.pallas_call(
        step_kernel,
        in_specs=[SMEM, VMEM, VMEM, VMEM, VMEM, VMEM, VMEM],
        out_specs=[VMEM, VMEM, VMEM],
        out_shape=[
            jax.ShapeDtypeStruct((depth, 2 * half), jnp.float32),
            jax.ShapeDtypeStruct((keep.shape[0], 2 * half), jnp.bfloat16),
            jax.ShapeDtypeStruct((1, own), jnp.float32),
        ],
        compiler_params=pltpu.CompilerParams(vmem_limit_bytes=24 * 1024 * 1024),
        cost_estimate=pl.CostEstimate(
            flops=8 * depth * members * half,
            bytes_accessed=members * half * 4 + depth * half * 8,
            transcendentals=0,
        ),
    )(place, reward, left, right_own, right_other, keep, recv)


def local(hidden, weight, left_factors, right_factors, target):
    members, features = left_factors.shape
    rows = hidden.shape[0]
    tokens = rows // members
    depth, cols = weight.shape
    half = cols // 2
    ylo = lax.axis_index("ylo")
    z = lax.axis_index("z")
    core = lax.axis_index("core")
    low = ylo == 0

    def own(a):
        return jnp.where(low, a[:, :half], a[:, half:])

    def other(a):
        return jnp.where(low, a[:, half:], a[:, :half])

    def order(a, b, axis=0):
        return jnp.where(
            low, jnp.concatenate([a, b], axis=axis), jnp.concatenate([b, a], axis=axis)
        )

    mine, sent = own(right_factors), other(right_factors)
    slab_recv = lax.ppermute(
        jnp.concatenate([other(weight), sent, mine], axis=0), "ylo", SWAP
    )
    theirs, theirs_far = slab_recv[depth : depth + members], slab_recv[depth + members :]
    right_local = jnp.concatenate([mine, theirs], axis=0)
    packed = jnp.concatenate(
        [order(own(weight), slab_recv[:depth]), order(mine, theirs)], axis=0
    )
    gathered = lax.all_gather(packed, ("z", "core"), axis=0, tiled=False)

    after, hidden_b, left_b, target_b, sent, theirs_far = lax.optimization_barrier(
        (packed, hidden, left_factors, target, sent, theirs_far)
    )
    rows_recv = lax.ppermute(hidden_b, "ylo", SWAP)
    target_recv = lax.ppermute(other(target_b), "ylo", SWAP)
    projected_own = (
        jnp.einsum(
            "mtd,md->mt",
            hidden_b.reshape(members, tokens, features),
            left_b,
            preferred_element_type=jnp.float32,
        ).reshape(rows, 1)
        * (noise_scale / math.sqrt(features))
    )
    projected_recv = lax.ppermute(projected_own, "ylo", SWAP)
    projected = jnp.concatenate([projected_own, projected_recv], axis=0)
    target_all = jnp.concatenate([own(target_b), target_recv], axis=0)
    hidden_all = jnp.concatenate([hidden_b, rows_recv], axis=0)
    spread_rows = hidden_all.reshape(2 * rows, 2, features // (2 * depth), depth)
    hidden_all = spread_rows.transpose(0, 2, 1, 3).reshape(2 * rows, features)

    left_split = left_b.reshape(members, features // depth, depth).transpose(1, 0, 2)
    left_all = lax.all_to_all(left_split, ("ylo", "z", "core"), 0, 0, tiled=True)
    left_all = left_all.reshape(2, features // (2 * depth), members, depth)
    left_all = left_all.transpose(1, 0, 2, 3).reshape(-1, depth)
    far = order(sent, theirs_far)
    right_other = lax.all_gather(far, ("z", "core"), axis=0, tiled=False)

    hidden_all, left_all, right_other = lax.optimization_barrier((hidden_all, left_all, right_other))
    place = jnp.stack([ylo, z * 4 * members + core * 2 * members + ylo * members]).astype(jnp.int32)
    keep, send, part, right_own = project(
        place, gathered, hidden_all, target_all, right_local, projected, 32
    )

    near = lax.all_to_all(part, ("ylo", "core", "x", "yhi"), 0, 0, tiled=True)
    near, send = lax.optimization_barrier((near, send))
    recv = lax.ppermute(send, "ylo", SWAP)
    near = near.reshape(2, 2, 8, 2 * members).sum(axis=(0, 2)).reshape(1, 1, 4 * members)
    reward = lax.all_to_all(jnp.broadcast_to(near, (16, 1, 4 * members)), "z", 0, 0, tiled=True)

    step, up_out, fitness = step_product(
        place, reward, left_all, right_own, right_other, keep, recv, members
    )
    return (up_out, step, fitness.reshape(members))


def solution(mesh):
    fine = Mesh(mesh.devices.reshape(SIZES), AXES)
    pop = ("ylo", "z", "core")
    shard = ("x", "yhi")
    in_specs = (P(pop, None), P(pop, shard), P(pop, None), P(pop, shard), P(pop, shard))
    out_specs = (P(pop, shard), P(pop, shard), P(pop))
    return jax.shard_map(local, mesh=fine, in_specs=in_specs, out_specs=out_specs, check_vma=False)
```

time: 166 us -> 160 us (0.964)
  blocking collectives: 38.1 us -> 66.8 us
  waiting for transfers between devices: 35.7 us -> 19.2 us
  starting transfers between devices: 47.1 us -> 33.3 us
  Pallas kernels: 13.7 us -> 9.93 us
    all_to_all x0 -> x2, blocking collectives: none -> 30.8 us  [the longest x1 18 us: local(): lax.all_to_all(jnp.broadcast_to(near, (16, 1, 4 * members)), 'z', 0, 0, t...]
    all_to_all x2 -> x0, waiting for transfers between devices: 17.5 us -> none  [the longest x1 10.6 us: local(): lax.all_to_all(jnp.broadcast_to(near, (16, 1, 4 * members)), 'z', 0, 0, t...]
    all_to_all x2 -> x0, starting transfers between devices: 12.9 us -> none  [the longest x1 6.9 us: local(): near = lax.all_to_all(part, ('ylo', 'core', 'x', 'yhi'), 0, 0, tiled=True)]
    all_gather x1, waiting for transfers between devices: 9.77 us -> 16.7 us  [local(): gathered = lax.all_gather(packed, ('z', 'core'), axis=0, tiled=False)]
    ppermute x1, waiting for transfers between devices: 5.87 us -> 0.01 us  [local(): target_recv = lax.ppermute(other(target_b), 'ylo', SWAP)]
    pallas_call x2, Pallas kernels: 13.7 us -> 9.93 us  [the longest x1 7.65 us: project(): pl.pallas_call(project_kernel, in_specs=[SMEM, ANY, VMEM, VMEM, VMEM, VME...]
    all_gather x1, blocking collectives: 38.1 us -> 36.1 us  [local(): right_other = lax.all_gather(far, ('z', 'core'), axis=0, tiled=False)]
    concatenate x2 -> x5, other arithmetic: 0.73 us -> 2.71 us  [the longest x1 1.75 us: local(): target_all = jnp.concatenate([own(target_b), target_recv], axis=0)]
  transfers between devices with their start and end apart: 9 -> 7, of which waited for: 5 -> 2; matrix products, arithmetic and copies ran while one was open for 7% -> 7% of each run, Pallas kernels for 2% -> 0%
where the time goes in v3:
time: 160 us; the launch traced here: 159 us
  blocking collectives  66.8 us (42%)
  starting transfers between devices  33.3 us (21%)
  waiting for transfers between devices  19.2 us (12%)
  between operations  14.2 us (9%)
  Pallas kernels  9.93 us (6%)
  local copies, waits for them, and re-layouts  7.89 us (5%)
  other arithmetic  7.25 us (5%)
    all_gather x1, blocking collectives, local(): right_other = lax.all_gather(far, ('z', 'core'), axis=0, tiled=False)  36.1 us
    all_to_all x1, starting transfers between devices, local(): lax.all_to_all(left_split, ('ylo', 'z', 'core'), 0, 0, tiled=True)  18.3 us
    all_to_all x1, blocking collectives, local(): lax.all_to_all(jnp.broadcast_to(near, (16, 1, 4 * members)), 'z', 0, 0, t...  18 us
    all_gather x1, waiting for transfers between devices, local(): gathered = lax.all_gather(packed, ('z', 'core'), axis=0, tiled=False)  16.7 us
    all_to_all x1, blocking collectives, local(): near = lax.all_to_all(part, ('ylo', 'core', 'x', 'yhi'), 0, 0, tiled=True)  12.7 us
    pallas_call x1, Pallas kernels, project(): pl.pallas_call(project_kernel, in_specs=[SMEM, ANY, VMEM, VMEM, VMEM, VME...  7.65 us
    ppermute x1, starting transfers between devices, local(): lax.ppermute(jnp.concatenate([other(weight), sent, mine], axis=0), 'ylo',...  4.03 us
    ppermute x1, starting transfers between devices, local(): projected_recv = lax.ppermute(projected_own, 'ylo', SWAP)  3.4 us
  transfers between devices with their start and end apart: 7, of which 2 were waited for; matrix products, arithmetic and copies ran while one was open for 7% of the time, Pallas kernels for 0%

profile of v3, /device:TPU:1, one launch (start us, length us, event | category | flops | bytes accessed | tf_op | source)
XLA Modules:
  0.0 159.1 jit_solution(17140062451281317792)
XLA Ops:
  7.2 0.0 copy-start.1
  7.2 0.0 all-gather.3.cloned.1.call-start
  7.2 0.8 broadcast_select_fusion.5
  8.0 1.0 broadcast_select_fusion.3
  9.0 0.0 copy-start.2
  9.1 4.0 %collective-permute-start = (bf16[80,896]{1,0:T(8,128)(2,1)S(1)}, bf16[80,896]{1,0:T(8,128)(2,1)S(1)}, u32[]{:S(2)}, u32[]{:S(2)}) collective-permute-start(bf16[80,896]{1,0:T(8,128)(2,1)S(1)} %pad_maximum_fusion.3), channel_id=1, source_target_pairs={{0,256},{256,0},{1,257},{257,1},{2,258},{258,2},{3,259},{259,3},{4... | collective-permute-start | bytes 430088 | tf_op jit(solution)/shard_map/ppermute | solution.py:184
  13.1 2.5 %collective-permute-done = bf16[80,896]{1,0:T(8,128)(2,1)S(1)} collective-permute-done((bf16[80,896]{1,0:T(8,128)(2,1)S(1)}, bf16[80,896]{1,0:T(8,128)(2,1)S(1)}, u32[]{:S(2)}, u32[]{:S(2)}) %collective-permute-start) | collective-permute-done | bytes 143392 | tf_op jit(solution)/shard_map/ppermute | solution.py:184
  15.6 0.6 fusion.2
  16.3 0.7 pad_maximum_fusion.2
  17.0 0.0 all-gather.3.cloned.1.call-update
  17.0 0.1 pad_add_fusion.place
  17.1 0.0 copy-done.1
  17.1 0.7 copy.27
  17.8 3.4 %collective-permute-start.1 = (bf16[128,4096]{0,1:T(8,128)(2,1)S(1)}, bf16[128,4096]{0,1:T(8,128)(2,1)S(1)}, u32[]{:S(2)}, u32[]{:S(2)}) collective-permute-start(bf16[128,4096]{0,1:T(8,128)(2,1)S(1)} %copy.27), channel_id=1, source_target_pairs={{0,256},{256,0},{1,257},{257,1},{2,258},{258,2},{3,259},{259,3},{4... | collective-permute-start | bytes 3145736 | tf_op jit(solution)/shard_map/ppermute | solution.py:197
  21.1 0.0 copy-done.2
  21.1 0.2 reshape.106
  21.3 0.1 copy.29
  21.4 0.8 reshape.115
  22.2 18.3 %all-to-all-start = ((bf16[64,2,256]{2,1,0:T(2,128)(2,1)}), bf16[64,2,256]{2,1,0:T(2,128)(2,1)}, u32[]{:S(2)}, u32[]{:S(2)}) async-start(bf16[64,2,256]{2,1,0:T(2,128)(2,1)} %reshape.115), calls=%async_computation | async-start | bytes 131072 | tf_op jit(solution)/shard_map/all_to_all | solution.py:216
  40.5 0.5 fusion
  41.0 0.1 mul.33
  41.1 3.4 %collective-permute-start.3 = (f32[128,1]{0,1:T(1,128)S(1)}, f32[128,1]{0,1:T(1,128)S(1)}, u32[]{:S(2)}, u32[]{:S(2)}) collective-permute-start(f32[128,1]{0,1:T(1,128)S(1)} %mul.33), channel_id=1, source_target_pairs={{0,256},{256,0},{1,257},{257,1},{2,258},{258,2},{3,259},{259,3},{4... | collective-permute-start | bytes 1544 | tf_op jit(solution)/shard_map/ppermute | solution.py:208
  44.5 1.8 %broadcast_select_fusion.1 = (bf16[128,896]{1,0:T(8,128)(2,1)S(1)}, bf16[128,896]{1,0:T(8,128)(2,1)}) fusion(pred[]{:T(512)S(6)} %eq.3, bf16[128,1792]{1,0:T(8,128)(2,1)} %param.9), kind=kLoop, calls=%fused_computation.5 | loop fusion | flops 229376 | bytes 917505 | tf_op jit(solution)/shard_map/jit(_where)/select_n | solution.py:173
  46.3 1.9 %collective-permute-start.2 = (bf16[128,896]{1,0:T(8,128)(2,1)}, bf16[128,896]{1,0:T(8,128)(2,1)}, u32[]{:S(2)}, u32[]{:S(2)}) collective-permute-start(bf16[128,896]{1,0:T(8,128)(2,1)} %get-tuple-element.38), channel_id=1, source_target_pairs={{0,256},{256,0},{1,257},{257,1},{2,258},{258,2},{3,259},{259,3},{4... | collective-permute-start | bytes 688136 | tf_op jit(solution)/shard_map/ppermute | solution.py:198
  48.2 0.8 maximum_select_fusion.2
  49.0 36.1 %all_gather.12.right_other = bf16[32,16,896]{2,1,0:T(8,128)(2,1)S(1)} all-gather(bf16[1,16,896]{2,1,0:T(8,128)(2,1)S(1)} %maximum_select_fusion.2), channel_id=1, replica_groups=mesh['ylo'=2,'z'=16,'core'=2,'x'=4,'yhi'=2] {'z','core'}, dimensions={0}, use_global_device_ids=true | all-gather | bytes 946176 | tf_op jit(solution)/shard_map/all_gather | solution.py:220
  85.1 0.0 collective-permute-done.3
  85.1 0.1 copy.32.projected
  85.2 0.0 collective-permute-done.2
  85.3 1.7 %pad_maximum_fusion.1.target = bf16[256,896]{1,0:T(8,128)(2,1)} fusion(bf16[128,896]{1,0:T(8,128)(2,1)} %collective-permute-done.2, bf16[128,896]{1,0:T(8,128)(2,1)S(1)} %get-tuple-element.37), kind=kLoop, calls=%fused_computation.1 | loop fusion | flops 917504 | bytes 917504 | tf_op jit(solution)/shard_map/concatenate | solution.py:210
  87.0 0.0 all-to-all-done
  87.0 1.0 reshape.116
  88.0 0.0 collective-permute-done.1
  88.1 0.2 pad_maximum_fusion
  88.3 0.1 copy.28
  88.4 2.9 %copy.31.hidden = bf16[256,4096]{1,0:T(8,128)(2,1)} copy(bf16[256,4096]{0,1:T(8,128)(2,1)S(1)} %bitcast.23) | data formatting | bytes 4194304 | tf_op jit(solution)/shard_map/optimization_barrier | solution.py:222
  91.4 16.7 %all-gather.3.cloned.1.call-done = bf16[4608,896]{1,0:T(8,128)(2,1)} async-done(((bf16[144,896]{1,0:T(8,128)(2,1)}), bf16[4608,896]{1,0:T(8,128)(2,1)}) %all-gather.3.cloned.1.call-update) | async-done | bytes 8257552 | tf_op jit(solution)/shard_map/all_gather | solution.py:192
  108.0 7.6 %shard_map.76 = (bf16[128,896]{1,0:T(8,128)(2,1)S(1)}, bf16[128,896]{1,0:T(8,128)(2,1)S(1)}, f32[32,1,16]{2,1,0:T(1,128)S(1)}, bf16[32,16,896]{2,1,0:T(8,128)(2,1)}) custom-call(s32[2]{0:T(128)S(1)} %pad_add_fusion.place, bf16[32,144,896]{2,1,0:T(8,128)(2,1)} %bitcast.24, bf16[256,4096]{1,0:T(8,128)(2,1)} %copy.31.hidden, ...), custom_call_target="tpu_custom_call" | custom-call | flops 1879048192 | bytes 7340032 | tf_op jit(solution)/shard_map/pallas_call | solution.py:76
  115.7 12.7 %all_to_all.15 = f32[32,1,16]{2,1,0:T(1,128)S(1)} all-to-all(f32[32,1,16]{2,1,0:T(1,128)S(1)} %get-tuple-element.26), channel_id=1, replica_groups=mesh['ylo'=2,'z'=16,'core'=2,'x'=4,'yhi'=2] {'ylo','core','x','yhi'}, dimensions={0} | all-to-all | bytes 4096 | tf_op jit(solution)/shard_map/all_to_all | solution.py:228
  128.4 2.2 %collective-permute-start.4 = (bf16[128,896]{1,0:T(8,128)(2,1)S(1)}, bf16[128,896]{1,0:T(8,128)(2,1)S(1)}, u32[]{:S(2)}, u32[]{:S(2)}) collective-permute-start(bf16[128,896]{1,0:T(8,128)(2,1)S(1)} %get-tuple-element.33), channel_id=1, source_target_pairs={{0,256},{256,0},{1,257},{257,1},{2,258},{258,2},{3,259},{259,3},{4... | collective-permute-start | bytes 688136 | tf_op jit(solution)/shard_map/ppermute | solution.py:230
  130.7 0.1 broadcast_in_dim.7
  130.8 18.0 %all_to_all.16.reward = f32[16,1,32]{2,1,0:T(1,128)S(1)} all-to-all(f32[16,1,32]{2,1,0:T(1,128)S(1)} %broadcast_in_dim.8), channel_id=1, replica_groups=mesh['ylo'=2,'z'=16,'core'=2,'x'=4,'yhi'=2] {'z'}, dimensions={0} | all-to-all | bytes 4096 | tf_op jit(solution)/shard_map/all_to_all | solution.py:232
  148.8 0.0 collective-permute-done.4.recv
  148.8 0.0 copy-start
  148.8 1.2 copy-done
  150.0 2.3 %shard_map.77 = (f32[64,1792]{1,0:T(8,128)}, bf16[128,1792]{1,0:T(8,128)(2,1)}, f32[1,8]{1,0:T(1,128)}) custom-call(s32[2]{0:T(128)S(1)} %pad_add_fusion.place, f32[16,1,32]{2,1,0:T(1,128)S(1)} %all_to_all.16.reward, bf16[512,64]{1,0:T(8,128)(2,1)S(1)} %bitcast.21, bf16[32,16,896]{2,1,0:T(8,128)(2,1)S(1)} %copy-done, ...), custom_call_target="tpu_custom_call" | custom-call | flops 234881024 | bytes 2293760 | tf_op jit(solution)/shard_map/pallas_call | solution.py:143
  (9 shorter events, 0.1 us)
Async XLA Ops:
  7.2 9.9 %copy-start.1 = (bf16[128,4096]{1,0:T(8,128)(2,1)S(1)}, bf16[128,4096]{1,0:T(8,128)(2,1)}, u32[]{:S(2)}) copy-start(bf16[128,4096]{1,0:T(8,128)(2,1)} %param.5) | copy-start | bytes 3145732
  7.2 100.9 %all-gather.3.cloned.1.call-start = ((), (), s32[]{:S(2)}) async-start(), calls=%async_computation.3 | async-start | bytes 8515584 | tf_op jit(solution)/shard_map/all_gather | solution.py:192
  9.0 12.1 %copy-start.2 = (bf16[8,4096]{1,0:T(8,128)(2,1)S(1)}, bf16[8,4096]{1,0:T(8,128)(2,1)}, u32[]{:S(2)}) copy-start(bf16[8,4096]{1,0:T(8,128)(2,1)} %param.7) | copy-start | bytes 196612
  9.1 6.5 %collective-permute-start = (bf16[80,896]{1,0:T(8,128)(2,1)S(1)}, bf16[80,896]{1,0:T(8,128)(2,1)S(1)}, u32[]{:S(2)}, u32[]{:S(2)}) collective-permute-start(bf16[80,896]{1,0:T(8,128)(2,1)S(1)} %pad_maximum_fusion.3), channel_id=1, source_target_pairs={{0,256},{256,0},{1,257},{257,1},{2,258},{258,2},{3,259},{259,3},{4... | collective-permute-start | bytes 430088 | tf_op jit(solution)/shard_map/ppermute | solution.py:184
  17.8 70.3 %collective-permute-start.1 = (bf16[128,4096]{0,1:T(8,128)(2,1)S(1)}, bf16[128,4096]{0,1:T(8,128)(2,1)S(1)}, u32[]{:S(2)}, u32[]{:S(2)}) collective-permute-start(bf16[128,4096]{0,1:T(8,128)(2,1)S(1)} %copy.27), channel_id=1, source_target_pairs={{0,256},{256,0},{1,257},{257,1},{2,258},{258,2},{3,259},{259,3},{4... | collective-permute-start | bytes 3145736 | tf_op jit(solution)/shard_map/ppermute | solution.py:197
  22.2 64.8 %all-to-all-start = ((bf16[64,2,256]{2,1,0:T(2,128)(2,1)}), bf16[64,2,256]{2,1,0:T(2,128)(2,1)}, u32[]{:S(2)}, u32[]{:S(2)}) async-start(bf16[64,2,256]{2,1,0:T(2,128)(2,1)} %reshape.115), calls=%async_computation | async-start | bytes 131072 | tf_op jit(solution)/shard_map/all_to_all | solution.py:216
  41.1 44.0 %collective-permute-start.3 = (f32[128,1]{0,1:T(1,128)S(1)}, f32[128,1]{0,1:T(1,128)S(1)}, u32[]{:S(2)}, u32[]{:S(2)}) collective-permute-start(f32[128,1]{0,1:T(1,128)S(1)} %mul.33), channel_id=1, source_target_pairs={{0,256},{256,0},{1,257},{257,1},{2,258},{258,2},{3,259},{259,3},{4... | collective-permute-start | bytes 1544 | tf_op jit(solution)/shard_map/ppermute | solution.py:208
  46.3 39.0 %collective-permute-start.2 = (bf16[128,896]{1,0:T(8,128)(2,1)}, bf16[128,896]{1,0:T(8,128)(2,1)}, u32[]{:S(2)}, u32[]{:S(2)}) collective-permute-start(bf16[128,896]{1,0:T(8,128)(2,1)} %get-tuple-element.38), channel_id=1, source_target_pairs={{0,256},{256,0},{1,257},{257,1},{2,258},{258,2},{3,259},{259,3},{4... | collective-permute-start | bytes 688136 | tf_op jit(solution)/shard_map/ppermute | solution.py:198
  128.4 20.4 %collective-permute-start.4 = (bf16[128,896]{1,0:T(8,128)(2,1)S(1)}, bf16[128,896]{1,0:T(8,128)(2,1)S(1)}, u32[]{:S(2)}, u32[]{:S(2)}) collective-permute-start(bf16[128,896]{1,0:T(8,128)(2,1)S(1)} %get-tuple-element.33), channel_id=1, source_target_pairs={{0,256},{256,0},{1,257},{257,1},{2,258},{258,2},{3,259},{259,3},{4... | collective-permute-start | bytes 688136 | tf_op jit(solution)/shard_map/ppermute | solution.py:230
  148.8 1.2 copy-start
Sparse Core Ops, SparseCore 0:
  17.1 90.8 all-gather.2

commit v4 on v3

--- a/solution.py
+++ b/solution.py
@@ -15,78 +15,85 @@
 
 
 def project_kernel(
-    place, gathered, hidden, target, right, projected, keep, send, reward, portion, total, held, sems
+    place, gathered, hidden_hbm, target_hbm, right, projected, keep, send, reward, held, hidden, target, sems
 ):
-    chunks, slabs, width, cols = held.shape
+    blocks, width, _ = held.shape[1:]
+    cols = target.shape[1]
+    rows, features = hidden.shape
+    load_hidden = pltpu.make_async_copy(hidden_hbm, hidden, sems.at[0])
+    load_hidden.start()
+    members = right.shape[0]
+    tokens = rows // members
+    spans = column_spans(cols)
     copies = []
-    for i in range(chunks):
+    for i, (at, size) in enumerate(spans):
         copy = pltpu.make_async_copy(
-            gathered.at[pl.ds(i * slabs, slabs), pl.ds(0, width), :], held.at[i], sems.at[i]
+            gathered.at[:, pl.ds(0, width), pl.ds(at, size)],
+            held.at[i, :, :, pl.ds(0, size)],
+            sems.at[2 + i],
         )
         copy.start()
         copies.append(copy)
-    last = pltpu.make_async_copy(
-        gathered.at[:, pl.ds(width, portion.shape[1]), :], portion, sems.at[chunks]
-    )
-    last.start()
-    span = slabs * width
-    for i in range(chunks):
+        if i == 0:
+            load_target = pltpu.make_async_copy(target_hbm, target, sems.at[1])
+            load_target.start()
+    scale = projected[...].reshape(members, tokens, 1)
+    summed = jnp.zeros((members, 1), jnp.float32)
+    load_hidden.wait()
+    for i, (at, size) in enumerate(spans):
         copies[i].wait()
-        part = jnp.dot(
-            hidden[:, i * span : (i + 1) * span],
-            held[i].reshape(span, cols),
+        if i == 0:
+            load_target.wait()
+        base = jnp.dot(
+            hidden[...],
+            held[i, :, :, :size].reshape(features, size),
             preferred_element_type=jnp.float32,
-        )
-        if i == 0:
-            total[...] = part
-        else:
-            total[...] += part
-    rows = total.shape[0]
-    members = right.shape[0]
-    tokens = rows // members
-    base = total[...].reshape(members, tokens, cols)
-    factor = right[...].astype(jnp.float32)
-    value = base + projected[...].reshape(members, tokens, 1) * factor[:, None, :]
-    up = value.reshape(rows, cols).astype(jnp.bfloat16)
-    keep[...] = up[: rows // 2]
-    send[...] = up[rows // 2 :]
-    aim = target[...].astype(jnp.float32).reshape(members, tokens, cols)
-    gain = value * (0.5 + 0.5 * jnp.tanh(0.5 * value)) * aim
-    summed = jnp.sum(jnp.sum(gain, axis=1), axis=-1, keepdims=True)
+        ).reshape(members, tokens, size)
+        factor = right[:, at : at + size].astype(jnp.float32)
+        value = base + scale * factor[:, None, :]
+        up = value.reshape(rows, size).astype(jnp.bfloat16)
+        keep[:, at : at + size] = up[: rows // 2]
+        send[:, at : at + size] = up[rows // 2 :]
+        aim = target[:, at : at + size].astype(jnp.float32).reshape(members, tokens, size)
+        gain = value * (0.5 + 0.5 * jnp.tanh(0.5 * value)) * aim
+        summed += jnp.sum(jnp.sum(gain, axis=1), axis=-1, keepdims=True)
     shape = (members, reward.shape[-1])
     row = lax.broadcasted_iota(jnp.int32, shape, 0) + place[0] * (members // 2)
     row = jnp.where(row < members, row, row - members)
     spot = row == lax.broadcasted_iota(jnp.int32, shape, 1)
     line = jnp.sum(jnp.where(spot, summed, 0.0), axis=0, keepdims=True)
     reward[...] = jnp.broadcast_to(line[None], reward.shape)
-    last.wait()
-
-
+
+
+def column_spans(cols, size=256):
+    return [(at, min(size, cols - at)) for at in range(0, cols, size)]
+
+
+ANY = pl.BlockSpec(memory_space=pl.ANY)
 VMEM = pl.BlockSpec(memory_space=pltpu.VMEM)
 SMEM = pl.BlockSpec(memory_space=pltpu.SMEM)
-ANY = pl.BlockSpec(memory_space=pl.ANY)
 
 
 def project(place, gathered, hidden, target, right, projected, peers):
-    blocks, depth, cols = gathered.shape
+    blocks, _, cols = gathered.shape
     rows, features = hidden.shape
     members = right.shape[0]
-    slabs = 4
     width = features // blocks
+    spans = column_spans(cols)
     return pl.pallas_call(
         project_kernel,
-        in_specs=[SMEM, ANY, VMEM, VMEM, VMEM, VMEM],
-        out_specs=[VMEM, VMEM, VMEM, VMEM],
+        in_specs=[SMEM, ANY, ANY, ANY, VMEM, VMEM],
+        out_specs=[VMEM, VMEM, VMEM],
         out_shape=[
             jax.ShapeDtypeStruct((rows // 2, cols), jnp.bfloat16),
             jax.ShapeDtypeStruct((rows // 2, cols), jnp.bfloat16),
             jax.ShapeDtypeStruct((peers, 1, members), jnp.float32),
-            jax.ShapeDtypeStruct((blocks, depth - width, cols), jnp.bfloat16),
         ],
         scratch_shapes=[
-            pltpu.VMEM((rows, cols), jnp.float32),
-            pltpu.VMEM((blocks // slabs, slabs, width, cols), jnp.bfloat16),
-            pltpu.SemaphoreType.DMA((blocks // slabs + 1,)),
+            pltpu.VMEM((len(spans), blocks, width, spans[0][1]), jnp.bfloat16),
+            pltpu.VMEM(hidden.shape, jnp.bfloat16),
+            pltpu.VMEM(target.shape, jnp.bfloat16),
+            pltpu.SemaphoreType.DMA((len(spans) + 2,)),
         ],
         compiler_params=pltpu.CompilerParams(vmem_limit_bytes=53 * 1024 * 1024),
         cost_estimate=pl.CostEstimate(
@@ -97,14 +104,17 @@
     )(place, gathered, hidden, target, right, projected)
 
 
-def step_kernel(place, reward, left, right_own, right_other, keep, recv, out, up, fitness):
+def step_kernel(place, reward, left, gathered, right_other, out, fitness, right_own, sem):
+    count = right_own.shape[1]
+    copy = pltpu.make_async_copy(
+        gathered.at[:, pl.ds(gathered.shape[1] - count, count), :], right_own, sem
+    )
+    copy.start()
     members, depth = left.shape
     blocks, _, lanes = reward.shape
     half = right_own.shape[2]
     own_at = pl.multiple_of(place[0] * half, 128)
     other_at = pl.multiple_of((1 - place[0]) * half, 128)
-    up[:, pl.ds(own_at, half)] = keep[...]
-    up[:, pl.ds(other_at, half)] = recv[...]
     value = reward[...].reshape(blocks, lanes)
     total = jnp.sum(jnp.sum(value, axis=0, keepdims=True), axis=1, keepdims=True)
     centered = value - total * (1.0 / members)
@@ -134,28 +144,32 @@
         out[:, pl.ds(at, half)] = (product[:depth] + product[depth:]) * (1.0 / math.sqrt(members))
 
     multiply(right_other[...], other_at)
+    copy.wait()
     multiply(right_own[...], own_at)
 
 
-def step_product(place, reward, left, right_own, right_other, keep, recv, own):
+def step_product(place, reward, left, gathered, right_other, own):
     members, depth = left.shape
     half = right_other.shape[2]
     return pl.pallas_call(
         step_kernel,
-        in_specs=[SMEM, VMEM, VMEM, VMEM, VMEM, VMEM, VMEM],
-        out_specs=[VMEM, VMEM, VMEM],
+        in_specs=[SMEM, VMEM, VMEM, ANY, VMEM],
+        out_specs=[VMEM, VMEM],
         out_shape=[
             jax.ShapeDtypeStruct((depth, 2 * half), jnp.float32),
-            jax.ShapeDtypeStruct((keep.shape[0], 2 * half), jnp.bfloat16),
             jax.ShapeDtypeStruct((1, own), jnp.float32),
         ],
-        compiler_params=pltpu.CompilerParams(vmem_limit_bytes=24 * 1024 * 1024),
+        scratch_shapes=[
+            pltpu.VMEM(right_other.shape, jnp.bfloat16),
+            pltpu.SemaphoreType.DMA,
+        ],
+        compiler_params=pltpu.CompilerParams(vmem_limit_bytes=53 * 1024 * 1024),
         cost_estimate=pl.CostEstimate(
-            flops=8 * depth * members * half,
+            flops=128 * depth * members * half,
             bytes_accessed=members * half * 4 + depth * half * 8,
             transcendentals=0,
         ),
-    )(place, reward, left, right_own, right_other, keep, recv)
+    )(place, reward, left, gathered, right_other)
 
 
 def local(hidden, weight, left_factors, right_factors, target):
@@ -184,16 +198,17 @@
     slab_recv = lax.ppermute(
         jnp.concatenate([other(weight), sent, mine], axis=0), "ylo", SWAP
     )
-    theirs, theirs_far = slab_recv[depth : depth + members], slab_recv[depth + members :]
-    right_local = jnp.concatenate([mine, theirs], axis=0)
+    theirs = slab_recv[depth : depth + members]
     packed = jnp.concatenate(
         [order(own(weight), slab_recv[:depth]), order(mine, theirs)], axis=0
     )
     gathered = lax.all_gather(packed, ("z", "core"), axis=0, tiled=False)
 
-    after, hidden_b, left_b, target_b, sent, theirs_far = lax.optimization_barrier(
-        (packed, hidden, left_factors, target, sent, theirs_far)
-    )
+    _, hidden_b, left_b, target_b, sent, slab_b, mine_b = lax.optimization_barrier(
+        (packed, hidden, left_factors, target, sent, slab_recv, mine)
+    )
+    theirs_far = slab_b[depth + members :]
+    right_local = jnp.concatenate([mine_b, slab_b[depth : depth + members]], axis=0)
     rows_recv = lax.ppermute(hidden_b, "ylo", SWAP)
     target_recv = lax.ppermute(other(target_b), "ylo", SWAP)
     projected_own = (
@@ -221,19 +236,18 @@
 
     hidden_all, left_all, right_other = lax.optimization_barrier((hidden_all, left_all, right_other))
     place = jnp.stack([ylo, z * 4 * members + core * 2 * members + ylo * members]).astype(jnp.int32)
-    keep, send, part, right_own = project(
+    keep, send, part = project(
         place, gathered, hidden_all, target_all, right_local, projected, 32
     )
 
     near = lax.all_to_all(part, ("ylo", "core", "x", "yhi"), 0, 0, tiled=True)
-    near, send = lax.optimization_barrier((near, send))
+    near = near.reshape(2, 2, 8, 2 * members).sum(axis=(0, 2)).reshape(1, 1, 4 * members)
+    wide = jnp.broadcast_to(near, (16, 1, 4 * members))
     recv = lax.ppermute(send, "ylo", SWAP)
-    near = near.reshape(2, 2, 8, 2 * members).sum(axis=(0, 2)).reshape(1, 1, 4 * members)
-    reward = lax.all_to_all(jnp.broadcast_to(near, (16, 1, 4 * members)), "z", 0, 0, tiled=True)
-
-    step, up_out, fitness = step_product(
-        place, reward, left_all, right_own, right_other, keep, recv, members
-    )
+    reward = lax.all_to_all(wide, "z", 0, 0, tiled=True)
+
+    step, fitness = step_product(place, reward, left_all, gathered, right_other, members)
+    up_out = order(keep, recv, axis=1)
     return (up_out, step, fitness.reshape(members))
 
 

time: 160 us -> 160 us (level)
  blocking collectives: 66.8 us -> 52.4 us
  waiting for transfers between devices: 19.2 us -> 28.7 us
  starting transfers between devices: 33.3 us -> 39.8 us
  local copies, waits for them, and re-layouts: 7.89 us -> 5.9 us
  Pallas kernels: 9.93 us -> 11.7 us
    all_to_all x1 -> x0, blocking collectives: 18 us -> none  [local(): lax.all_to_all(jnp.broadcast_to(near, (16, 1, 4 * members)), 'z', 0, 0, t...]
    all_to_all x0 -> x1, waiting for transfers between devices: none -> 9 us  [local(): reward = lax.all_to_all(wide, 'z', 0, 0, tiled=True)]
    all_to_all x0 -> x1, starting transfers between devices: none -> 6.69 us  [local(): reward = lax.all_to_all(wide, 'z', 0, 0, tiled=True)]
    all_gather x1, blocking collectives: 36.1 us -> 38.9 us  [local(): right_other = lax.all_gather(far, ('z', 'core'), axis=0, tiled=False)]
    ppermute x1, waiting for transfers between devices: 0.01 us -> 2.74 us  [local(): projected_recv = lax.ppermute(projected_own, 'ylo', SWAP)]
    all_gather x1, waiting for transfers between devices: 16.7 us -> 14.5 us  [local(): gathered = lax.all_gather(packed, ('z', 'core'), axis=0, tiled=False)]
    unnamed x8, local copies, waits for them, and re-layouts: 2.96 us -> 0.94 us
    pallas_call x2, Pallas kernels: 9.93 us -> 11.7 us  [the longest x1 8.28 us: project(): pl.pallas_call(project_kernel, in_specs=[SMEM, ANY, ANY, ANY, VMEM, VMEM]...]
  transfers between devices with their start and end apart: 7 -> 8, of which waited for: 2 -> 4; matrix products, arithmetic and copies ran while one was open for 7% -> 5% of each run, Pallas kernels for 0% -> 2%
where the time goes in v4:
time: 160 us; the launch traced here: 159 us
  blocking collectives  52.4 us (33%)
  starting transfers between devices  39.8 us (25%)
  waiting for transfers between devices  28.7 us (18%)
  between operations  14.3 us (9%)
  Pallas kernels  11.7 us (7%)
  other arithmetic  5.91 us (4%)
  local copies, waits for them, and re-layouts  5.9 us (4%)
    all_gather x1, blocking collectives, local(): right_other = lax.all_gather(far, ('z', 'core'), axis=0, tiled=False)  38.9 us
    all_to_all x1, starting transfers between devices, local(): lax.all_to_all(left_split, ('ylo', 'z', 'core'), 0, 0, tiled=True)  18.2 us
    all_gather x1, waiting for transfers between devices, local(): gathered = lax.all_gather(packed, ('z', 'core'), axis=0, tiled=False)  14.5 us
    all_to_all x1, blocking collectives, local(): near = lax.all_to_all(part, ('ylo', 'core', 'x', 'yhi'), 0, 0, tiled=True)  13.5 us
    all_to_all x1, waiting for transfers between devices, local(): reward = lax.all_to_all(wide, 'z', 0, 0, tiled=True)  9 us
    pallas_call x1, Pallas kernels, project(): pl.pallas_call(project_kernel, in_specs=[SMEM, ANY, ANY, ANY, VMEM, VMEM]...  8.28 us
    all_to_all x1, starting transfers between devices, local(): reward = lax.all_to_all(wide, 'z', 0, 0, tiled=True)  6.69 us
    ppermute x1, starting transfers between devices, local(): lax.ppermute(jnp.concatenate([other(weight), sent, mine], axis=0), 'ylo',...  4.03 us
  transfers between devices with their start and end apart: 8, of which 4 were waited for; matrix products, arithmetic and copies ran while one was open for 5% of the time, Pallas kernels for 2%

profile of v4, /device:TPU:1, one launch (start us, length us, event | category | flops | bytes accessed | tf_op | source)
XLA Modules:
  0.0 159.3 jit_solution(14549735328420347113)
XLA Ops:
  7.2 0.0 copy-start
  7.2 0.0 all-gather.3.cloned.1.call-start
  7.2 0.8 broadcast_select_fusion.5
  8.0 1.0 broadcast_select_fusion.3
  9.0 0.0 copy-start.2
  9.1 4.0 %collective-permute-start = (bf16[80,896]{1,0:T(8,128)(2,1)S(1)}, bf16[80,896]{1,0:T(8,128)(2,1)S(1)}, u32[]{:S(2)}, u32[]{:S(2)}) collective-permute-start(bf16[80,896]{1,0:T(8,128)(2,1)S(1)} %pad_maximum_fusion.3), channel_id=1, source_target_pairs={{0,256},{256,0},{1,257},{257,1},{2,258},{258,2},{3,259},{259,3},{4... | collective-permute-start | bytes 430088 | tf_op jit(solution)/shard_map/ppermute | solution.py:198
  13.1 2.5 %collective-permute-done = bf16[80,896]{1,0:T(8,128)(2,1)S(1)} collective-permute-done((bf16[80,896]{1,0:T(8,128)(2,1)S(1)}, bf16[80,896]{1,0:T(8,128)(2,1)S(1)}, u32[]{:S(2)}, u32[]{:S(2)}) %collective-permute-start) | collective-permute-done | bytes 143392 | tf_op jit(solution)/shard_map/ppermute | solution.py:198
  15.6 0.0 copy-start.1
  15.7 0.7 pad_maximum_fusion.2
  16.4 0.0 all-gather.3.cloned.1.call-update
  16.4 0.1 pad_add_fusion.place
  16.5 0.0 copy-done
  16.5 0.7 copy.27
  17.2 3.4 %collective-permute-start.1 = (bf16[128,4096]{0,1:T(8,128)(2,1)S(1)}, bf16[128,4096]{0,1:T(8,128)(2,1)}, u32[]{:S(2)}, u32[]{:S(2)}) collective-permute-start(bf16[128,4096]{0,1:T(8,128)(2,1)S(1)} %copy.27), channel_id=1, source_target_pairs={{0,256},{256,0},{1,257},{257,1},{2,258},{258,2},{3,259},{259,3},{4... | collective-permute-start | bytes 3145736 | tf_op jit(solution)/shard_map/ppermute | solution.py:212
  20.5 0.0 copy-done.2
  20.5 0.2 reshape.106
  20.7 0.1 copy.29
  20.8 0.8 reshape.115
  21.6 18.2 %all-to-all-start = ((bf16[64,2,256]{2,1,0:T(2,128)(2,1)}), bf16[64,2,256]{2,1,0:T(2,128)(2,1)S(1)}, u32[]{:S(2)}, u32[]{:S(2)}) async-start(bf16[64,2,256]{2,1,0:T(2,128)(2,1)} %reshape.115), calls=%async_computation | async-start | bytes 131072 | tf_op jit(solution)/shard_map/all_to_all | solution.py:231
  39.8 0.0 copy-done.1
  39.8 0.1 broadcast_select_fusion.1
  39.8 3.4 %collective-permute-start.2 = (bf16[128,896]{1,0:T(8,128)(2,1)S(1)}, bf16[128,896]{1,0:T(8,128)(2,1)S(1)}, u32[]{:S(2)}, u32[]{:S(2)}) collective-permute-start(bf16[128,896]{1,0:T(8,128)(2,1)S(1)} %get-tuple-element.32), channel_id=1, source_target_pairs={{0,256},{256,0},{1,257},{257,1},{2,258},{258,2},{3,259},{259,3},{4... | collective-permute-start | bytes 688136 | tf_op jit(solution)/shard_map/ppermute | solution.py:213
  43.3 0.5 fusion
  43.8 38.9 %all_gather.12.right_other = bf16[32,16,896]{2,1,0:T(8,128)(2,1)} all-gather(bf16[1,16,896]{2,1,0:T(8,128)(2,1)S(1)} %maximum_select_fusion.3), channel_id=1, replica_groups=mesh['ylo'=2,'z'=16,'core'=2,'x'=4,'yhi'=2] {'z','core'}, dimensions={0}, use_global_device_ids=true | all-gather | bytes 946176 | tf_op jit(solution)/shard_map/all_gather | solution.py:235
  82.7 0.1 mul.33
  82.8 1.9 %collective-permute-start.3 = (f32[128,1]{0,1:T(1,128)S(1)}, f32[128,1]{0,1:T(1,128)S(1)}, u32[]{:S(2)}, u32[]{:S(2)}) collective-permute-start(f32[128,1]{0,1:T(1,128)S(1)} %mul.33), channel_id=1, source_target_pairs={{0,256},{256,0},{1,257},{257,1},{2,258},{258,2},{3,259},{259,3},{4... | collective-permute-start | bytes 1544 | tf_op jit(solution)/shard_map/ppermute | solution.py:223
  84.7 2.7 %collective-permute-done.3 = f32[128,1]{0,1:T(1,128)S(1)} collective-permute-done((f32[128,1]{0,1:T(1,128)S(1)}, f32[128,1]{0,1:T(1,128)S(1)}, u32[]{:S(2)}, u32[]{:S(2)}) %collective-permute-start.3) | collective-permute-done | bytes 544 | tf_op jit(solution)/shard_map/ppermute | solution.py:223
  87.4 0.1 copy.32.projected
  87.6 0.0 collective-permute-done.2
  87.6 0.8 pad_maximum_fusion.1.target_hbm
  88.4 0.0 all-to-all-done
  88.4 0.1 reshape.116
  88.6 0.0 collective-permute-done.1
  88.6 1.5 pad_maximum_fusion
  90.1 0.1 copy.28
  90.2 2.9 %copy.31.hidden_hbm = bf16[256,4096]{1,0:T(8,128)(2,1)} copy(bf16[256,4096]{0,1:T(8,128)(2,1)S(1)} %bitcast.24) | data formatting | bytes 4194304 | tf_op jit(solution)/shard_map/optimization_barrier | solution.py:237
  93.2 14.5 %all-gather.3.cloned.1.call-done = bf16[4608,896]{1,0:T(8,128)(2,1)} async-done(((bf16[144,896]{1,0:T(8,128)(2,1)}), bf16[4608,896]{1,0:T(8,128)(2,1)}) %all-gather.3.cloned.1.call-update) | async-done | bytes 8257552 | tf_op jit(solution)/shard_map/all_gather | solution.py:205
  107.6 8.3 %shard_map.76 = (bf16[128,896]{1,0:T(8,128)(2,1)S(1)}, bf16[128,896]{1,0:T(8,128)(2,1)S(1)}, f32[32,1,16]{2,1,0:T(1,128)S(1)}) custom-call(s32[2]{0:T(128)S(1)} %pad_add_fusion.place, bf16[32,144,896]{2,1,0:T(8,128)(2,1)} %bitcast.25, bf16[256,4096]{1,0:T(8,128)(2,1)} %copy.31.hidden_hbm, bf16[256,896]{1,0:T(8,128)(2,1)} %pad_maximum_fusion.1.target_hbm, ...), custom_call_target="tpu_custom_call" | custom-call | flops 1879048192 | bytes 7340032 | tf_op jit(solution)/shard_map/pallas_call | solution.py:83
  115.9 13.5 %all_to_all.15 = f32[32,1,16]{2,1,0:T(1,128)S(1)} all-to-all(f32[32,1,16]{2,1,0:T(1,128)S(1)} %get-tuple-element.26), channel_id=1, replica_groups=mesh['ylo'=2,'z'=16,'core'=2,'x'=4,'yhi'=2] {'ylo','core','x','yhi'}, dimensions={0} | all-to-all | bytes 4096 | tf_op jit(solution)/shard_map/all_to_all | solution.py:243
  129.5 0.1 broadcast_in_dim.7
  129.6 0.6 broadcast_in_dim.8
  130.2 6.7 %all-to-all-start.2 = ((f32[16,1,32]{2,1,0:T(1,128)}), f32[16,1,32]{2,1,0:T(1,128)S(1)}, u32[]{:S(2)}, u32[]{:S(2)}) async-start(f32[16,1,32]{2,1,0:T(1,128)} %broadcast_in_dim.8), calls=%async_computation.2 | async-start | bytes 16384 | tf_op jit(solution)/shard_map/all_to_all | solution.py:247
  136.9 2.2 %collective-permute-start.4 = (bf16[128,896]{1,0:T(8,128)(2,1)S(1)}, bf16[128,896]{1,0:T(8,128)(2,1)S(1)}, u32[]{:S(2)}, u32[]{:S(2)}) collective-permute-start(bf16[128,896]{1,0:T(8,128)(2,1)S(1)} %get-tuple-element.25), channel_id=1, source_target_pairs={{0,256},{256,0},{1,257},{257,1},{2,258},{258,2},{3,259},{259,3},{4... | collective-permute-start | bytes 688136 | tf_op jit(solution)/shard_map/ppermute | solution.py:246
  139.1 9.0 %all-to-all-done.2.reward = f32[16,1,32]{2,1,0:T(1,128)S(1)} async-done(((f32[16,1,32]{2,1,0:T(1,128)}), f32[16,1,32]{2,1,0:T(1,128)S(1)}, u32[]{:S(2)}, u32[]{:S(2)}) %all-to-all-start.2) | async-done | bytes 2080 | tf_op jit(solution)/shard_map/all_to_all | solution.py:247
  148.1 3.5 %shard_map.77 = (f32[64,1792]{1,0:T(8,128)}, f32[1,8]{1,0:T(1,128)}) custom-call(s32[2]{0:T(128)S(1)} %pad_add_fusion.place, f32[16,1,32]{2,1,0:T(1,128)S(1)} %all-to-all-done.2.reward, bf16[512,64]{1,0:T(8,128)(2,1)S(1)} %bitcast.22, bf16[32,144,896]{2,1,0:T(8,128)(2,1)} %bitcast.26, bf16[32,16,896]{2,1,0:T(8,128)(2,1)} %all_gather.12.right_other), custom_call_target="tpu_custom_call" | custom-call | flops 3758096384 | bytes 2293760 | tf_op jit(solution)/shard_map/pallas_call | solution.py:154
  151.6 0.0 collective-permute-done.4
  151.6 0.9 maximum_select_fusion
  (12 shorter events, 0.2 us)
Async XLA Ops:
  7.2 9.3 %copy-start = (bf16[128,4096]{1,0:T(8,128)(2,1)S(1)}, bf16[128,4096]{1,0:T(8,128)(2,1)}, u32[]{:S(2)}) copy-start(bf16[128,4096]{1,0:T(8,128)(2,1)} %param.5) | copy-start | bytes 3145732
  7.2 100.5 %all-gather.3.cloned.1.call-start = ((), (), s32[]{:S(2)}) async-start(), calls=%async_computation.3 | async-start | bytes 8515584 | tf_op jit(solution)/shard_map/all_gather | solution.py:205
  9.0 11.5 %copy-start.2 = (bf16[8,4096]{1,0:T(8,128)(2,1)S(1)}, bf16[8,4096]{1,0:T(8,128)(2,1)}, u32[]{:S(2)}) copy-start(bf16[8,4096]{1,0:T(8,128)(2,1)} %param.7) | copy-start | bytes 196612
  9.1 6.5 %collective-permute-start = (bf16[80,896]{1,0:T(8,128)(2,1)S(1)}, bf16[80,896]{1,0:T(8,128)(2,1)S(1)}, u32[]{:S(2)}, u32[]{:S(2)}) collective-permute-start(bf16[80,896]{1,0:T(8,128)(2,1)S(1)} %pad_maximum_fusion.3), channel_id=1, source_target_pairs={{0,256},{256,0},{1,257},{257,1},{2,258},{258,2},{3,259},{259,3},{4... | collective-permute-start | bytes 430088 | tf_op jit(solution)/shard_map/ppermute | solution.py:198
  15.6 24.2 %copy-start.1 = (bf16[128,1792]{1,0:T(8,128)(2,1)S(1)}, bf16[128,1792]{1,0:T(8,128)(2,1)}, u32[]{:S(2)}) copy-start(bf16[128,1792]{1,0:T(8,128)(2,1)} %param.9) | copy-start | bytes 1376260
  17.2 71.4 %collective-permute-start.1 = (bf16[128,4096]{0,1:T(8,128)(2,1)S(1)}, bf16[128,4096]{0,1:T(8,128)(2,1)}, u32[]{:S(2)}, u32[]{:S(2)}) collective-permute-start(bf16[128,4096]{0,1:T(8,128)(2,1)S(1)} %copy.27), channel_id=1, source_target_pairs={{0,256},{256,0},{1,257},{257,1},{2,258},{258,2},{3,259},{259,3},{4... | collective-permute-start | bytes 3145736 | tf_op jit(solution)/shard_map/ppermute | solution.py:212
  21.6 66.8 %all-to-all-start = ((bf16[64,2,256]{2,1,0:T(2,128)(2,1)}), bf16[64,2,256]{2,1,0:T(2,128)(2,1)S(1)}, u32[]{:S(2)}, u32[]{:S(2)}) async-start(bf16[64,2,256]{2,1,0:T(2,128)(2,1)} %reshape.115), calls=%async_computation | async-start | bytes 131072 | tf_op jit(solution)/shard_map/all_to_all | solution.py:231
  39.8 47.7 %collective-permute-start.2 = (bf16[128,896]{1,0:T(8,128)(2,1)S(1)}, bf16[128,896]{1,0:T(8,128)(2,1)S(1)}, u32[]{:S(2)}, u32[]{:S(2)}) collective-permute-start(bf16[128,896]{1,0:T(8,128)(2,1)S(1)} %get-tuple-element.32), channel_id=1, source_target_pairs={{0,256},{256,0},{1,257},{257,1},{2,258},{258,2},{3,259},{259,3},{4... | collective-permute-start | bytes 688136 | tf_op jit(solution)/shard_map/ppermute | solution.py:213
  82.8 4.7 %collective-permute-start.3 = (f32[128,1]{0,1:T(1,128)S(1)}, f32[128,1]{0,1:T(1,128)S(1)}, u32[]{:S(2)}, u32[]{:S(2)}) collective-permute-start(f32[128,1]{0,1:T(1,128)S(1)} %mul.33), channel_id=1, source_target_pairs={{0,256},{256,0},{1,257},{257,1},{2,258},{258,2},{3,259},{259,3},{4... | collective-permute-start | bytes 1544 | tf_op jit(solution)/shard_map/ppermute | solution.py:223
  130.2 17.9 %all-to-all-start.2 = ((f32[16,1,32]{2,1,0:T(1,128)}), f32[16,1,32]{2,1,0:T(1,128)S(1)}, u32[]{:S(2)}, u32[]{:S(2)}) async-start(f32[16,1,32]{2,1,0:T(1,128)} %broadcast_in_dim.8), calls=%async_computation.2 | async-start | bytes 16384 | tf_op jit(solution)/shard_map/all_to_all | solution.py:247
  136.9 14.7 %collective-permute-start.4 = (bf16[128,896]{1,0:T(8,128)(2,1)S(1)}, bf16[128,896]{1,0:T(8,128)(2,1)S(1)}, u32[]{:S(2)}, u32[]{:S(2)}) collective-permute-start(bf16[128,896]{1,0:T(8,128)(2,1)S(1)} %get-tuple-element.25), channel_id=1, source_target_pairs={{0,256},{256,0},{1,257},{257,1},{2,258},{258,2},{3,259},{259,3},{4... | collective-permute-start | bytes 688136 | tf_op jit(solution)/shard_map/ppermute | solution.py:246
Sparse Core Ops, SparseCore 0:
  16.5 91.0 all-gather.2

commit v5 on v3

--- a/solution.py
+++ b/solution.py
@@ -15,21 +15,25 @@
 
 
 def project_kernel(
-    place, gathered, hidden, target, right, projected, keep, send, reward, portion, total, held, sems
+    place, gathered, hidden_hbm, target_hbm, right, projected, keep, send, reward, total, held, hidden, target, sems
 ):
     chunks, slabs, width, cols = held.shape
+    rows = hidden.shape[0]
+    members = right.shape[0]
+    tokens = rows // members
+    load_hidden = pltpu.make_async_copy(hidden_hbm, hidden, sems.at[0])
+    load_hidden.start()
     copies = []
     for i in range(chunks):
         copy = pltpu.make_async_copy(
-            gathered.at[pl.ds(i * slabs, slabs), pl.ds(0, width), :], held.at[i], sems.at[i]
+            gathered.at[pl.ds(i * slabs, slabs), pl.ds(0, width), :], held.at[i], sems.at[2 + i]
         )
         copy.start()
         copies.append(copy)
-    last = pltpu.make_async_copy(
-        gathered.at[:, pl.ds(width, portion.shape[1]), :], portion, sems.at[chunks]
-    )
-    last.start()
+    load_target = pltpu.make_async_copy(target_hbm, target, sems.at[1])
+    load_target.start()
     span = slabs * width
+    load_hidden.wait()
     for i in range(chunks):
         copies[i].wait()
         part = jnp.dot(
@@ -41,25 +45,25 @@
             total[...] = part
         else:
             total[...] += part
-    rows = total.shape[0]
-    members = right.shape[0]
-    tokens = rows // members
-    base = total[...].reshape(members, tokens, cols)
-    factor = right[...].astype(jnp.float32)
-    value = base + projected[...].reshape(members, tokens, 1) * factor[:, None, :]
-    up = value.reshape(rows, cols).astype(jnp.bfloat16)
-    keep[...] = up[: rows // 2]
-    send[...] = up[rows // 2 :]
-    aim = target[...].astype(jnp.float32).reshape(members, tokens, cols)
-    gain = value * (0.5 + 0.5 * jnp.tanh(0.5 * value)) * aim
-    summed = jnp.sum(jnp.sum(gain, axis=1), axis=-1, keepdims=True)
+    load_target.wait()
+    scale = projected[...].reshape(members, tokens, 1)
+    summed = jnp.zeros((members, 1), jnp.float32)
+    for at in range(0, cols, 128):
+        base = total[:, at : at + 128].reshape(members, tokens, 128)
+        factor = right[:, at : at + 128].astype(jnp.float32)
+        value = base + scale * factor[:, None, :]
+        up = value.reshape(rows, 128).astype(jnp.bfloat16)
+        keep[:, at : at + 128] = up[: rows // 2]
+        send[:, at : at + 128] = up[rows // 2 :]
+        aim = target[:, at : at + 128].astype(jnp.float32).reshape(members, tokens, 128)
+        gain = value * (0.5 + 0.5 * jnp.tanh(0.5 * value)) * aim
+        summed += jnp.sum(jnp.sum(gain, axis=1), axis=-1, keepdims=True)
     shape = (members, reward.shape[-1])
     row = lax.broadcasted_iota(jnp.int32, shape, 0) + place[0] * (members // 2)
     row = jnp.where(row < members, row, row - members)
     spot = row == lax.broadcasted_iota(jnp.int32, shape, 1)
     line = jnp.sum(jnp.where(spot, summed, 0.0), axis=0, keepdims=True)
     reward[...] = jnp.broadcast_to(line[None], reward.shape)
-    last.wait()
 
 
 VMEM = pl.BlockSpec(memory_space=pltpu.VMEM)
@@ -68,25 +72,26 @@
 
 
 def project(place, gathered, hidden, target, right, projected, peers):
-    blocks, depth, cols = gathered.shape
+    blocks, _, cols = gathered.shape
     rows, features = hidden.shape
     members = right.shape[0]
-    slabs = 4
     width = features // blocks
+    slabs = blocks // 8
     return pl.pallas_call(
         project_kernel,
-        in_specs=[SMEM, ANY, VMEM, VMEM, VMEM, VMEM],
-        out_specs=[VMEM, VMEM, VMEM, VMEM],
+        in_specs=[SMEM, ANY, ANY, ANY, VMEM, VMEM],
+        out_specs=[VMEM, VMEM, VMEM],
         out_shape=[
             jax.ShapeDtypeStruct((rows // 2, cols), jnp.bfloat16),
             jax.ShapeDtypeStruct((rows // 2, cols), jnp.bfloat16),
             jax.ShapeDtypeStruct((peers, 1, members), jnp.float32),
-            jax.ShapeDtypeStruct((blocks, depth - width, cols), jnp.bfloat16),
         ],
         scratch_shapes=[
             pltpu.VMEM((rows, cols), jnp.float32),
             pltpu.VMEM((blocks // slabs, slabs, width, cols), jnp.bfloat16),
-            pltpu.SemaphoreType.DMA((blocks // slabs + 1,)),
+            pltpu.VMEM(hidden.shape, jnp.bfloat16),
+            pltpu.VMEM(target.shape, jnp.bfloat16),
+            pltpu.SemaphoreType.DMA((blocks // slabs + 2,)),
         ],
         compiler_params=pltpu.CompilerParams(vmem_limit_bytes=53 * 1024 * 1024),
         cost_estimate=pl.CostEstimate(
@@ -97,14 +102,12 @@
     )(place, gathered, hidden, target, right, projected)
 
 
-def step_kernel(place, reward, left, right_own, right_other, keep, recv, out, up, fitness):
+def step_kernel(place, reward, left, right_own, right_other, out, fitness):
     members, depth = left.shape
     blocks, _, lanes = reward.shape
     half = right_own.shape[2]
     own_at = pl.multiple_of(place[0] * half, 128)
     other_at = pl.multiple_of((1 - place[0]) * half, 128)
-    up[:, pl.ds(own_at, half)] = keep[...]
-    up[:, pl.ds(other_at, half)] = recv[...]
     value = reward[...].reshape(blocks, lanes)
     total = jnp.sum(jnp.sum(value, axis=0, keepdims=True), axis=1, keepdims=True)
     centered = value - total * (1.0 / members)
@@ -137,25 +140,24 @@
     multiply(right_own[...], own_at)
 
 
-def step_product(place, reward, left, right_own, right_other, keep, recv, own):
+def step_product(place, reward, left, right_own, right_other, own):
     members, depth = left.shape
     half = right_other.shape[2]
     return pl.pallas_call(
         step_kernel,
-        in_specs=[SMEM, VMEM, VMEM, VMEM, VMEM, VMEM, VMEM],
-        out_specs=[VMEM, VMEM, VMEM],
+        in_specs=[SMEM, VMEM, VMEM, VMEM, VMEM],
+        out_specs=[VMEM, VMEM],
         out_shape=[
             jax.ShapeDtypeStruct((depth, 2 * half), jnp.float32),
-            jax.ShapeDtypeStruct((keep.shape[0], 2 * half), jnp.bfloat16),
             jax.ShapeDtypeStruct((1, own), jnp.float32),
         ],
         compiler_params=pltpu.CompilerParams(vmem_limit_bytes=24 * 1024 * 1024),
         cost_estimate=pl.CostEstimate(
-            flops=8 * depth * members * half,
+            flops=128 * depth * members * half,
             bytes_accessed=members * half * 4 + depth * half * 8,
             transcendentals=0,
         ),
-    )(place, reward, left, right_own, right_other, keep, recv)
+    )(place, reward, left, right_own, right_other)
 
 
 def local(hidden, weight, left_factors, right_factors, target):
@@ -184,16 +186,17 @@
     slab_recv = lax.ppermute(
         jnp.concatenate([other(weight), sent, mine], axis=0), "ylo", SWAP
     )
-    theirs, theirs_far = slab_recv[depth : depth + members], slab_recv[depth + members :]
-    right_local = jnp.concatenate([mine, theirs], axis=0)
+    theirs = slab_recv[depth : depth + members]
     packed = jnp.concatenate(
         [order(own(weight), slab_recv[:depth]), order(mine, theirs)], axis=0
     )
     gathered = lax.all_gather(packed, ("z", "core"), axis=0, tiled=False)
 
-    after, hidden_b, left_b, target_b, sent, theirs_far = lax.optimization_barrier(
-        (packed, hidden, left_factors, target, sent, theirs_far)
-    )
+    _, hidden_b, left_b, target_b, sent, slab_b, mine_b = lax.optimization_barrier(
+        (packed, hidden, left_factors, target, sent, slab_recv, mine)
+    )
+    theirs_far = slab_b[depth + members :]
+    right_local = jnp.concatenate([mine_b, slab_b[depth : depth + members]], axis=0)
     rows_recv = lax.ppermute(hidden_b, "ylo", SWAP)
     target_recv = lax.ppermute(other(target_b), "ylo", SWAP)
     projected_own = (
@@ -221,19 +224,18 @@
 
     hidden_all, left_all, right_other = lax.optimization_barrier((hidden_all, left_all, right_other))
     place = jnp.stack([ylo, z * 4 * members + core * 2 * members + ylo * members]).astype(jnp.int32)
-    keep, send, part, right_own = project(
+    keep, send, part = project(
         place, gathered, hidden_all, target_all, right_local, projected, 32
     )
 
+    gathered, part = lax.optimization_barrier((gathered, part))
+    right_own = gathered[:, 2 * depth :]
     near = lax.all_to_all(part, ("ylo", "core", "x", "yhi"), 0, 0, tiled=True)
-    near, send = lax.optimization_barrier((near, send))
-    recv = lax.ppermute(send, "ylo", SWAP)
     near = near.reshape(2, 2, 8, 2 * members).sum(axis=(0, 2)).reshape(1, 1, 4 * members)
     reward = lax.all_to_all(jnp.broadcast_to(near, (16, 1, 4 * members)), "z", 0, 0, tiled=True)
-
-    step, up_out, fitness = step_product(
-        place, reward, left_all, right_own, right_other, keep, recv, members
-    )
+    recv = lax.ppermute(send, "ylo", SWAP)
+    up_out = order(keep, recv, axis=1)
+    step, fitness = step_product(place, reward, left_all, right_own, right_other, members)
     return (up_out, step, fitness.reshape(members))
 
 

time: 160 us -> 157 us (0.981)
  blocking collectives: 66.8 us -> 49.9 us
  starting transfers between devices: 33.3 us -> 40.9 us
  waiting for transfers between devices: 19.2 us -> 25.2 us
    all_to_all x1 -> x0, blocking collectives: 18 us -> none  [local(): lax.all_to_all(jnp.broadcast_to(near, (16, 1, 4 * members)), 'z', 0, 0, t...]
    all_to_all x0 -> x1, waiting for transfers between devices: none -> 7.74 us  [local(): lax.all_to_all(jnp.broadcast_to(near, (16, 1, 4 * members)), 'z', 0, 0, t...]
    all_to_all x0 -> x1, starting transfers between devices: none -> 6.54 us  [local(): lax.all_to_all(jnp.broadcast_to(near, (16, 1, 4 * members)), 'z', 0, 0, t...]
    all_gather x1, waiting for transfers between devices: 16.7 us -> 13.3 us  [local(): gathered = lax.all_gather(packed, ('z', 'core'), axis=0, tiled=False)]
    ppermute x1, waiting for transfers between devices: 0.01 us -> 1.64 us  [local(): projected_recv = lax.ppermute(projected_own, 'ylo', SWAP)]
  transfers between devices with their start and end apart: 7 -> 8, of which waited for: 2 -> 4; matrix products, arithmetic and copies ran while one was open for 7% -> 8% of each run, Pallas kernels for 0% -> 1%
where the time goes in v5:
time: 157 us; the launch traced here: 156 us
  blocking collectives  49.9 us (32%)
  starting transfers between devices  40.9 us (26%)
  waiting for transfers between devices  25.2 us (16%)
  between operations  14.3 us (9%)
  local copies, waits for them, and re-layouts  9.35 us (6%)
  Pallas kernels  8.67 us (6%)
  other arithmetic  7.37 us (5%)
    all_gather x1, blocking collectives, local(): right_other = lax.all_gather(far, ('z', 'core'), axis=0, tiled=False)  36.1 us
    all_to_all x1, starting transfers between devices, local(): lax.all_to_all(left_split, ('ylo', 'z', 'core'), 0, 0, tiled=True)  18.3 us
    all_to_all x1, blocking collectives, local(): near = lax.all_to_all(part, ('ylo', 'core', 'x', 'yhi'), 0, 0, tiled=True)  13.8 us
    all_gather x1, waiting for transfers between devices, local(): gathered = lax.all_gather(packed, ('z', 'core'), axis=0, tiled=False)  13.3 us
    all_to_all x1, waiting for transfers between devices, local(): lax.all_to_all(jnp.broadcast_to(near, (16, 1, 4 * members)), 'z', 0, 0, t...  7.74 us
    all_to_all x1, starting transfers between devices, local(): lax.all_to_all(jnp.broadcast_to(near, (16, 1, 4 * members)), 'z', 0, 0, t...  6.54 us
    pallas_call x1, Pallas kernels, project(): pl.pallas_call(project_kernel, in_specs=[SMEM, ANY, ANY, ANY, VMEM, VMEM]...  6.5 us
    ppermute x1, starting transfers between devices, local(): lax.ppermute(jnp.concatenate([other(weight), sent, mine], axis=0), 'ylo',...  4.03 us
  transfers between devices with their start and end apart: 8, of which 4 were waited for; matrix products, arithmetic and copies ran while one was open for 8% of the time, Pallas kernels for 1%

profile of v5, /device:TPU:1, one launch (start us, length us, event | category | flops | bytes accessed | tf_op | source)
XLA Modules:
  0.0 156.2 jit_solution(12837351034873555042)
XLA Ops:
  7.2 0.0 copy-start
  7.2 0.0 all-gather.3.cloned.1.call-start
  7.2 0.8 broadcast_select_fusion.5
  8.0 1.0 broadcast_select_fusion.3
  9.0 0.0 copy-start.2
  9.1 4.0 %collective-permute-start = (bf16[80,896]{1,0:T(8,128)(2,1)S(1)}, bf16[80,896]{1,0:T(8,128)(2,1)S(1)}, u32[]{:S(2)}, u32[]{:S(2)}) collective-permute-start(bf16[80,896]{1,0:T(8,128)(2,1)S(1)} %pad_maximum_fusion.3), channel_id=1, source_target_pairs={{0,256},{256,0},{1,257},{257,1},{2,258},{258,2},{3,259},{259,3},{4... | collective-permute-start | bytes 430088 | tf_op jit(solution)/shard_map/ppermute | solution.py:186
  13.1 2.5 %collective-permute-done = bf16[80,896]{1,0:T(8,128)(2,1)S(1)} collective-permute-done((bf16[80,896]{1,0:T(8,128)(2,1)S(1)}, bf16[80,896]{1,0:T(8,128)(2,1)S(1)}, u32[]{:S(2)}, u32[]{:S(2)}) %collective-permute-start) | collective-permute-done | bytes 143392 | tf_op jit(solution)/shard_map/ppermute | solution.py:186
  15.6 0.6 copy-done.1
  16.3 0.7 pad_maximum_fusion.2
  17.0 0.0 all-gather.3.cloned.1.call-update
  17.0 0.1 pad_add_fusion.place
  17.1 0.0 copy-done
  17.1 0.7 copy.27
  17.8 3.4 %collective-permute-start.1 = (bf16[128,4096]{0,1:T(8,128)(2,1)S(1)}, bf16[128,4096]{0,1:T(8,128)(2,1)S(1)}, u32[]{:S(2)}, u32[]{:S(2)}) collective-permute-start(bf16[128,4096]{0,1:T(8,128)(2,1)S(1)} %copy.27), channel_id=1, source_target_pairs={{0,256},{256,0},{1,257},{257,1},{2,258},{258,2},{3,259},{259,3},{4... | collective-permute-start | bytes 3145736 | tf_op jit(solution)/shard_map/ppermute | solution.py:200
  21.1 0.0 copy-done.2
  21.1 0.2 reshape.106
  21.3 0.1 copy.29
  21.4 0.8 reshape.115
  22.2 18.3 %all-to-all-start = ((bf16[64,2,256]{2,1,0:T(2,128)(2,1)}), bf16[64,2,256]{2,1,0:T(2,128)(2,1)}, u32[]{:S(2)}, u32[]{:S(2)}) async-start(bf16[64,2,256]{2,1,0:T(2,128)(2,1)} %reshape.115), calls=%async_computation | async-start | bytes 131072 | tf_op jit(solution)/shard_map/all_to_all | solution.py:219
  40.6 1.8 %broadcast_select_fusion.1 = (bf16[128,896]{1,0:T(8,128)(2,1)S(1)}, bf16[128,896]{1,0:T(8,128)(2,1)}) fusion(pred[]{:T(512)S(6)} %eq.3, bf16[128,1792]{1,0:T(8,128)(2,1)} %param.9), kind=kLoop, calls=%fused_computation.6 | loop fusion | flops 229376 | bytes 917505 | tf_op jit(solution)/shard_map/jit(_where)/select_n | solution.py:175
  42.3 3.4 %collective-permute-start.2 = (bf16[128,896]{1,0:T(8,128)(2,1)}, bf16[128,896]{1,0:T(8,128)(2,1)}, u32[]{:S(2)}, u32[]{:S(2)}) collective-permute-start(bf16[128,896]{1,0:T(8,128)(2,1)} %get-tuple-element.36), channel_id=1, source_target_pairs={{0,256},{256,0},{1,257},{257,1},{2,258},{258,2},{3,259},{259,3},{4... | collective-permute-start | bytes 688136 | tf_op jit(solution)/shard_map/ppermute | solution.py:201
  45.7 0.7 fusion.2
  46.5 0.5 fusion
  47.0 36.1 %all_gather.12.right_other = bf16[32,16,896]{2,1,0:T(8,128)(2,1)S(1)} all-gather(bf16[1,16,896]{2,1,0:T(8,128)(2,1)S(1)} %maximum_select_fusion.3), channel_id=1, replica_groups=mesh['ylo'=2,'z'=16,'core'=2,'x'=4,'yhi'=2] {'z','core'}, dimensions={0}, use_global_device_ids=true | all-gather | bytes 946176 | tf_op jit(solution)/shard_map/all_gather | solution.py:223
  83.1 0.1 mul.33
  83.2 3.0 %collective-permute-start.3 = (f32[128,1]{0,1:T(1,128)S(1)}, f32[128,1]{0,1:T(1,128)S(1)}, u32[]{:S(2)}, u32[]{:S(2)}) collective-permute-start(f32[128,1]{0,1:T(1,128)S(1)} %mul.33), channel_id=1, source_target_pairs={{0,256},{256,0},{1,257},{257,1},{2,258},{258,2},{3,259},{259,3},{4... | collective-permute-start | bytes 1544 | tf_op jit(solution)/shard_map/ppermute | solution.py:211
  86.2 1.6 %collective-permute-done.3 = f32[128,1]{0,1:T(1,128)S(1)} collective-permute-done((f32[128,1]{0,1:T(1,128)S(1)}, f32[128,1]{0,1:T(1,128)S(1)}, u32[]{:S(2)}, u32[]{:S(2)}) %collective-permute-start.3) | collective-permute-done | bytes 544 | tf_op jit(solution)/shard_map/ppermute | solution.py:211
  87.8 0.1 copy.32.projected
  88.0 0.0 collective-permute-done.2
  88.0 1.8 %pad_maximum_fusion.1.target_hbm = bf16[256,896]{1,0:T(8,128)(2,1)} fusion(bf16[128,896]{1,0:T(8,128)(2,1)} %collective-permute-done.2, bf16[128,896]{1,0:T(8,128)(2,1)S(1)} %get-tuple-element.35), kind=kLoop, calls=%fused_computation.1 | loop fusion | flops 917504 | bytes 917504 | tf_op jit(solution)/shard_map/concatenate | solution.py:213
  89.8 0.0 all-to-all-done
  89.8 1.0 reshape.116
  90.8 0.0 collective-permute-done.1
  90.8 0.2 pad_maximum_fusion
  91.0 0.1 copy.28
  91.2 2.9 %copy.31.hidden_hbm = bf16[256,4096]{1,0:T(8,128)(2,1)} copy(bf16[256,4096]{0,1:T(8,128)(2,1)S(1)} %bitcast.26) | data formatting | bytes 4194304 | tf_op jit(solution)/shard_map/optimization_barrier | solution.py:225
  94.1 13.3 %all-gather.3.cloned.1.call-done = bf16[4608,896]{1,0:T(8,128)(2,1)} async-done(((bf16[144,896]{1,0:T(8,128)(2,1)}), bf16[4608,896]{1,0:T(8,128)(2,1)}) %all-gather.3.cloned.1.call-update) | async-done | bytes 8257552 | tf_op jit(solution)/shard_map/all_gather | solution.py:193
  107.5 6.5 %shard_map.76 = (bf16[128,896]{1,0:T(8,128)(2,1)S(1)}, bf16[128,896]{1,0:T(8,128)(2,1)S(1)}, f32[32,1,16]{2,1,0:T(1,128)S(1)}) custom-call(s32[2]{0:T(128)S(1)} %pad_add_fusion.place, bf16[32,144,896]{2,1,0:T(8,128)(2,1)} %bitcast.23, bf16[256,4096]{1,0:T(8,128)(2,1)} %copy.31.hidden_hbm, bf16[256,896]{1,0:T(8,128)(2,1)} %pad_maximum_fusion.1.target_hbm, ...), custom_call_target="tpu_custom_call" | custom-call | flops 1879048192 | bytes 7340032 | tf_op jit(solution)/shard_map/pallas_call | solution.py:80
  114.0 13.8 %all_to_all.15 = f32[32,1,16]{2,1,0:T(1,128)S(1)} all-to-all(f32[32,1,16]{2,1,0:T(1,128)S(1)} %get-tuple-element.29), channel_id=1, replica_groups=mesh['ylo'=2,'z'=16,'core'=2,'x'=4,'yhi'=2] {'ylo','core','x','yhi'}, dimensions={0} | all-to-all | bytes 4096 | tf_op jit(solution)/shard_map/all_to_all | solution.py:233
  127.8 0.1 broadcast_in_dim.7
  127.9 0.6 broadcast_in_dim.8
  128.5 6.5 %all-to-all-start.2 = ((f32[16,1,32]{2,1,0:T(1,128)}), f32[16,1,32]{2,1,0:T(1,128)S(1)}, u32[]{:S(2)}, u32[]{:S(2)}) async-start(f32[16,1,32]{2,1,0:T(1,128)} %broadcast_in_dim.8), calls=%async_computation.2 | async-start | bytes 16384 | tf_op jit(solution)/shard_map/all_to_all | solution.py:235
  135.1 1.3 slice.49.right_own
  136.3 2.2 %collective-permute-start.4 = (bf16[128,896]{1,0:T(8,128)(2,1)S(1)}, bf16[128,896]{1,0:T(8,128)(2,1)S(1)}, u32[]{:S(2)}, u32[]{:S(2)}) collective-permute-start(bf16[128,896]{1,0:T(8,128)(2,1)S(1)} %get-tuple-element.27), channel_id=1, source_target_pairs={{0,256},{256,0},{1,257},{257,1},{2,258},{258,2},{3,259},{259,3},{4... | collective-permute-start | bytes 688136 | tf_op jit(solution)/shard_map/ppermute | solution.py:236
  138.5 7.7 %all-to-all-done.2.reward = f32[16,1,32]{2,1,0:T(1,128)S(1)} async-done(((f32[16,1,32]{2,1,0:T(1,128)}), f32[16,1,32]{2,1,0:T(1,128)S(1)}, u32[]{:S(2)}, u32[]{:S(2)}) %all-to-all-start.2) | async-done | bytes 2080 | tf_op jit(solution)/shard_map/all_to_all | solution.py:235
  146.3 2.2 %shard_map.77 = (f32[64,1792]{1,0:T(8,128)}, f32[1,8]{1,0:T(1,128)}) custom-call(s32[2]{0:T(128)S(1)} %pad_add_fusion.place, f32[16,1,32]{2,1,0:T(1,128)S(1)} %all-to-all-done.2.reward, bf16[512,64]{1,0:T(8,128)(2,1)S(1)} %bitcast.22, bf16[32,16,896]{2,1,0:T(8,128)(2,1)S(1)} %slice.49.right_own, bf16[32,16,896]{2,1,0:T(8,128)(2,1)S(1)} %all_gather.12.right_other), custom_call_target="tpu_custom_call" | custom-call | flops 3758096384 | bytes 2293760 | tf_op jit(solution)/shard_map/pallas_call | solution.py:146
  148.5 0.0 collective-permute-done.4
  148.5 0.9 maximum_select_fusion
  (12 shorter events, 0.2 us)
Async XLA Ops:
  7.2 9.9 %copy-start = (bf16[128,4096]{1,0:T(8,128)(2,1)S(1)}, bf16[128,4096]{1,0:T(8,128)(2,1)}, u32[]{:S(2)}) copy-start(bf16[128,4096]{1,0:T(8,128)(2,1)} %param.5) | copy-start | bytes 3145732
  7.2 100.3 %all-gather.3.cloned.1.call-start = ((), (), s32[]{:S(2)}) async-start(), calls=%async_computation.3 | async-start | bytes 8515584 | tf_op jit(solution)/shard_map/all_gather | solution.py:193
  9.0 12.1 %copy-start.2 = (bf16[8,4096]{1,0:T(8,128)(2,1)S(1)}, bf16[8,4096]{1,0:T(8,128)(2,1)}, u32[]{:S(2)}) copy-start(bf16[8,4096]{1,0:T(8,128)(2,1)} %param.7) | copy-start | bytes 196612
  9.1 6.5 %collective-permute-start = (bf16[80,896]{1,0:T(8,128)(2,1)S(1)}, bf16[80,896]{1,0:T(8,128)(2,1)S(1)}, u32[]{:S(2)}, u32[]{:S(2)}) collective-permute-start(bf16[80,896]{1,0:T(8,128)(2,1)S(1)} %pad_maximum_fusion.3), channel_id=1, source_target_pairs={{0,256},{256,0},{1,257},{257,1},{2,258},{258,2},{3,259},{259,3},{4... | collective-permute-start | bytes 430088 | tf_op jit(solution)/shard_map/ppermute | solution.py:186
  15.6 0.7 copy-start.1
  17.8 73.0 %collective-permute-start.1 = (bf16[128,4096]{0,1:T(8,128)(2,1)S(1)}, bf16[128,4096]{0,1:T(8,128)(2,1)S(1)}, u32[]{:S(2)}, u32[]{:S(2)}) collective-permute-start(bf16[128,4096]{0,1:T(8,128)(2,1)S(1)} %copy.27), channel_id=1, source_target_pairs={{0,256},{256,0},{1,257},{257,1},{2,258},{258,2},{3,259},{259,3},{4... | collective-permute-start | bytes 3145736 | tf_op jit(solution)/shard_map/ppermute | solution.py:200
  22.2 67.6 %all-to-all-start = ((bf16[64,2,256]{2,1,0:T(2,128)(2,1)}), bf16[64,2,256]{2,1,0:T(2,128)(2,1)}, u32[]{:S(2)}, u32[]{:S(2)}) async-start(bf16[64,2,256]{2,1,0:T(2,128)(2,1)} %reshape.115), calls=%async_computation | async-start | bytes 131072 | tf_op jit(solution)/shard_map/all_to_all | solution.py:219
  42.3 45.6 %collective-permute-start.2 = (bf16[128,896]{1,0:T(8,128)(2,1)}, bf16[128,896]{1,0:T(8,128)(2,1)}, u32[]{:S(2)}, u32[]{:S(2)}) collective-permute-start(bf16[128,896]{1,0:T(8,128)(2,1)} %get-tuple-element.36), channel_id=1, source_target_pairs={{0,256},{256,0},{1,257},{257,1},{2,258},{258,2},{3,259},{259,3},{4... | collective-permute-start | bytes 688136 | tf_op jit(solution)/shard_map/ppermute | solution.py:201
  83.2 4.7 %collective-permute-start.3 = (f32[128,1]{0,1:T(1,128)S(1)}, f32[128,1]{0,1:T(1,128)S(1)}, u32[]{:S(2)}, u32[]{:S(2)}) collective-permute-start(f32[128,1]{0,1:T(1,128)S(1)} %mul.33), channel_id=1, source_target_pairs={{0,256},{256,0},{1,257},{257,1},{2,258},{258,2},{3,259},{259,3},{4... | collective-permute-start | bytes 1544 | tf_op jit(solution)/shard_map/ppermute | solution.py:211
  128.5 17.8 %all-to-all-start.2 = ((f32[16,1,32]{2,1,0:T(1,128)}), f32[16,1,32]{2,1,0:T(1,128)S(1)}, u32[]{:S(2)}, u32[]{:S(2)}) async-start(f32[16,1,32]{2,1,0:T(1,128)} %broadcast_in_dim.8), calls=%async_computation.2 | async-start | bytes 16384 | tf_op jit(solution)/shard_map/all_to_all | solution.py:235
  136.3 12.1 %collective-permute-start.4 = (bf16[128,896]{1,0:T(8,128)(2,1)S(1)}, bf16[128,896]{1,0:T(8,128)(2,1)S(1)}, u32[]{:S(2)}, u32[]{:S(2)}) collective-permute-start(bf16[128,896]{1,0:T(8,128)(2,1)S(1)} %get-tuple-element.27), channel_id=1, source_target_pairs={{0,256},{256,0},{1,257},{257,1},{2,258},{258,2},{3,259},{259,3},{4... | collective-permute-start | bytes 688136 | tf_op jit(solution)/shard_map/ppermute | solution.py:236
Sparse Core Ops, SparseCore 0:
  17.1 90.2 all-gather.2

commit v6 on v5

--- a/solution.py
+++ b/solution.py
@@ -102,12 +102,10 @@
     )(place, gathered, hidden, target, right, projected)
 
 
-def step_kernel(place, reward, left, right_own, right_other, out, fitness):
+def step_kernel(place, reward, left, right_left, right_right, out, fitness):
     members, depth = left.shape
     blocks, _, lanes = reward.shape
-    half = right_own.shape[2]
-    own_at = pl.multiple_of(place[0] * half, 128)
-    other_at = pl.multiple_of((1 - place[0]) * half, 128)
+    half = right_left.shape[2]
     value = reward[...].reshape(blocks, lanes)
     total = jnp.sum(jnp.sum(value, axis=0, keepdims=True), axis=1, keepdims=True)
     centered = value - total * (1.0 / members)
@@ -134,15 +132,15 @@
             (((0,), (0,)), ((), ())),
             preferred_element_type=jnp.float32,
         )
-        out[:, pl.ds(at, half)] = (product[:depth] + product[depth:]) * (1.0 / math.sqrt(members))
-
-    multiply(right_other[...], other_at)
-    multiply(right_own[...], own_at)
-
-
-def step_product(place, reward, left, right_own, right_other, own):
+        out[:, at : at + half] = (product[:depth] + product[depth:]) * (1.0 / math.sqrt(members))
+
+    multiply(right_left[...], 0)
+    multiply(right_right[...], half)
+
+
+def step_product(place, reward, left, right_left, right_right, own):
     members, depth = left.shape
-    half = right_other.shape[2]
+    half = right_right.shape[2]
     return pl.pallas_call(
         step_kernel,
         in_specs=[SMEM, VMEM, VMEM, VMEM, VMEM],
@@ -157,7 +155,7 @@
             bytes_accessed=members * half * 4 + depth * half * 8,
             transcendentals=0,
         ),
-    )(place, reward, left, right_own, right_other)
+    )(place, reward, left, right_left, right_right)
 
 
 def local(hidden, weight, left_factors, right_factors, target):
@@ -182,21 +180,25 @@
             low, jnp.concatenate([a, b], axis=axis), jnp.concatenate([b, a], axis=axis)
         )
 
-    mine, sent = own(right_factors), other(right_factors)
+    near_left, near_right = right_factors[:, :half], right_factors[:, half:]
     slab_recv = lax.ppermute(
-        jnp.concatenate([other(weight), sent, mine], axis=0), "ylo", SWAP
-    )
-    theirs = slab_recv[depth : depth + members]
+        jnp.concatenate([other(weight), near_left, near_right], axis=0), "ylo", SWAP
+    )
     packed = jnp.concatenate(
-        [order(own(weight), slab_recv[:depth]), order(mine, theirs)], axis=0
+        [
+            order(own(weight), slab_recv[:depth]),
+            order(near_left, slab_recv[depth : depth + members]),
+            order(near_right, slab_recv[depth + members :]),
+        ],
+        axis=0,
     )
     gathered = lax.all_gather(packed, ("z", "core"), axis=0, tiled=False)
 
-    _, hidden_b, left_b, target_b, sent, slab_b, mine_b = lax.optimization_barrier(
-        (packed, hidden, left_factors, target, sent, slab_recv, mine)
-    )
-    theirs_far = slab_b[depth + members :]
-    right_local = jnp.concatenate([mine_b, slab_b[depth : depth + members]], axis=0)
+    _, hidden_b, left_b, target_b, right_b, slab_b = lax.optimization_barrier(
+        (packed, hidden, left_factors, target, right_factors, slab_recv)
+    )
+    theirs = jnp.where(low, slab_b[depth : depth + members], slab_b[depth + members :])
+    right_local = jnp.concatenate([own(right_b), theirs], axis=0)
     rows_recv = lax.ppermute(hidden_b, "ylo", SWAP)
     target_recv = lax.ppermute(other(target_b), "ylo", SWAP)
     projected_own = (
@@ -219,23 +221,21 @@
     left_all = lax.all_to_all(left_split, ("ylo", "z", "core"), 0, 0, tiled=True)
     left_all = left_all.reshape(2, features // (2 * depth), members, depth)
     left_all = left_all.transpose(1, 0, 2, 3).reshape(-1, depth)
-    far = order(sent, theirs_far)
-    right_other = lax.all_gather(far, ("z", "core"), axis=0, tiled=False)
-
-    hidden_all, left_all, right_other = lax.optimization_barrier((hidden_all, left_all, right_other))
+    hidden_all, left_all = lax.optimization_barrier((hidden_all, left_all))
     place = jnp.stack([ylo, z * 4 * members + core * 2 * members + ylo * members]).astype(jnp.int32)
     keep, send, part = project(
         place, gathered, hidden_all, target_all, right_local, projected, 32
     )
 
     gathered, part = lax.optimization_barrier((gathered, part))
-    right_own = gathered[:, 2 * depth :]
+    right_left = gathered[:, 2 * depth : 2 * depth + 2 * members]
+    right_right = gathered[:, 2 * depth + 2 * members :]
     near = lax.all_to_all(part, ("ylo", "core", "x", "yhi"), 0, 0, tiled=True)
     near = near.reshape(2, 2, 8, 2 * members).sum(axis=(0, 2)).reshape(1, 1, 4 * members)
     reward = lax.all_to_all(jnp.broadcast_to(near, (16, 1, 4 * members)), "z", 0, 0, tiled=True)
     recv = lax.ppermute(send, "ylo", SWAP)
     up_out = order(keep, recv, axis=1)
-    step, fitness = step_product(place, reward, left_all, right_own, right_other, members)
+    step, fitness = step_product(place, reward, left_all, right_left, right_right, members)
     return (up_out, step, fitness.reshape(members))
 
 

time: 157 us -> 156 us (level)
  waiting for transfers between devices: 25.2 us -> 64.9 us
  blocking collectives: 49.9 us -> 13.7 us
  other arithmetic: 7.37 us -> 5.1 us
    all_gather x1 -> x0, blocking collectives: 36.1 us -> none  [local(): right_other = lax.all_gather(far, ('z', 'core'), axis=0, tiled=False)]
    all_gather x1, waiting for transfers between devices: 13.3 us -> 47.1 us  [local(): gathered = lax.all_gather(packed, ('z', 'core'), axis=0, tiled=False)]
    ppermute x1, waiting for transfers between devices: 0.01 us -> 6.67 us  [local(): target_recv = lax.ppermute(other(target_b), 'ylo', SWAP)]
    select_n x2 -> x3, other arithmetic: 2.77 us -> 1.04 us  [own(): return jnp.where(low, a[:, :half], a[:, half:])]
    ppermute x1, waiting for transfers between devices: 1.64 us -> 0.01 us  [local(): projected_recv = lax.ppermute(projected_own, 'ylo', SWAP)]
  transfers between devices with their start and end apart: 8 -> 8, of which waited for: 4 -> 5; matrix products, arithmetic and copies ran while one was open for 8% -> 6% of each run, Pallas kernels for 1% -> 1%
where the time goes in v6:
time: 156 us; the launch traced here: 155 us
  waiting for transfers between devices  64.9 us (42%)
  starting transfers between devices  40 us (26%)
  between operations  14.3 us (9%)
  blocking collectives  13.7 us (9%)
  Pallas kernels  8.67 us (6%)
  local copies, waits for them, and re-layouts  8.3 us (5%)
  other arithmetic  5.1 us (3%)
    all_gather x1, waiting for transfers between devices, local(): gathered = lax.all_gather(packed, ('z', 'core'), axis=0, tiled=False)  47.1 us
    all_to_all x1, starting transfers between devices, local(): lax.all_to_all(left_split, ('ylo', 'z', 'core'), 0, 0, tiled=True)  18.1 us
    all_to_all x1, blocking collectives, local(): near = lax.all_to_all(part, ('ylo', 'core', 'x', 'yhi'), 0, 0, tiled=True)  13.7 us
    all_to_all x1, waiting for transfers between devices, local(): lax.all_to_all(jnp.broadcast_to(near, (16, 1, 4 * members)), 'z', 0, 0, t...  7.39 us
    all_to_all x1, starting transfers between devices, local(): lax.all_to_all(jnp.broadcast_to(near, (16, 1, 4 * members)), 'z', 0, 0, t...  6.91 us
    ppermute x1, waiting for transfers between devices, local(): target_recv = lax.ppermute(other(target_b), 'ylo', SWAP)  6.67 us
    pallas_call x1, Pallas kernels, project(): pl.pallas_call(project_kernel, in_specs=[SMEM, ANY, ANY, ANY, VMEM, VMEM]...  6.5 us
    ppermute x1, starting transfers between devices, local(): lax.ppermute(jnp.concatenate([other(weight), near_left, near_right], axis...  4.03 us
  transfers between devices with their start and end apart: 8, of which 5 were waited for; matrix products, arithmetic and copies ran while one was open for 6% of the time, Pallas kernels for 1%

profile of v6, /device:TPU:1, one launch (start us, length us, event | category | flops | bytes accessed | tf_op | source)
XLA Modules:
  0.0 155.5 jit_solution(5736942096968807361)
XLA Ops:
  7.2 0.0 copy-start
  7.2 0.0 all-gather.3.cloned.1.call-start
  7.2 0.8 fusion.4
  8.0 1.0 broadcast_select_fusion.3
  9.0 0.0 copy-start.3
  9.1 4.0 %collective-permute-start = (bf16[80,896]{1,0:T(8,128)(2,1)S(1)}, bf16[80,896]{1,0:T(8,128)(2,1)S(1)}, u32[]{:S(2)}, u32[]{:S(2)}) collective-permute-start(bf16[80,896]{1,0:T(8,128)(2,1)S(1)} %pad_maximum_fusion.3), channel_id=1, source_target_pairs={{0,256},{256,0},{1,257},{257,1},{2,258},{258,2},{3,259},{259,3},{4... | collective-permute-start | bytes 430088 | tf_op jit(solution)/shard_map/ppermute | solution.py:184
  13.1 2.5 %collective-permute-done = bf16[80,896]{1,0:T(8,128)(2,1)S(1)} collective-permute-done((bf16[80,896]{1,0:T(8,128)(2,1)S(1)}, bf16[80,896]{1,0:T(8,128)(2,1)S(1)}, u32[]{:S(2)}, u32[]{:S(2)}) %collective-permute-start) | collective-permute-done | bytes 143392 | tf_op jit(solution)/shard_map/ppermute | solution.py:184
  15.7 0.7 pad_maximum_fusion.2
  16.4 0.0 all-gather.3.cloned.1.call-update
  16.4 0.1 pad_add_fusion.place
  16.5 0.0 copy-done
  16.5 0.7 copy.27
  17.2 0.0 copy-start.2
  17.2 3.4 %collective-permute-start.1 = (bf16[128,4096]{0,1:T(8,128)(2,1)S(1)}, bf16[128,4096]{0,1:T(8,128)(2,1)}, u32[]{:S(2)}, u32[]{:S(2)}) collective-permute-start(bf16[128,4096]{0,1:T(8,128)(2,1)S(1)} %copy.27), channel_id=1, source_target_pairs={{0,256},{256,0},{1,257},{257,1},{2,258},{258,2},{3,259},{259,3},{4... | collective-permute-start | bytes 3145736 | tf_op jit(solution)/shard_map/ppermute | solution.py:202
  20.6 0.0 copy-done.3
  20.6 0.2 reshape.51
  20.7 0.1 copy.29
  20.8 0.8 reshape.60
  21.6 18.1 %all-to-all-start = ((bf16[64,2,256]{2,1,0:T(2,128)(2,1)}), bf16[64,2,256]{2,1,0:T(2,128)(2,1)S(1)}, u32[]{:S(2)}, u32[]{:S(2)}) async-start(bf16[64,2,256]{2,1,0:T(2,128)(2,1)} %reshape.60), calls=%async_computation | async-start | bytes 131072 | tf_op jit(solution)/shard_map/all_to_all | solution.py:221
  39.8 0.5 fusion
  40.3 0.1 mul.33
  40.4 3.4 %collective-permute-start.3 = (f32[128,1]{0,1:T(1,128)S(1)}, f32[128,1]{0,1:T(1,128)S(1)}, u32[]{:S(2)}, u32[]{:S(2)}) collective-permute-start(f32[128,1]{0,1:T(1,128)S(1)} %mul.33), channel_id=1, source_target_pairs={{0,256},{256,0},{1,257},{257,1},{2,258},{258,2},{3,259},{259,3},{4... | collective-permute-start | bytes 1544 | tf_op jit(solution)/shard_map/ppermute | solution.py:213
  43.8 0.0 copy-done.1
  43.8 0.1 broadcast_select_fusion.1
  43.8 1.9 %collective-permute-start.2 = (bf16[128,896]{1,0:T(8,128)(2,1)S(1)}, bf16[128,896]{1,0:T(8,128)(2,1)S(1)}, u32[]{:S(2)}, u32[]{:S(2)}) collective-permute-start(bf16[128,896]{1,0:T(8,128)(2,1)S(1)} %get-tuple-element.34), channel_id=1, source_target_pairs={{0,256},{256,0},{1,257},{257,1},{2,258},{258,2},{3,259},{259,3},{4... | collective-permute-start | bytes 688136 | tf_op jit(solution)/shard_map/ppermute | solution.py:203
  45.8 0.0 copy-done.2
  45.8 0.0 collective-permute-done.3
  45.8 0.1 copy.32.projected
  46.0 6.7 %collective-permute-done.2 = bf16[128,896]{1,0:T(8,128)(2,1)S(1)} collective-permute-done((bf16[128,896]{1,0:T(8,128)(2,1)S(1)}, bf16[128,896]{1,0:T(8,128)(2,1)S(1)}, u32[]{:S(2)}, u32[]{:S(2)}) %collective-permute-start.2) | collective-permute-done | bytes 229408 | tf_op jit(solution)/shard_map/ppermute | solution.py:203
  52.7 0.8 pad_maximum_fusion.1.target_hbm
  53.5 1.2 all-to-all-done
  54.7 0.1 reshape.61
  54.9 0.0 collective-permute-done.1
  54.9 1.5 pad_maximum_fusion
  56.3 0.1 copy.28
  56.5 2.9 %copy.31.hidden_hbm = bf16[256,4096]{1,0:T(8,128)(2,1)} copy(bf16[256,4096]{0,1:T(8,128)(2,1)S(1)} %bitcast.23) | data formatting | bytes 4194304 | tf_op jit(solution)/shard_map/optimization_barrier | solution.py:224
  59.4 47.1 %all-gather.3.cloned.1.call-done = bf16[5120,896]{1,0:T(8,128)(2,1)} async-done(((bf16[160,896]{1,0:T(8,128)(2,1)}), bf16[5120,896]{1,0:T(8,128)(2,1)}) %all-gather.3.cloned.1.call-update) | async-done | bytes 9175056 | tf_op jit(solution)/shard_map/all_gather | solution.py:195
  106.5 6.5 %shard_map.76 = (bf16[128,896]{1,0:T(8,128)(2,1)S(1)}, bf16[128,896]{1,0:T(8,128)(2,1)S(1)}, f32[32,1,16]{2,1,0:T(1,128)S(1)}) custom-call(s32[2]{0:T(128)S(1)} %pad_add_fusion.place, bf16[32,160,896]{2,1,0:T(8,128)(2,1)} %bitcast.20, bf16[256,4096]{1,0:T(8,128)(2,1)} %copy.31.hidden_hbm, bf16[256,896]{1,0:T(8,128)(2,1)} %pad_maximum_fusion.1.target_hbm, ...), custom_call_target="tpu_custom_call" | custom-call | flops 1879048192 | bytes 7340032 | tf_op jit(solution)/shard_map/pallas_call | solution.py:80
  113.0 13.7 %all_to_all.15 = f32[32,1,16]{2,1,0:T(1,128)S(1)} all-to-all(f32[32,1,16]{2,1,0:T(1,128)S(1)} %get-tuple-element.26), channel_id=1, replica_groups=mesh['ylo'=2,'z'=16,'core'=2,'x'=4,'yhi'=2] {'ylo','core','x','yhi'}, dimensions={0} | all-to-all | bytes 4096 | tf_op jit(solution)/shard_map/all_to_all | solution.py:233
  126.7 0.1 broadcast_in_dim.7
  126.8 0.6 broadcast_in_dim.8
  127.4 6.9 %all-to-all-start.2 = ((f32[16,1,32]{2,1,0:T(1,128)}), f32[16,1,32]{2,1,0:T(1,128)S(1)}, u32[]{:S(2)}, u32[]{:S(2)}) async-start(f32[16,1,32]{2,1,0:T(1,128)} %broadcast_in_dim.8), calls=%async_computation.2 | async-start | bytes 16384 | tf_op jit(solution)/shard_map/all_to_all | solution.py:235
  134.3 1.6 %fusion.2 = (bf16[32,16,896]{2,1,0:T(8,128)(2,1)S(1)}, bf16[32,16,896]{2,1,0:T(8,128)(2,1)S(1)}) fusion(bf16[32,160,896]{2,1,0:T(8,128)(2,1)} %bitcast.21), kind=kLoop, calls=%fused_computation.20 | loop fusion | bytes 3670016 | tf_op jit(solution)/shard_map/slice | solution.py:232
  135.9 2.2 %collective-permute-start.4 = (bf16[128,896]{1,0:T(8,128)(2,1)S(1)}, bf16[128,896]{1,0:T(8,128)(2,1)S(1)}, u32[]{:S(2)}, u32[]{:S(2)}) collective-permute-start(bf16[128,896]{1,0:T(8,128)(2,1)S(1)} %get-tuple-element.24), channel_id=1, source_target_pairs={{0,256},{256,0},{1,257},{257,1},{2,258},{258,2},{3,259},{259,3},{4... | collective-permute-start | bytes 688136 | tf_op jit(solution)/shard_map/ppermute | solution.py:236
  138.2 7.4 %all-to-all-done.2.reward = f32[16,1,32]{2,1,0:T(1,128)S(1)} async-done(((f32[16,1,32]{2,1,0:T(1,128)}), f32[16,1,32]{2,1,0:T(1,128)S(1)}, u32[]{:S(2)}, u32[]{:S(2)}) %all-to-all-start.2) | async-done | bytes 2080 | tf_op jit(solution)/shard_map/all_to_all | solution.py:235
  145.6 2.2 %shard_map.77 = (f32[64,1792]{1,0:T(8,128)}, f32[1,8]{1,0:T(1,128)}) custom-call(s32[2]{0:T(128)S(1)} %pad_add_fusion.place, f32[16,1,32]{2,1,0:T(1,128)S(1)} %all-to-all-done.2.reward, bf16[512,64]{1,0:T(8,128)(2,1)S(1)} %bitcast.19, bf16[32,16,896]{2,1,0:T(8,128)(2,1)S(1)} %get-tuple-element.32.right_left, ...), custom_call_target="tpu_custom_call" | custom-call | flops 3758096384 | bytes 2293760 | tf_op jit(solution)/shard_map/pallas_call | solution.py:144
  147.7 0.0 collective-permute-done.4
  147.7 0.9 maximum_select_fusion
  (13 shorter events, 0.2 us)
Async XLA Ops:
  7.2 9.3 %copy-start = (bf16[128,4096]{1,0:T(8,128)(2,1)S(1)}, bf16[128,4096]{1,0:T(8,128)(2,1)}, u32[]{:S(2)}) copy-start(bf16[128,4096]{1,0:T(8,128)(2,1)} %param.5) | copy-start | bytes 3145732
  7.2 99.3 %all-gather.3.cloned.1.call-start = ((), (), s32[]{:S(2)}) async-start(), calls=%async_computation.3 | async-start | bytes 9461760 | tf_op jit(solution)/shard_map/all_gather | solution.py:195
  9.0 11.5 %copy-start.3 = (bf16[8,4096]{1,0:T(8,128)(2,1)S(1)}, bf16[8,4096]{1,0:T(8,128)(2,1)}, u32[]{:S(2)}) copy-start(bf16[8,4096]{1,0:T(8,128)(2,1)} %param.7) | copy-start | bytes 196612
  9.1 6.5 %collective-permute-start = (bf16[80,896]{1,0:T(8,128)(2,1)S(1)}, bf16[80,896]{1,0:T(8,128)(2,1)S(1)}, u32[]{:S(2)}, u32[]{:S(2)}) collective-permute-start(bf16[80,896]{1,0:T(8,128)(2,1)S(1)} %pad_maximum_fusion.3), channel_id=1, source_target_pairs={{0,256},{256,0},{1,257},{257,1},{2,258},{258,2},{3,259},{259,3},{4... | collective-permute-start | bytes 430088 | tf_op jit(solution)/shard_map/ppermute | solution.py:184
  16.5 27.3 %copy-start.1 = (bf16[128,1792]{1,0:T(8,128)(2,1)S(1)}, bf16[128,1792]{1,0:T(8,128)(2,1)}, u32[]{:S(2)}) copy-start(bf16[128,1792]{1,0:T(8,128)(2,1)} %param.9) | copy-start | bytes 1376260
  17.2 28.6 %copy-start.2 = (bf16[8,1792]{1,0:T(8,128)(2,1)S(1)}, bf16[8,1792]{1,0:T(8,128)(2,1)}, u32[]{:S(2)}) copy-start(bf16[8,1792]{1,0:T(8,128)(2,1)} %param.8) | copy-start | bytes 86020
  17.2 37.7 %collective-permute-start.1 = (bf16[128,4096]{0,1:T(8,128)(2,1)S(1)}, bf16[128,4096]{0,1:T(8,128)(2,1)}, u32[]{:S(2)}, u32[]{:S(2)}) collective-permute-start(bf16[128,4096]{0,1:T(8,128)(2,1)S(1)} %copy.27), channel_id=1, source_target_pairs={{0,256},{256,0},{1,257},{257,1},{2,258},{258,2},{3,259},{259,3},{4... | collective-permute-start | bytes 3145736 | tf_op jit(solution)/shard_map/ppermute | solution.py:202
  21.6 33.1 %all-to-all-start = ((bf16[64,2,256]{2,1,0:T(2,128)(2,1)}), bf16[64,2,256]{2,1,0:T(2,128)(2,1)S(1)}, u32[]{:S(2)}, u32[]{:S(2)}) async-start(bf16[64,2,256]{2,1,0:T(2,128)(2,1)} %reshape.60), calls=%async_computation | async-start | bytes 131072 | tf_op jit(solution)/shard_map/all_to_all | solution.py:221
  40.4 5.5 %collective-permute-start.3 = (f32[128,1]{0,1:T(1,128)S(1)}, f32[128,1]{0,1:T(1,128)S(1)}, u32[]{:S(2)}, u32[]{:S(2)}) collective-permute-start(f32[128,1]{0,1:T(1,128)S(1)} %mul.33), channel_id=1, source_target_pairs={{0,256},{256,0},{1,257},{257,1},{2,258},{258,2},{3,259},{259,3},{4... | collective-permute-start | bytes 1544 | tf_op jit(solution)/shard_map/ppermute | solution.py:213
  43.8 8.8 %collective-permute-start.2 = (bf16[128,896]{1,0:T(8,128)(2,1)S(1)}, bf16[128,896]{1,0:T(8,128)(2,1)S(1)}, u32[]{:S(2)}, u32[]{:S(2)}) collective-permute-start(bf16[128,896]{1,0:T(8,128)(2,1)S(1)} %get-tuple-element.34), channel_id=1, source_target_pairs={{0,256},{256,0},{1,257},{257,1},{2,258},{258,2},{3,259},{259,3},{4... | collective-permute-start | bytes 688136 | tf_op jit(solution)/shard_map/ppermute | solution.py:203
  127.4 18.1 %all-to-all-start.2 = ((f32[16,1,32]{2,1,0:T(1,128)}), f32[16,1,32]{2,1,0:T(1,128)S(1)}, u32[]{:S(2)}, u32[]{:S(2)}) async-start(f32[16,1,32]{2,1,0:T(1,128)} %broadcast_in_dim.8), calls=%async_computation.2 | async-start | bytes 16384 | tf_op jit(solution)/shard_map/all_to_all | solution.py:235
  135.9 11.8 %collective-permute-start.4 = (bf16[128,896]{1,0:T(8,128)(2,1)S(1)}, bf16[128,896]{1,0:T(8,128)(2,1)S(1)}, u32[]{:S(2)}, u32[]{:S(2)}) collective-permute-start(bf16[128,896]{1,0:T(8,128)(2,1)S(1)} %get-tuple-element.24), channel_id=1, source_target_pairs={{0,256},{256,0},{1,257},{257,1},{2,258},{258,2},{3,259},{259,3},{4... | collective-permute-start | bytes 688136 | tf_op jit(solution)/shard_map/ppermute | solution.py:236
Sparse Core Ops, SparseCore 0:
  16.5 89.9 all-gather.2

commit v7 on v6

--- a/solution.py
+++ b/solution.py
@@ -24,18 +24,23 @@
     load_hidden = pltpu.make_async_copy(hidden_hbm, hidden, sems.at[0])
     load_hidden.start()
     copies = []
+    deep = width // 2
     for i in range(chunks):
-        copy = pltpu.make_async_copy(
-            gathered.at[pl.ds(i * slabs, slabs), pl.ds(0, width), :], held.at[i], sems.at[2 + i]
-        )
-        copy.start()
-        copies.append(copy)
+        for j in range(2):
+            copy = pltpu.make_async_copy(
+                gathered.at[pl.ds(i * slabs, slabs), pl.ds(0, deep), pl.ds(j * cols, cols)],
+                held.at[i, :, pl.ds(j * deep, deep), :],
+                sems.at[2 + 2 * i + j],
+            )
+            copy.start()
+            copies.append(copy)
     load_target = pltpu.make_async_copy(target_hbm, target, sems.at[1])
     load_target.start()
     span = slabs * width
     load_hidden.wait()
     for i in range(chunks):
-        copies[i].wait()
+        copies[2 * i].wait()
+        copies[2 * i + 1].wait()
         part = jnp.dot(
             hidden[:, i * span : (i + 1) * span],
             held[i].reshape(span, cols),
@@ -72,7 +77,8 @@
 
 
 def project(place, gathered, hidden, target, right, projected, peers):
-    blocks, _, cols = gathered.shape
+    blocks = gathered.shape[0]
+    cols = target.shape[1]
     rows, features = hidden.shape
     members = right.shape[0]
     width = features // blocks
@@ -91,7 +97,7 @@
             pltpu.VMEM((blocks // slabs, slabs, width, cols), jnp.bfloat16),
             pltpu.VMEM(hidden.shape, jnp.bfloat16),
             pltpu.VMEM(target.shape, jnp.bfloat16),
-            pltpu.SemaphoreType.DMA((blocks // slabs + 2,)),
+            pltpu.SemaphoreType.DMA((2 * (blocks // slabs) + 2,)),
         ],
         compiler_params=pltpu.CompilerParams(vmem_limit_bytes=53 * 1024 * 1024),
         cost_estimate=pl.CostEstimate(
@@ -102,10 +108,10 @@
     )(place, gathered, hidden, target, right, projected)
 
 
-def step_kernel(place, reward, left, right_left, right_right, out, fitness):
+def step_kernel(place, reward, left, right, out, fitness):
     members, depth = left.shape
     blocks, _, lanes = reward.shape
-    half = right_left.shape[2]
+    cols = right.shape[2]
     value = reward[...].reshape(blocks, lanes)
     total = jnp.sum(jnp.sum(value, axis=0, keepdims=True), axis=1, keepdims=True)
     centered = value - total * (1.0 / members)
@@ -125,37 +131,37 @@
     low = (weighted - high.astype(jnp.float32)).astype(jnp.bfloat16)
     both = jnp.concatenate([high, low], axis=1)
 
-    def multiply(right, at):
+    factors = right[...].reshape(members, cols)
+    for at in range(0, cols, cols // 2):
         product = lax.dot_general(
             both,
-            right.reshape(members, half),
+            factors[:, at : at + cols // 2],
             (((0,), (0,)), ((), ())),
             preferred_element_type=jnp.float32,
         )
-        out[:, at : at + half] = (product[:depth] + product[depth:]) * (1.0 / math.sqrt(members))
-
-    multiply(right_left[...], 0)
-    multiply(right_right[...], half)
-
-
-def step_product(place, reward, left, right_left, right_right, own):
+        out[:, at : at + cols // 2] = (product[:depth] + product[depth:]) * (
+            1.0 / math.sqrt(members)
+        )
+
+
+def step_product(place, reward, left, right, own):
     members, depth = left.shape
-    half = right_right.shape[2]
+    cols = right.shape[2]
     return pl.pallas_call(
         step_kernel,
-        in_specs=[SMEM, VMEM, VMEM, VMEM, VMEM],
+        in_specs=[SMEM, VMEM, VMEM, VMEM],
         out_specs=[VMEM, VMEM],
         out_shape=[
-            jax.ShapeDtypeStruct((depth, 2 * half), jnp.float32),
+            jax.ShapeDtypeStruct((depth, cols), jnp.float32),
             jax.ShapeDtypeStruct((1, own), jnp.float32),
         ],
         compiler_params=pltpu.CompilerParams(vmem_limit_bytes=24 * 1024 * 1024),
         cost_estimate=pl.CostEstimate(
-            flops=128 * depth * members * half,
-            bytes_accessed=members * half * 4 + depth * half * 8,
+            flops=128 * depth * members * cols,
+            bytes_accessed=members * cols * 4 + depth * cols * 4,
             transcendentals=0,
         ),
-    )(place, reward, left, right_left, right_right)
+    )(place, reward, left, right)
 
 
 def local(hidden, weight, left_factors, right_factors, target):
@@ -180,15 +186,15 @@
             low, jnp.concatenate([a, b], axis=axis), jnp.concatenate([b, a], axis=axis)
         )
 
-    near_left, near_right = right_factors[:, :half], right_factors[:, half:]
-    slab_recv = lax.ppermute(
-        jnp.concatenate([other(weight), near_left, near_right], axis=0), "ylo", SWAP
-    )
+    far = other(weight)
+    far = jnp.concatenate([far[: depth // 2], far[depth // 2 :]], axis=1)
+    slab_recv = lax.ppermute(jnp.concatenate([far, right_factors], axis=0), "ylo", SWAP)
+    weight_recv = slab_recv[: depth // 2]
+    weight_recv = jnp.concatenate([weight_recv[:, :half], weight_recv[:, half:]], axis=0)
     packed = jnp.concatenate(
         [
-            order(own(weight), slab_recv[:depth]),
-            order(near_left, slab_recv[depth : depth + members]),
-            order(near_right, slab_recv[depth + members :]),
+            order(own(weight), weight_recv, axis=1),
+            order(right_factors, slab_recv[depth // 2 :]),
         ],
         axis=0,
     )
@@ -197,8 +203,7 @@
     _, hidden_b, left_b, target_b, right_b, slab_b = lax.optimization_barrier(
         (packed, hidden, left_factors, target, right_factors, slab_recv)
     )
-    theirs = jnp.where(low, slab_b[depth : depth + members], slab_b[depth + members :])
-    right_local = jnp.concatenate([own(right_b), theirs], axis=0)
+    right_local = jnp.concatenate([own(right_b), own(slab_b[depth // 2 :])], axis=0)
     rows_recv = lax.ppermute(hidden_b, "ylo", SWAP)
     target_recv = lax.ppermute(other(target_b), "ylo", SWAP)
     projected_own = (
@@ -228,14 +233,13 @@
     )
 
     gathered, part = lax.optimization_barrier((gathered, part))
-    right_left = gathered[:, 2 * depth : 2 * depth + 2 * members]
-    right_right = gathered[:, 2 * depth + 2 * members :]
+    right_all = gathered[:, depth:]
     near = lax.all_to_all(part, ("ylo", "core", "x", "yhi"), 0, 0, tiled=True)
     near = near.reshape(2, 2, 8, 2 * members).sum(axis=(0, 2)).reshape(1, 1, 4 * members)
     reward = lax.all_to_all(jnp.broadcast_to(near, (16, 1, 4 * members)), "z", 0, 0, tiled=True)
     recv = lax.ppermute(send, "ylo", SWAP)
     up_out = order(keep, recv, axis=1)
-    step, fitness = step_product(place, reward, left_all, right_left, right_right, members)
+    step, fitness = step_product(place, reward, left_all, right_all, members)
     return (up_out, step, fitness.reshape(members))
 
 

time: 156 us -> 157 us (level)
  other arithmetic: 5.1 us -> 6.8 us
where the time goes in v7:
time: 157 us; the launch traced here: 156 us
  waiting for transfers between devices  64.7 us (41%)
  starting transfers between devices  39.7 us (25%)
  between operations  14.3 us (9%)
  blocking collectives  14 us (9%)
  Pallas kernels  8.74 us (6%)
  local copies, waits for them, and re-layouts  7.51 us (5%)
  other arithmetic  6.8 us (4%)
    all_gather x1, waiting for transfers between devices, local(): gathered = lax.all_gather(packed, ('z', 'core'), axis=0, tiled=False)  47.1 us
    all_to_all x1, starting transfers between devices, local(): lax.all_to_all(left_split, ('ylo', 'z', 'core'), 0, 0, tiled=True)  18.2 us
    all_to_all x1, blocking collectives, local(): near = lax.all_to_all(part, ('ylo', 'core', 'x', 'yhi'), 0, 0, tiled=True)  14 us
    all_to_all x1, waiting for transfers between devices, local(): lax.all_to_all(jnp.broadcast_to(near, (16, 1, 4 * members)), 'z', 0, 0, t...  7.37 us
    ppermute x1, waiting for transfers between devices, local(): target_recv = lax.ppermute(other(target_b), 'ylo', SWAP)  6.68 us
    all_to_all x1, starting transfers between devices, local(): lax.all_to_all(jnp.broadcast_to(near, (16, 1, 4 * members)), 'z', 0, 0, t...  6.62 us
    pallas_call x1, Pallas kernels, project(): pl.pallas_call(project_kernel, in_specs=[SMEM, ANY, ANY, ANY, VMEM, VMEM]...  6.56 us
    ppermute x1, starting transfers between devices, local(): lax.ppermute(jnp.concatenate([far, right_factors], axis=0), 'ylo', SWAP)  4.03 us
  transfers between devices with their start and end apart: 8, of which 5 were waited for; matrix products, arithmetic and copies ran while one was open for 6% of the time, Pallas kernels for 1%

profile of v7, /device:TPU:1, one launch (start us, length us, event | category | flops | bytes accessed | tf_op | source)
XLA Modules:
  0.0 156.3 jit_solution(13991147349451723090)
XLA Ops:
  7.2 0.0 copy-start
  7.2 0.0 all-gather.3.cloned.1.call-start
  7.2 1.1 broadcast_select_fusion.3
  8.3 0.0 copy-start.3
  8.3 0.8 pad_maximum_fusion.3
  9.1 4.0 %collective-permute-start = (bf16[40,1792]{1,0:T(8,128)(2,1)S(1)}, bf16[40,1792]{1,0:T(8,128)(2,1)S(1)}, u32[]{:S(2)}, u32[]{:S(2)}) collective-permute-start(bf16[40,1792]{1,0:T(8,128)(2,1)S(1)} %pad_maximum_fusion.3), channel_id=1, source_target_pairs={{0,256},{256,0},{1,257},{257,1},{2,258},{258,2},{3,259},{259,3},{4... | collective-permute-start | bytes 430088 | tf_op jit(solution)/shard_map/ppermute | solution.py:191
  13.2 2.5 %collective-permute-done = bf16[40,1792]{1,0:T(8,128)(2,1)S(1)} collective-permute-done((bf16[40,1792]{1,0:T(8,128)(2,1)S(1)}, bf16[40,1792]{1,0:T(8,128)(2,1)S(1)}, u32[]{:S(2)}, u32[]{:S(2)}) %collective-permute-start) | collective-permute-done | bytes 143392 | tf_op jit(solution)/shard_map/ppermute | solution.py:191
  15.6 0.8 maximum_select_fusion.2
  16.5 0.1 maximum_select_fusion.1
  16.6 0.7 pad_maximum_fusion.2
  17.3 0.0 all-gather.3.cloned.1.call-update
  17.3 0.1 pad_add_fusion.place
  17.4 0.0 copy-done
  17.4 0.7 copy.27
  18.1 0.0 copy-start.2
  18.1 3.4 %collective-permute-start.1 = (bf16[128,4096]{0,1:T(8,128)(2,1)S(1)}, bf16[128,4096]{0,1:T(8,128)(2,1)}, u32[]{:S(2)}, u32[]{:S(2)}) collective-permute-start(bf16[128,4096]{0,1:T(8,128)(2,1)S(1)} %copy.27), channel_id=1, source_target_pairs={{0,256},{256,0},{1,257},{257,1},{2,258},{258,2},{3,259},{259,3},{4... | collective-permute-start | bytes 3145736 | tf_op jit(solution)/shard_map/ppermute | solution.py:207
  21.5 0.2 reshape.51
  21.6 0.1 copy.29
  21.7 0.8 reshape.60
  22.5 18.2 %all-to-all-start = ((bf16[64,2,256]{2,1,0:T(2,128)(2,1)}), bf16[64,2,256]{2,1,0:T(2,128)(2,1)S(1)}, u32[]{:S(2)}, u32[]{:S(2)}) async-start(bf16[64,2,256]{2,1,0:T(2,128)(2,1)} %reshape.60), calls=%async_computation | async-start | bytes 131072 | tf_op jit(solution)/shard_map/all_to_all | solution.py:226
  40.7 0.5 fusion
  41.2 0.1 mul.33
  41.3 3.4 %collective-permute-start.3 = (f32[128,1]{0,1:T(1,128)S(1)}, f32[128,1]{0,1:T(1,128)S(1)}, u32[]{:S(2)}, u32[]{:S(2)}) collective-permute-start(f32[128,1]{0,1:T(1,128)S(1)} %mul.33), channel_id=1, source_target_pairs={{0,256},{256,0},{1,257},{257,1},{2,258},{258,2},{3,259},{259,3},{4... | collective-permute-start | bytes 1544 | tf_op jit(solution)/shard_map/ppermute | solution.py:218
  44.7 0.1 broadcast_select_fusion.1
  44.7 1.9 %collective-permute-start.2 = (bf16[128,896]{1,0:T(8,128)(2,1)S(1)}, bf16[128,896]{1,0:T(8,128)(2,1)S(1)}, u32[]{:S(2)}, u32[]{:S(2)}) collective-permute-start(bf16[128,896]{1,0:T(8,128)(2,1)S(1)} %get-tuple-element.32), channel_id=1, source_target_pairs={{0,256},{256,0},{1,257},{257,1},{2,258},{258,2},{3,259},{259,3},{4... | collective-permute-start | bytes 688136 | tf_op jit(solution)/shard_map/ppermute | solution.py:208
  46.7 0.0 copy-done.2
  46.7 0.0 collective-permute-done.3
  46.7 0.1 copy.32.projected
  46.9 6.7 %collective-permute-done.2 = bf16[128,896]{1,0:T(8,128)(2,1)S(1)} collective-permute-done((bf16[128,896]{1,0:T(8,128)(2,1)S(1)}, bf16[128,896]{1,0:T(8,128)(2,1)S(1)}, u32[]{:S(2)}, u32[]{:S(2)}) %collective-permute-start.2) | collective-permute-done | bytes 229408 | tf_op jit(solution)/shard_map/ppermute | solution.py:208
  53.5 0.8 pad_maximum_fusion.1.target_hbm
  54.4 1.1 all-to-all-done
  55.4 0.1 reshape.61
  55.6 0.0 collective-permute-done.1
  55.6 1.5 pad_maximum_fusion
  57.1 0.1 copy.28
  57.2 2.9 %copy.31.hidden_hbm = bf16[256,4096]{1,0:T(8,128)(2,1)} copy(bf16[256,4096]{0,1:T(8,128)(2,1)S(1)} %bitcast.23) | data formatting | bytes 4194304 | tf_op jit(solution)/shard_map/optimization_barrier | solution.py:229
  60.2 47.1 %all-gather.3.cloned.1.call-done = bf16[2560,1792]{1,0:T(8,128)(2,1)} async-done(((bf16[80,1792]{1,0:T(8,128)(2,1)}), bf16[2560,1792]{1,0:T(8,128)(2,1)}) %all-gather.3.cloned.1.call-update) | async-done | bytes 9175056 | tf_op jit(solution)/shard_map/all_gather | solution.py:201
  107.3 6.6 %shard_map.76 = (bf16[128,896]{1,0:T(8,128)(2,1)S(1)}, bf16[128,896]{1,0:T(8,128)(2,1)S(1)}, f32[32,1,16]{2,1,0:T(1,128)S(1)}) custom-call(s32[2]{0:T(128)S(1)} %pad_add_fusion.place, bf16[32,80,1792]{2,1,0:T(8,128)(2,1)} %bitcast.20, bf16[256,4096]{1,0:T(8,128)(2,1)} %copy.31.hidden_hbm, bf16[256,896]{1,0:T(8,128)(2,1)} %pad_maximum_fusion.1.target_hbm, ...), custom_call_target="tpu_custom_call" | custom-call | flops 1879048192 | bytes 7340032 | tf_op jit(solution)/shard_map/pallas_call | solution.py:86
  113.8 14.0 %all_to_all.15 = f32[32,1,16]{2,1,0:T(1,128)S(1)} all-to-all(f32[32,1,16]{2,1,0:T(1,128)S(1)} %get-tuple-element.26), channel_id=1, replica_groups=mesh['ylo'=2,'z'=16,'core'=2,'x'=4,'yhi'=2] {'ylo','core','x','yhi'}, dimensions={0} | all-to-all | bytes 4096 | tf_op jit(solution)/shard_map/all_to_all | solution.py:237
  127.8 0.1 broadcast_in_dim.7
  127.9 0.6 broadcast_in_dim.8
  128.5 6.6 %all-to-all-start.2 = ((f32[16,1,32]{2,1,0:T(1,128)}), f32[16,1,32]{2,1,0:T(1,128)S(1)}, u32[]{:S(2)}, u32[]{:S(2)}) async-start(f32[16,1,32]{2,1,0:T(1,128)} %broadcast_in_dim.8), calls=%async_computation.2 | async-start | bytes 16384 | tf_op jit(solution)/shard_map/all_to_all | solution.py:239
  135.2 1.6 %slice.65.right = bf16[32,16,1792]{2,1,0:T(8,128)(2,1)S(1)} slice(bf16[32,80,1792]{2,1,0:T(8,128)(2,1)} %bitcast.21), slice={[0:32], [64:80], [0:1792]} | slice | bytes 3670016 | tf_op jit(solution)/shard_map/slice | solution.py:236
  136.8 2.2 %collective-permute-start.4 = (bf16[128,896]{1,0:T(8,128)(2,1)S(1)}, bf16[128,896]{1,0:T(8,128)(2,1)S(1)}, u32[]{:S(2)}, u32[]{:S(2)}) collective-permute-start(bf16[128,896]{1,0:T(8,128)(2,1)S(1)} %get-tuple-element.24), channel_id=1, source_target_pairs={{0,256},{256,0},{1,257},{257,1},{2,258},{258,2},{3,259},{259,3},{4... | collective-permute-start | bytes 688136 | tf_op jit(solution)/shard_map/ppermute | solution.py:240
  139.0 7.4 %all-to-all-done.2.reward = f32[16,1,32]{2,1,0:T(1,128)S(1)} async-done(((f32[16,1,32]{2,1,0:T(1,128)}), f32[16,1,32]{2,1,0:T(1,128)S(1)}, u32[]{:S(2)}, u32[]{:S(2)}) %all-to-all-start.2) | async-done | bytes 2080 | tf_op jit(solution)/shard_map/all_to_all | solution.py:239
  146.4 2.2 %shard_map.77 = (f32[64,1792]{1,0:T(8,128)}, f32[1,8]{1,0:T(1,128)}) custom-call(s32[2]{0:T(128)S(1)} %pad_add_fusion.place, f32[16,1,32]{2,1,0:T(1,128)S(1)} %all-to-all-done.2.reward, bf16[512,64]{1,0:T(8,128)(2,1)S(1)} %bitcast.19, bf16[32,16,1792]{2,1,0:T(8,128)(2,1)S(1)} %slice.65.right), custom_call_target="tpu_custom_call" | custom-call | flops 7516192768 | bytes 4128768 | tf_op jit(solution)/shard_map/pallas_call | solution.py:150
  148.6 0.0 collective-permute-done.4
  148.6 0.9 maximum_select_fusion
  (12 shorter events, 0.1 us)
Async XLA Ops:
  7.2 10.2 %copy-start = (bf16[128,4096]{1,0:T(8,128)(2,1)S(1)}, bf16[128,4096]{1,0:T(8,128)(2,1)}, u32[]{:S(2)}) copy-start(bf16[128,4096]{1,0:T(8,128)(2,1)} %param.5) | copy-start | bytes 3145732
  7.2 100.1 %all-gather.3.cloned.1.call-start = ((), (), s32[]{:S(2)}) async-start(), calls=%async_computation.3 | async-start | bytes 9461760 | tf_op jit(solution)/shard_map/all_gather | solution.py:201
  8.3 13.2 %copy-start.3 = (bf16[8,4096]{1,0:T(8,128)(2,1)S(1)}, bf16[8,4096]{1,0:T(8,128)(2,1)}, u32[]{:S(2)}) copy-start(bf16[8,4096]{1,0:T(8,128)(2,1)} %param.7) | copy-start | bytes 196612
  9.1 6.5 %collective-permute-start = (bf16[40,1792]{1,0:T(8,128)(2,1)S(1)}, bf16[40,1792]{1,0:T(8,128)(2,1)S(1)}, u32[]{:S(2)}, u32[]{:S(2)}) collective-permute-start(bf16[40,1792]{1,0:T(8,128)(2,1)S(1)} %pad_maximum_fusion.3), channel_id=1, source_target_pairs={{0,256},{256,0},{1,257},{257,1},{2,258},{258,2},{3,259},{259,3},{4... | collective-permute-start | bytes 430088 | tf_op jit(solution)/shard_map/ppermute | solution.py:191
  17.4 27.2 %copy-start.1 = (bf16[128,1792]{1,0:T(8,128)(2,1)S(1)}, bf16[128,1792]{1,0:T(8,128)(2,1)}, u32[]{:S(2)}) copy-start(bf16[128,1792]{1,0:T(8,128)(2,1)} %param.9) | copy-start | bytes 1376260
  18.1 28.6 %copy-start.2 = (bf16[8,1792]{1,0:T(8,128)(2,1)S(1)}, bf16[8,1792]{1,0:T(8,128)(2,1)}, u32[]{:S(2)}) copy-start(bf16[8,1792]{1,0:T(8,128)(2,1)} %param.8) | copy-start | bytes 86020
  18.1 37.5 %collective-permute-start.1 = (bf16[128,4096]{0,1:T(8,128)(2,1)S(1)}, bf16[128,4096]{0,1:T(8,128)(2,1)}, u32[]{:S(2)}, u32[]{:S(2)}) collective-permute-start(bf16[128,4096]{0,1:T(8,128)(2,1)S(1)} %copy.27), channel_id=1, source_target_pairs={{0,256},{256,0},{1,257},{257,1},{2,258},{258,2},{3,259},{259,3},{4... | collective-permute-start | bytes 3145736 | tf_op jit(solution)/shard_map/ppermute | solution.py:207
  22.5 32.9 %all-to-all-start = ((bf16[64,2,256]{2,1,0:T(2,128)(2,1)}), bf16[64,2,256]{2,1,0:T(2,128)(2,1)S(1)}, u32[]{:S(2)}, u32[]{:S(2)}) async-start(bf16[64,2,256]{2,1,0:T(2,128)(2,1)} %reshape.60), calls=%async_computation | async-start | bytes 131072 | tf_op jit(solution)/shard_map/all_to_all | solution.py:226
  41.3 5.4 %collective-permute-start.3 = (f32[128,1]{0,1:T(1,128)S(1)}, f32[128,1]{0,1:T(1,128)S(1)}, u32[]{:S(2)}, u32[]{:S(2)}) collective-permute-start(f32[128,1]{0,1:T(1,128)S(1)} %mul.33), channel_id=1, source_target_pairs={{0,256},{256,0},{1,257},{257,1},{2,258},{258,2},{3,259},{259,3},{4... | collective-permute-start | bytes 1544 | tf_op jit(solution)/shard_map/ppermute | solution.py:218
  44.7 8.8 %collective-permute-start.2 = (bf16[128,896]{1,0:T(8,128)(2,1)S(1)}, bf16[128,896]{1,0:T(8,128)(2,1)S(1)}, u32[]{:S(2)}, u32[]{:S(2)}) collective-permute-start(bf16[128,896]{1,0:T(8,128)(2,1)S(1)} %get-tuple-element.32), channel_id=1, source_target_pairs={{0,256},{256,0},{1,257},{257,1},{2,258},{258,2},{3,259},{259,3},{4... | collective-permute-start | bytes 688136 | tf_op jit(solution)/shard_map/ppermute | solution.py:208
  128.5 17.9 %all-to-all-start.2 = ((f32[16,1,32]{2,1,0:T(1,128)}), f32[16,1,32]{2,1,0:T(1,128)S(1)}, u32[]{:S(2)}, u32[]{:S(2)}) async-start(f32[16,1,32]{2,1,0:T(1,128)} %broadcast_in_dim.8), calls=%async_computation.2 | async-start | bytes 16384 | tf_op jit(solution)/shard_map/all_to_all | solution.py:239
  136.8 11.8 %collective-permute-start.4 = (bf16[128,896]{1,0:T(8,128)(2,1)S(1)}, bf16[128,896]{1,0:T(8,128)(2,1)S(1)}, u32[]{:S(2)}, u32[]{:S(2)}) collective-permute-start(bf16[128,896]{1,0:T(8,128)(2,1)S(1)} %get-tuple-element.24), channel_id=1, source_target_pairs={{0,256},{256,0},{1,257},{257,1},{2,258},{258,2},{3,259},{259,3},{4... | collective-permute-start | bytes 688136 | tf_op jit(solution)/shard_map/ppermute | solution.py:240
Sparse Core Ops, SparseCore 0:
  17.4 89.7 all-gather.2

commit v8 on v5

--- a/solution.py
+++ b/solution.py
@@ -105,56 +105,63 @@
 def step_kernel(place, reward, left, right_own, right_other, out, fitness):
     members, depth = left.shape
     blocks, _, lanes = reward.shape
-    half = right_own.shape[2]
-    own_at = pl.multiple_of(place[0] * half, 128)
-    other_at = pl.multiple_of((1 - place[0]) * half, 128)
     value = reward[...].reshape(blocks, lanes)
     total = jnp.sum(jnp.sum(value, axis=0, keepdims=True), axis=1, keepdims=True)
     centered = value - total * (1.0 / members)
     squares = jnp.sum(jnp.sum(centered * centered, axis=0, keepdims=True), axis=1, keepdims=True)
     score = centered / jnp.sqrt(squares * (1.0 / members) + spread_eps)
-    shape = (blocks, lanes, lanes)
-    spot = lax.broadcasted_iota(jnp.int32, shape, 1) == lax.broadcasted_iota(jnp.int32, shape, 2)
-    column = jnp.sum(jnp.where(spot, score[:, None, :], 0.0), axis=-1, keepdims=True)
-    column = column.reshape(members, 1)
-    pick = (members, fitness.shape[1])
+    run = fitness.shape[1]
+    shape = (blocks, lanes // 2, lanes)
+    index = lax.broadcasted_iota(jnp.int32, shape, 1)
+    lane = lax.broadcasted_iota(jnp.int32, shape, 2)
+    columns = []
+    for side in (place[0], 1 - place[0]):
+        spot = lane == index + jnp.where(index < run, 0, run) + side * run
+        column = jnp.sum(jnp.where(spot, score[:, None, :], 0.0), axis=-1, keepdims=True)
+        columns.append(column.reshape(members // 2, 1))
+    pick = (members // 2, run)
     mine = lax.broadcasted_iota(jnp.int32, pick, 0) == (
         lax.broadcasted_iota(jnp.int32, pick, 1) + place[1]
     )
-    fitness[...] = jnp.sum(jnp.where(mine, column, 0.0), axis=0, keepdims=True)
-    weighted = left[...].astype(jnp.float32) * column
-    high = weighted.astype(jnp.bfloat16)
-    low = (weighted - high.astype(jnp.float32)).astype(jnp.bfloat16)
-    both = jnp.concatenate([high, low], axis=1)
-
-    def multiply(right, at):
-        product = lax.dot_general(
-            both,
-            right.reshape(members, half),
-            (((0,), (0,)), ((), ())),
-            preferred_element_type=jnp.float32,
-        )
-        out[:, pl.ds(at, half)] = (product[:depth] + product[depth:]) * (1.0 / math.sqrt(members))
-
-    multiply(right_other[...], other_at)
-    multiply(right_own[...], own_at)
+    fitness[...] = jnp.sum(jnp.where(mine, columns[0], 0.0), axis=0, keepdims=True)
+    both = []
+    for side, column in enumerate(columns):
+        rows = left[side * (members // 2) : (side + 1) * (members // 2)]
+        weighted = rows.astype(jnp.float32) * column
+        high = weighted.astype(jnp.bfloat16)
+        low = (weighted - high.astype(jnp.float32)).astype(jnp.bfloat16)
+        both.append(jnp.concatenate([high, low], axis=1))
+    cols = right_own.shape[1]
+    for at in range(0, cols, cols // 2):
+        product = sum(
+            lax.dot_general(
+                factor,
+                right[:, at : at + cols // 2],
+                (((0,), (0,)), ((), ())),
+                preferred_element_type=jnp.float32,
+            )
+            for factor, right in zip(both, (right_own, right_other))
+        )
+        out[:, at : at + cols // 2] = (product[:depth] + product[depth:]) * (
+            1.0 / math.sqrt(members)
+        )
 
 
 def step_product(place, reward, left, right_own, right_other, own):
     members, depth = left.shape
-    half = right_other.shape[2]
+    cols = right_own.shape[1]
     return pl.pallas_call(
         step_kernel,
         in_specs=[SMEM, VMEM, VMEM, VMEM, VMEM],
         out_specs=[VMEM, VMEM],
         out_shape=[
-            jax.ShapeDtypeStruct((depth, 2 * half), jnp.float32),
+            jax.ShapeDtypeStruct((depth, cols), jnp.float32),
             jax.ShapeDtypeStruct((1, own), jnp.float32),
         ],
         compiler_params=pltpu.CompilerParams(vmem_limit_bytes=24 * 1024 * 1024),
         cost_estimate=pl.CostEstimate(
-            flops=128 * depth * members * half,
-            bytes_accessed=members * half * 4 + depth * half * 8,
+            flops=128 * depth * members * cols,
+            bytes_accessed=members * cols * 4 + depth * cols * 4,
             transcendentals=0,
         ),
     )(place, reward, left, right_own, right_other)
@@ -182,21 +189,17 @@
             low, jnp.concatenate([a, b], axis=axis), jnp.concatenate([b, a], axis=axis)
         )
 
-    mine, sent = own(right_factors), other(right_factors)
-    slab_recv = lax.ppermute(
-        jnp.concatenate([other(weight), sent, mine], axis=0), "ylo", SWAP
-    )
-    theirs = slab_recv[depth : depth + members]
-    packed = jnp.concatenate(
-        [order(own(weight), slab_recv[:depth]), order(mine, theirs)], axis=0
-    )
+    weight_recv = lax.ppermute(other(weight), "ylo", SWAP)
+    packed = order(own(weight), weight_recv)
     gathered = lax.all_gather(packed, ("z", "core"), axis=0, tiled=False)
 
-    _, hidden_b, left_b, target_b, sent, slab_b, mine_b = lax.optimization_barrier(
-        (packed, hidden, left_factors, target, sent, slab_recv, mine)
-    )
-    theirs_far = slab_b[depth + members :]
-    right_local = jnp.concatenate([mine_b, slab_b[depth : depth + members]], axis=0)
+    _, hidden_b, left_b, target_b, right_b = lax.optimization_barrier(
+        (packed, hidden, left_factors, target, right_factors)
+    )
+    right_own = lax.all_gather(right_b, ("z", "core"), axis=0, tiled=True)
+    right_other = lax.ppermute(right_own, "ylo", SWAP)
+    right_recv = lax.ppermute(other(right_b), "ylo", SWAP)
+    right_local = jnp.concatenate([own(right_b), right_recv], axis=0)
     rows_recv = lax.ppermute(hidden_b, "ylo", SWAP)
     target_recv = lax.ppermute(other(target_b), "ylo", SWAP)
     projected_own = (
@@ -218,18 +221,13 @@
     left_split = left_b.reshape(members, features // depth, depth).transpose(1, 0, 2)
     left_all = lax.all_to_all(left_split, ("ylo", "z", "core"), 0, 0, tiled=True)
     left_all = left_all.reshape(2, features // (2 * depth), members, depth)
-    left_all = left_all.transpose(1, 0, 2, 3).reshape(-1, depth)
-    far = order(sent, theirs_far)
-    right_other = lax.all_gather(far, ("z", "core"), axis=0, tiled=False)
-
-    hidden_all, left_all, right_other = lax.optimization_barrier((hidden_all, left_all, right_other))
-    place = jnp.stack([ylo, z * 4 * members + core * 2 * members + ylo * members]).astype(jnp.int32)
+    left_all = jnp.where(low, left_all, left_all[::-1]).reshape(-1, depth)
+    hidden_all, left_all, right_own = lax.optimization_barrier((hidden_all, left_all, right_own))
+    place = jnp.stack([ylo, z * 2 * members + core * members]).astype(jnp.int32)
     keep, send, part = project(
         place, gathered, hidden_all, target_all, right_local, projected, 32
     )
 
-    gathered, part = lax.optimization_barrier((gathered, part))
-    right_own = gathered[:, 2 * depth :]
     near = lax.all_to_all(part, ("ylo", "core", "x", "yhi"), 0, 0, tiled=True)
     near = near.reshape(2, 2, 8, 2 * members).sum(axis=(0, 2)).reshape(1, 1, 4 * members)
     reward = lax.all_to_all(jnp.broadcast_to(near, (16, 1, 4 * members)), "z", 0, 0, tiled=True)

time: 157 us -> 153 us (0.975)
  waiting for transfers between devices: 25.2 us -> 15.7 us
  starting transfers between devices: 40.9 us -> 45.3 us
    all_gather x1, waiting for transfers between devices: 13.3 us -> 4.47 us  [local(): gathered = lax.all_gather(packed, ('z', 'core'), axis=0, tiled=False)]
    ppermute x1 -> x3, starting transfers between devices: 4.03 us -> 9.36 us  [the longest x1 4.03 us: local(): weight_recv = lax.ppermute(other(weight), 'ylo', SWAP)]
    select_n x2, other arithmetic: 2.77 us -> 0.75 us  [own(): return jnp.where(low, a[:, :half], a[:, half:])]
    slice x4 -> x0, local copies, waits for them, and re-layouts: 2.01 us -> none  [the longest x1 1.26 us: local(): right_own = gathered[:, 2 * depth:]]
    ppermute x1, waiting for transfers between devices: 1.64 us -> 0.01 us  [local(): projected_recv = lax.ppermute(projected_own, 'ylo', SWAP)]
  transfers between devices with their start and end apart: 8 -> 10, of which waited for: 4 -> 3; matrix products, arithmetic and copies ran while one was open for 8% -> 9% of each run, Pallas kernels for 1% -> 6%
where the time goes in v8:
time: 153 us; the launch traced here: 152 us
  blocking collectives  51.3 us (34%)
  starting transfers between devices  45.3 us (30%)
  waiting for transfers between devices  15.7 us (10%)
  between operations  14.3 us (9%)
  local copies, waits for them, and re-layouts  9.28 us (6%)
  Pallas kernels  8.72 us (6%)
  other arithmetic  6.82 us (4%)
    all_gather x1, blocking collectives, local(): right_own = lax.all_gather(right_b, ('z', 'core'), axis=0, tiled=True)  36.4 us
    all_to_all x1, starting transfers between devices, local(): lax.all_to_all(left_split, ('ylo', 'z', 'core'), 0, 0, tiled=True)  18.7 us
    all_to_all x1, blocking collectives, local(): near = lax.all_to_all(part, ('ylo', 'core', 'x', 'yhi'), 0, 0, tiled=True)  14.9 us
    all_to_all x1, waiting for transfers between devices, local(): lax.all_to_all(jnp.broadcast_to(near, (16, 1, 4 * members)), 'z', 0, 0, t...  8.99 us
    pallas_call x1, Pallas kernels, project(): pl.pallas_call(project_kernel, in_specs=[SMEM, ANY, ANY, ANY, VMEM, VMEM]...  6.5 us
    all_to_all x1, starting transfers between devices, local(): lax.all_to_all(jnp.broadcast_to(near, (16, 1, 4 * members)), 'z', 0, 0, t...  6.33 us
    all_gather x1, waiting for transfers between devices, local(): gathered = lax.all_gather(packed, ('z', 'core'), axis=0, tiled=False)  4.47 us
    optimization_barrier x1, local copies, waits for them, and re-layouts, local(): lax.optimization_barrier((hidden_all, left_all, right_own))  4.14 us
  transfers between devices with their start and end apart: 10, of which 3 were waited for; matrix products, arithmetic and copies ran while one was open for 9% of the time, Pallas kernels for 6%

profile of v8, /device:TPU:1, one launch (start us, length us, event | category | flops | bytes accessed | tf_op | source)
XLA Modules:
  0.0 151.9 jit_solution(17983129777331176548)
XLA Ops:
  7.2 0.0 copy-start
  7.2 0.0 copy-start.2
  7.2 0.0 copy-start.1
  7.2 0.0 all-gather.2.cloned.1.call-start
  7.2 1.1 select_bitcast_fusion
  8.3 4.0 %collective-permute-start = (bf16[64,896]{1,0:T(8,128)(2,1)S(1)}, bf16[64,896]{1,0:T(8,128)(2,1)S(1)}, u32[]{:S(2)}, u32[]{:S(2)}) collective-permute-start(bf16[64,896]{1,0:T(8,128)(2,1)S(1)} %get-tuple-element.30), channel_id=1, source_target_pairs={{0,256},{256,0},{1,257},{257,1},{2,258},{258,2},{3,259},{259,3},{4... | collective-permute-start | bytes 344072 | tf_op jit(solution)/shard_map/ppermute | solution.py:192
  12.4 2.2 %collective-permute-done = bf16[64,896]{1,0:T(8,128)(2,1)S(1)} collective-permute-done((bf16[64,896]{1,0:T(8,128)(2,1)S(1)}, bf16[64,896]{1,0:T(8,128)(2,1)S(1)}, u32[]{:S(2)}, u32[]{:S(2)}) %collective-permute-start) | collective-permute-done | bytes 114720 | tf_op jit(solution)/shard_map/ppermute | solution.py:192
  14.5 0.7 maximum_select_fusion.1
  15.3 0.0 all-gather.2.cloned.1.call-update
  15.3 1.1 reshape.106
  16.4 0.1 copy.27
  16.5 0.8 reshape.114
  17.3 18.7 %all-to-all-start = ((bf16[64,2,256]{2,1,0:T(2,128)(2,1)}), bf16[64,2,256]{2,1,0:T(2,128)(2,1)S(1)}, u32[]{:S(2)}, u32[]{:S(2)}) async-start(bf16[64,2,256]{2,1,0:T(2,128)(2,1)} %reshape.114), calls=%async_computation | async-start | bytes 131072 | tf_op jit(solution)/shard_map/all_to_all | solution.py:222
  36.0 0.0 copy-done
  36.0 0.7 copy.25
  36.7 3.4 %collective-permute-start.1 = (bf16[128,4096]{0,1:T(8,128)(2,1)S(1)}, bf16[128,4096]{0,1:T(8,128)(2,1)}, u32[]{:S(2)}, u32[]{:S(2)}) collective-permute-start(bf16[128,4096]{0,1:T(8,128)(2,1)S(1)} %copy.25), channel_id=1, source_target_pairs={{0,256},{256,0},{1,257},{257,1},{2,258},{258,2},{3,259},{259,3},{4... | collective-permute-start | bytes 3145736 | tf_op jit(solution)/shard_map/ppermute | solution.py:203
  40.1 1.9 %collective-permute-start.3 = (bf16[8,896]{1,0:T(8,128)(2,1)S(1)}, bf16[8,896]{1,0:T(8,128)(2,1)S(1)}, u32[]{:S(2)}, u32[]{:S(2)}) collective-permute-start(bf16[8,896]{1,0:T(8,128)(2,1)S(1)} %get-tuple-element.32), channel_id=1, source_target_pairs={{0,256},{256,0},{1,257},{257,1},{2,258},{258,2},{3,259},{259,3},{4... | collective-permute-start | bytes 43016 | tf_op jit(solution)/shard_map/ppermute | solution.py:201
  42.1 0.7 broadcast_select_fusion.1
  42.8 3.4 %collective-permute-start.2 = (bf16[128,896]{1,0:T(8,128)(2,1)}, bf16[128,896]{1,0:T(8,128)(2,1)}, u32[]{:S(2)}, u32[]{:S(2)}) collective-permute-start(bf16[128,896]{1,0:T(8,128)(2,1)} %get-tuple-element.28), channel_id=1, source_target_pairs={{0,256},{256,0},{1,257},{257,1},{2,258},{258,2},{3,259},{259,3},{4... | collective-permute-start | bytes 688136 | tf_op jit(solution)/shard_map/ppermute | solution.py:204
  46.2 0.5 fusion
  46.7 0.1 mul.28
  46.7 1.9 %collective-permute-start.4 = (f32[128,1]{0,1:T(1,128)S(1)}, f32[128,1]{0,1:T(1,128)S(1)}, u32[]{:S(2)}, u32[]{:S(2)}) collective-permute-start(f32[128,1]{0,1:T(1,128)S(1)} %mul.28), channel_id=1, source_target_pairs={{0,256},{256,0},{1,257},{257,1},{2,258},{258,2},{3,259},{259,3},{4... | collective-permute-start | bytes 1544 | tf_op jit(solution)/shard_map/ppermute | solution.py:214
  48.7 36.4 %all_gather.8.right_own = bf16[256,1792]{1,0:T(8,128)(2,1)S(1)} all-gather(bf16[8,1792]{1,0:T(8,128)(2,1)S(1)} %copy-done.2), channel_id=1, replica_groups=mesh['ylo'=2,'z'=16,'core'=2,'x'=4,'yhi'=2] {'z','core'}, dimensions={0}, use_global_device_ids=true | all-gather | bytes 946176 | tf_op jit(solution)/shard_map/all_gather | solution.py:199
  85.0 3.4 %collective-permute-start.6 = (bf16[256,1792]{1,0:T(8,128)(2,1)S(1)}, bf16[256,1792]{1,0:T(8,128)(2,1)S(1)}, u32[]{:S(2)}, u32[]{:S(2)}) collective-permute-start(bf16[256,1792]{1,0:T(8,128)(2,1)S(1)} %all_gather.8.right_own), channel_id=1, source_target_pairs={{0,256},{256,0},{1,257},{257,1},{2,258},{258,2},{3,259},{259,3},{4... | collective-permute-start | bytes 2752520 | tf_op jit(solution)/shard_map/ppermute | solution.py:200
  88.5 0.1 pad_add_fusion.place
  88.5 0.0 collective-permute-done.4
  88.5 0.1 copy.29.projected
  88.7 0.0 collective-permute-done.3
  88.7 0.0 collective-permute-done.2
  88.7 1.8 %pad_maximum_fusion.1.target_hbm = bf16[256,896]{1,0:T(8,128)(2,1)} fusion(bf16[128,896]{1,0:T(8,128)(2,1)} %collective-permute-done.2, bf16[128,896]{1,0:T(8,128)(2,1)S(1)} %get-tuple-element.27), kind=kLoop, calls=%fused_computation.1 | loop fusion | flops 917504 | bytes 917504 | tf_op jit(solution)/shard_map/concatenate | solution.py:216
  90.5 0.0 all-to-all-done
  90.5 0.1 reshape.115
  90.7 0.0 collective-permute-done.1
  90.7 1.5 pad_maximum_fusion
  92.2 1.4 copy.26
  93.6 4.1 %copy.28.hidden_hbm = bf16[256,4096]{1,0:T(8,128)(2,1)} copy(bf16[256,4096]{0,1:T(8,128)(2,1)} %bitcast.21) | data formatting | bytes 4194304 | tf_op jit(solution)/shard_map/optimization_barrier | solution.py:225
  97.7 4.5 %all-gather.2.cloned.1.call-done.gathered = bf16[32,128,896]{2,1,0:T(8,128)(2,1)} async-done(((bf16[1,128,896]{2,1,0:T(8,128)(2,1)}), bf16[32,128,896]{2,1,0:T(8,128)(2,1)}) %all-gather.2.cloned.1.call-update) | async-done | bytes 7340048 | tf_op jit(solution)/shard_map/all_gather | solution.py:194
  102.2 6.5 %shard_map.76 = (bf16[128,896]{1,0:T(8,128)(2,1)S(1)}, bf16[128,896]{1,0:T(8,128)(2,1)S(1)}, f32[32,1,16]{2,1,0:T(1,128)S(1)}) custom-call(s32[2]{0:T(128)S(1)} %pad_add_fusion.place, bf16[32,128,896]{2,1,0:T(8,128)(2,1)} %all-gather.2.cloned.1.call-done.gathered, bf16[256,4096]{1,0:T(8,128)(2,1)} %copy.28.hidden_hbm, ...), custom_call_target="tpu_custom_call" | custom-call | flops 1879048192 | bytes 7340032 | tf_op jit(solution)/shard_map/pallas_call | solution.py:80
  108.7 14.9 %all_to_all.15 = f32[32,1,16]{2,1,0:T(1,128)S(1)} all-to-all(f32[32,1,16]{2,1,0:T(1,128)S(1)} %get-tuple-element.22), channel_id=1, replica_groups=mesh['ylo'=2,'z'=16,'core'=2,'x'=4,'yhi'=2] {'ylo','core','x','yhi'}, dimensions={0} | all-to-all | bytes 4096 | tf_op jit(solution)/shard_map/all_to_all | solution.py:231
  123.7 0.1 broadcast_in_dim.7
  123.8 0.6 broadcast_in_dim.8
  124.4 6.3 %all-to-all-start.2 = ((f32[16,1,32]{2,1,0:T(1,128)}), f32[16,1,32]{2,1,0:T(1,128)S(1)}, u32[]{:S(2)}, u32[]{:S(2)}) async-start(f32[16,1,32]{2,1,0:T(1,128)} %broadcast_in_dim.8), calls=%async_computation.2 | async-start | bytes 16384 | tf_op jit(solution)/shard_map/all_to_all | solution.py:233
  130.7 2.2 %collective-permute-start.5 = (bf16[128,896]{1,0:T(8,128)(2,1)S(1)}, bf16[128,896]{1,0:T(8,128)(2,1)S(1)}, u32[]{:S(2)}, u32[]{:S(2)}) collective-permute-start(bf16[128,896]{1,0:T(8,128)(2,1)S(1)} %get-tuple-element.21), channel_id=1, source_target_pairs={{0,256},{256,0},{1,257},{257,1},{2,258},{258,2},{3,259},{259,3},{4... | collective-permute-start | bytes 688136 | tf_op jit(solution)/shard_map/ppermute | solution.py:234
  132.9 0.0 collective-permute-done.6.right_other
  132.9 9.0 %all-to-all-done.2.reward = f32[16,1,32]{2,1,0:T(1,128)S(1)} async-done(((f32[16,1,32]{2,1,0:T(1,128)}), f32[16,1,32]{2,1,0:T(1,128)S(1)}, u32[]{:S(2)}, u32[]{:S(2)}) %all-to-all-start.2) | async-done | bytes 2080 | tf_op jit(solution)/shard_map/all_to_all | solution.py:233
  141.9 2.2 %shard_map.77 = (f32[64,1792]{1,0:T(8,128)}, f32[1,8]{1,0:T(1,128)}) custom-call(s32[2]{0:T(128)S(1)} %pad_add_fusion.place, f32[16,1,32]{2,1,0:T(1,128)S(1)} %all-to-all-done.2.reward, bf16[512,64]{1,0:T(8,128)(2,1)S(1)} %bitcast.19, bf16[256,1792]{1,0:T(8,128)(2,1)S(1)} %all_gather.8.right_own, bf16[256,1792]{1,0:T(8,128)(2,1)S(1)} %collective-permute-done.6.right_other), custom_call_target="tpu_custom_call" | custom-call | flops 7516192768 | bytes 4128768 | tf_op jit(solution)/shard_map/pallas_call | solution.py:153
  144.1 0.0 collective-permute-done.5
  144.2 0.9 maximum_select_fusion
  (10 shorter events, 0.1 us)
Async XLA Ops:
  7.2 28.9 %copy-start = (bf16[128,4096]{1,0:T(8,128)(2,1)S(1)}, bf16[128,4096]{1,0:T(8,128)(2,1)}, u32[]{:S(2)}) copy-start(bf16[128,4096]{1,0:T(8,128)(2,1)} %param.5) | copy-start | bytes 3145732
  7.2 32.9 %copy-start.2 = (bf16[8,1792]{1,0:T(8,128)(2,1)S(1)}, bf16[8,1792]{1,0:T(8,128)(2,1)}, u32[]{:S(2)}) copy-start(bf16[8,1792]{1,0:T(8,128)(2,1)} %param.8) | copy-start | bytes 86020
  7.2 34.9 %copy-start.1 = (bf16[128,1792]{1,0:T(8,128)(2,1)S(1)}, bf16[128,1792]{1,0:T(8,128)(2,1)}, u32[]{:S(2)}) copy-start(bf16[128,1792]{1,0:T(8,128)(2,1)} %param.9) | copy-start | bytes 1376260
  7.2 95.0 %all-gather.2.cloned.1.call-start = ((), (), s32[]{:S(2)}) async-start(), calls=%async_computation.3 | async-start | bytes 7569408 | tf_op jit(solution)/shard_map/all_gather | solution.py:194
  8.3 6.2 %collective-permute-start = (bf16[64,896]{1,0:T(8,128)(2,1)S(1)}, bf16[64,896]{1,0:T(8,128)(2,1)S(1)}, u32[]{:S(2)}, u32[]{:S(2)}) collective-permute-start(bf16[64,896]{1,0:T(8,128)(2,1)S(1)} %get-tuple-element.30), channel_id=1, source_target_pairs={{0,256},{256,0},{1,257},{257,1},{2,258},{258,2},{3,259},{259,3},{4... | collective-permute-start | bytes 344072 | tf_op jit(solution)/shard_map/ppermute | solution.py:192
  15.3 30.9 %copy-start.3 = (bf16[8,4096]{1,0:T(8,128)(2,1)S(1)}, bf16[8,4096]{1,0:T(8,128)(2,1)}, u32[]{:S(2)}) copy-start(bf16[8,4096]{1,0:T(8,128)(2,1)} %param.7) | copy-start | bytes 196612
  17.3 73.2 %all-to-all-start = ((bf16[64,2,256]{2,1,0:T(2,128)(2,1)}), bf16[64,2,256]{2,1,0:T(2,128)(2,1)S(1)}, u32[]{:S(2)}, u32[]{:S(2)}) async-start(bf16[64,2,256]{2,1,0:T(2,128)(2,1)} %reshape.114), calls=%async_computation | async-start | bytes 131072 | tf_op jit(solution)/shard_map/all_to_all | solution.py:222
  36.7 54.0 %collective-permute-start.1 = (bf16[128,4096]{0,1:T(8,128)(2,1)S(1)}, bf16[128,4096]{0,1:T(8,128)(2,1)}, u32[]{:S(2)}, u32[]{:S(2)}) collective-permute-start(bf16[128,4096]{0,1:T(8,128)(2,1)S(1)} %copy.25), channel_id=1, source_target_pairs={{0,256},{256,0},{1,257},{257,1},{2,258},{258,2},{3,259},{259,3},{4... | collective-permute-start | bytes 3145736 | tf_op jit(solution)/shard_map/ppermute | solution.py:203
  40.1 48.6 %collective-permute-start.3 = (bf16[8,896]{1,0:T(8,128)(2,1)S(1)}, bf16[8,896]{1,0:T(8,128)(2,1)S(1)}, u32[]{:S(2)}, u32[]{:S(2)}) collective-permute-start(bf16[8,896]{1,0:T(8,128)(2,1)S(1)} %get-tuple-element.32), channel_id=1, source_target_pairs={{0,256},{256,0},{1,257},{257,1},{2,258},{258,2},{3,259},{259,3},{4... | collective-permute-start | bytes 43016 | tf_op jit(solution)/shard_map/ppermute | solution.py:201
  42.8 45.9 %collective-permute-start.2 = (bf16[128,896]{1,0:T(8,128)(2,1)}, bf16[128,896]{1,0:T(8,128)(2,1)}, u32[]{:S(2)}, u32[]{:S(2)}) collective-permute-start(bf16[128,896]{1,0:T(8,128)(2,1)} %get-tuple-element.28), channel_id=1, source_target_pairs={{0,256},{256,0},{1,257},{257,1},{2,258},{258,2},{3,259},{259,3},{4... | collective-permute-start | bytes 688136 | tf_op jit(solution)/shard_map/ppermute | solution.py:204
  46.7 41.8 %collective-permute-start.4 = (f32[128,1]{0,1:T(1,128)S(1)}, f32[128,1]{0,1:T(1,128)S(1)}, u32[]{:S(2)}, u32[]{:S(2)}) collective-permute-start(f32[128,1]{0,1:T(1,128)S(1)} %mul.28), channel_id=1, source_target_pairs={{0,256},{256,0},{1,257},{257,1},{2,258},{258,2},{3,259},{259,3},{4... | collective-permute-start | bytes 1544 | tf_op jit(solution)/shard_map/ppermute | solution.py:214
  85.0 47.9 %collective-permute-start.6 = (bf16[256,1792]{1,0:T(8,128)(2,1)S(1)}, bf16[256,1792]{1,0:T(8,128)(2,1)S(1)}, u32[]{:S(2)}, u32[]{:S(2)}) collective-permute-start(bf16[256,1792]{1,0:T(8,128)(2,1)S(1)} %all_gather.8.right_own), channel_id=1, source_target_pairs={{0,256},{256,0},{1,257},{257,1},{2,258},{258,2},{3,259},{259,3},{4... | collective-permute-start | bytes 2752520 | tf_op jit(solution)/shard_map/ppermute | solution.py:200
  124.4 17.6 %all-to-all-start.2 = ((f32[16,1,32]{2,1,0:T(1,128)}), f32[16,1,32]{2,1,0:T(1,128)S(1)}, u32[]{:S(2)}, u32[]{:S(2)}) async-start(f32[16,1,32]{2,1,0:T(1,128)} %broadcast_in_dim.8), calls=%async_computation.2 | async-start | bytes 16384 | tf_op jit(solution)/shard_map/all_to_all | solution.py:233
  130.7 13.4 %collective-permute-start.5 = (bf16[128,896]{1,0:T(8,128)(2,1)S(1)}, bf16[128,896]{1,0:T(8,128)(2,1)S(1)}, u32[]{:S(2)}, u32[]{:S(2)}) collective-permute-start(bf16[128,896]{1,0:T(8,128)(2,1)S(1)} %get-tuple-element.21), channel_id=1, source_target_pairs={{0,256},{256,0},{1,257},{257,1},{2,258},{258,2},{3,259},{259,3},{4... | collective-permute-start | bytes 688136 | tf_op jit(solution)/shard_map/ppermute | solution.py:234
Sparse Core Ops, SparseCore 0:
  15.4 86.7 all-gather.1

commit v9 on v8

--- a/solution.py
+++ b/solution.py
@@ -197,10 +197,11 @@
         (packed, hidden, left_factors, target, right_factors)
     )
     right_own = lax.all_gather(right_b, ("z", "core"), axis=0, tiled=True)
-    right_other = lax.ppermute(right_own, "ylo", SWAP)
     right_recv = lax.ppermute(other(right_b), "ylo", SWAP)
     right_local = jnp.concatenate([own(right_b), right_recv], axis=0)
     rows_recv = lax.ppermute(hidden_b, "ylo", SWAP)
+    right_own, left_late, rows_recv = lax.optimization_barrier((right_own, left_b, rows_recv))
+    right_other = lax.ppermute(right_own, "ylo", SWAP)
     target_recv = lax.ppermute(other(target_b), "ylo", SWAP)
     projected_own = (
         jnp.einsum(
@@ -218,11 +219,13 @@
     spread_rows = hidden_all.reshape(2 * rows, 2, features // (2 * depth), depth)
     hidden_all = spread_rows.transpose(0, 2, 1, 3).reshape(2 * rows, features)
 
-    left_split = left_b.reshape(members, features // depth, depth).transpose(1, 0, 2)
+    left_split = left_late.reshape(members, features // depth, depth).transpose(1, 0, 2)
     left_all = lax.all_to_all(left_split, ("ylo", "z", "core"), 0, 0, tiled=True)
     left_all = left_all.reshape(2, features // (2 * depth), members, depth)
     left_all = jnp.where(low, left_all, left_all[::-1]).reshape(-1, depth)
-    hidden_all, left_all, right_own = lax.optimization_barrier((hidden_all, left_all, right_own))
+    hidden_all, left_all, right_own, right_other = lax.optimization_barrier(
+        (hidden_all, left_all, right_own, right_other)
+    )
     place = jnp.stack([ylo, z * 2 * members + core * members]).astype(jnp.int32)
     keep, send, part = project(
         place, gathered, hidden_all, target_all, right_local, projected, 32

time: 153 us -> 153 us (level)
  starting transfers between devices: 45.3 us -> 31.5 us
  waiting for transfers between devices: 15.7 us -> 23.2 us
  blocking collectives: 51.3 us -> 58.5 us
    all_to_all x1, waiting for transfers between devices: 0.01 us -> 12 us  [local(): lax.all_to_all(left_split, ('ylo', 'z', 'core'), 0, 0, tiled=True)]
    all_to_all x1, starting transfers between devices: 18.7 us -> 8.06 us  [local(): lax.all_to_all(left_split, ('ylo', 'z', 'core'), 0, 0, tiled=True)]
    all_gather x1, blocking collectives: 36.4 us -> 43.8 us  [local(): right_own = lax.all_gather(right_b, ('z', 'core'), axis=0, tiled=True)]
    all_gather x1, waiting for transfers between devices: 4.47 us -> 0.01 us  [local(): gathered = lax.all_gather(packed, ('z', 'core'), axis=0, tiled=False)]
    all_to_all x1, starting transfers between devices: 6.33 us -> 3.47 us  [local(): lax.all_to_all(jnp.broadcast_to(near, (16, 1, 4 * members)), 'z', 0, 0, t...]
  transfers between devices with their start and end apart: 10 -> 10, of which waited for: 3 -> 3; matrix products, arithmetic and copies ran while one was open for 9% -> 9% of each run, Pallas kernels for 6% -> 1%
where the time goes in v9:
time: 153 us
  blocking collectives  58.5 us (38%)
  starting transfers between devices  31.5 us (21%)
  waiting for transfers between devices  23.2 us (15%)
  between operations  14.3 us (9%)
  local copies, waits for them, and re-layouts  10.3 us (7%)
  Pallas kernels  8.72 us (6%)
  other arithmetic  5.84 us (4%)
    all_gather x1, blocking collectives, local(): right_own = lax.all_gather(right_b, ('z', 'core'), axis=0, tiled=True)  43.8 us
    all_to_all x1, blocking collectives, local(): near = lax.all_to_all(part, ('ylo', 'core', 'x', 'yhi'), 0, 0, tiled=True)  14.8 us
    all_to_all x1, waiting for transfers between devices, local(): lax.all_to_all(left_split, ('ylo', 'z', 'core'), 0, 0, tiled=True)  12 us
    all_to_all x1, waiting for transfers between devices, local(): lax.all_to_all(jnp.broadcast_to(near, (16, 1, 4 * members)), 'z', 0, 0, t...  8.91 us
    all_to_all x1, starting transfers between devices, local(): lax.all_to_all(left_split, ('ylo', 'z', 'core'), 0, 0, tiled=True)  8.06 us
    pallas_call x1, Pallas kernels, project(): pl.pallas_call(project_kernel, in_specs=[SMEM, ANY, ANY, ANY, VMEM, VMEM]...  6.5 us
    optimization_barrier x1, local copies, waits for them, and re-layouts, local(): lax.optimization_barrier((hidden_all, left_all, right_own, right_other))  4.13 us
    ppermute x1, starting transfers between devices, local(): weight_recv = lax.ppermute(other(weight), 'ylo', SWAP)  4.03 us
  transfers between devices with their start and end apart: 10, of which 3 were waited for; matrix products, arithmetic and copies ran while one was open for 9% of the time, Pallas kernels for 1%

profile of v9, /device:TPU:1, one launch (start us, length us, event | category | flops | bytes accessed | tf_op | source)
XLA Modules:
  0.0 152.7 jit_solution(11051855794525106248)
XLA Ops:
  7.2 0.0 copy-start.2
  7.2 0.0 all-gather.2.cloned.1.call-start
  7.2 0.0 copy-start
  7.3 0.0 copy-start.3
  7.3 1.1 select_bitcast_fusion
  8.4 4.0 %collective-permute-start = (bf16[64,896]{1,0:T(8,128)(2,1)S(1)}, bf16[64,896]{1,0:T(8,128)(2,1)S(1)}, u32[]{:S(2)}, u32[]{:S(2)}) collective-permute-start(bf16[64,896]{1,0:T(8,128)(2,1)S(1)} %get-tuple-element.38), channel_id=1, source_target_pairs={{0,256},{256,0},{1,257},{257,1},{2,258},{258,2},{3,259},{259,3},{4... | collective-permute-start | bytes 344072 | tf_op jit(solution)/shard_map/ppermute | solution.py:192
  12.4 2.2 %collective-permute-done = bf16[64,896]{1,0:T(8,128)(2,1)S(1)} collective-permute-done((bf16[64,896]{1,0:T(8,128)(2,1)S(1)}, bf16[64,896]{1,0:T(8,128)(2,1)S(1)}, u32[]{:S(2)}, u32[]{:S(2)}) %collective-permute-start) | collective-permute-done | bytes 114720 | tf_op jit(solution)/shard_map/ppermute | solution.py:192
  14.6 0.7 maximum_select_fusion.1
  15.3 0.0 all-gather.2.cloned.1.call-update
  15.3 1.6 %copy.25 = bf16[128,4096]{0,1:T(8,128)(2,1)S(1)} copy(bf16[128,4096]{1,0:T(8,128)(2,1)} %param.5) | data formatting | bytes 2097152 | tf_op jit(solution)/shard_map/optimization_barrier | solution.py:196
  16.9 3.4 %collective-permute-start.1 = (bf16[128,4096]{0,1:T(8,128)(2,1)S(1)}, bf16[128,4096]{0,1:T(8,128)(2,1)}, u32[]{:S(2)}, u32[]{:S(2)}) collective-permute-start(bf16[128,4096]{0,1:T(8,128)(2,1)S(1)} %copy.25), channel_id=1, source_target_pairs={{0,256},{256,0},{1,257},{257,1},{2,258},{258,2},{3,259},{259,3},{4... | collective-permute-start | bytes 3145736 | tf_op jit(solution)/shard_map/ppermute | solution.py:202
  20.3 1.9 %collective-permute-start.4 = (bf16[8,896]{1,0:T(8,128)(2,1)S(1)}, bf16[8,896]{1,0:T(8,128)(2,1)S(1)}, u32[]{:S(2)}, u32[]{:S(2)}) collective-permute-start(bf16[8,896]{1,0:T(8,128)(2,1)S(1)} %get-tuple-element.40), channel_id=1, source_target_pairs={{0,256},{256,0},{1,257},{257,1},{2,258},{258,2},{3,259},{259,3},{4... | collective-permute-start | bytes 43016 | tf_op jit(solution)/shard_map/ppermute | solution.py:200
  22.3 0.7 broadcast_select_fusion.1
  23.0 3.3 %collective-permute-start.3 = (bf16[128,896]{1,0:T(8,128)(2,1)}, bf16[128,896]{1,0:T(8,128)(2,1)S(1)}, u32[]{:S(2)}, u32[]{:S(2)}) collective-permute-start(bf16[128,896]{1,0:T(8,128)(2,1)} %get-tuple-element.36), channel_id=1, source_target_pairs={{0,256},{256,0},{1,257},{257,1},{2,258},{258,2},{3,259},{259,3},{4... | collective-permute-start | bytes 688136 | tf_op jit(solution)/shard_map/ppermute | solution.py:205
  26.4 0.0 copy-done
  26.4 0.0 copy-done.3
  26.4 0.5 fusion
  26.9 0.1 mul.28
  27.0 1.9 %collective-permute-start.5 = (f32[128,1]{0,1:T(1,128)S(1)}, f32[128,1]{0,1:T(1,128)S(1)}, u32[]{:S(2)}, u32[]{:S(2)}) collective-permute-start(f32[128,1]{0,1:T(1,128)S(1)} %mul.28), channel_id=1, source_target_pairs={{0,256},{256,0},{1,257},{257,1},{2,258},{258,2},{3,259},{259,3},{4... | collective-permute-start | bytes 1544 | tf_op jit(solution)/shard_map/ppermute | solution.py:215
  28.9 43.8 %all_gather.8.right_own = bf16[256,1792]{1,0:T(8,128)(2,1)S(1)} all-gather(bf16[8,1792]{1,0:T(8,128)(2,1)S(1)} %copy-done.2), channel_id=1, replica_groups=mesh['ylo'=2,'z'=16,'core'=2,'x'=4,'yhi'=2] {'z','core'}, dimensions={0}, use_global_device_ids=true | all-gather | bytes 946176 | tf_op jit(solution)/shard_map/all_gather | solution.py:199
  72.7 0.1 pad_add_fusion.place
  72.7 0.0 collective-permute-done.5
  72.7 0.1 copy.29.projected
  72.9 0.0 collective-permute-done.1
  72.9 3.1 %collective-permute-start.2 = (bf16[256,1792]{1,0:T(8,128)(2,1)S(1)}, bf16[256,1792]{1,0:T(8,128)(2,1)S(1)}, u32[]{:S(2)}, u32[]{:S(2)}) collective-permute-start(bf16[256,1792]{1,0:T(8,128)(2,1)S(1)} %all_gather.8.right_own), channel_id=1, source_target_pairs={{0,256},{256,0},{1,257},{257,1},{2,258},{258,2},{3,259},{259,3},{4... | collective-permute-start | bytes 2752520 | tf_op jit(solution)/shard_map/ppermute | solution.py:204
  76.0 0.0 collective-permute-done.4
  76.0 0.0 collective-permute-done.3
  76.0 0.8 pad_maximum_fusion.1.target_hbm
  76.8 1.0 reshape.106
  77.9 0.1 copy.27
  78.0 0.8 reshape.114
  78.8 8.1 %all-to-all-start = ((bf16[64,2,256]{2,1,0:T(2,128)(2,1)}), bf16[64,2,256]{2,1,0:T(2,128)(2,1)S(1)}, u32[]{:S(2)}, u32[]{:S(2)}) async-start(bf16[64,2,256]{2,1,0:T(2,128)(2,1)} %reshape.114), calls=%async_computation | async-start | bytes 131072 | tf_op jit(solution)/shard_map/all_to_all | solution.py:223
  86.8 1.5 pad_maximum_fusion
  88.3 1.5 %copy.26 = bf16[256,32,2,64]{0,3,2,1:T(8,128)(2,1)} copy(bf16[256,32,2,64]{0,3,1,2:T(8,128)(2,1)S(1)} %bitcast.21) | data formatting | bytes 4194304 | tf_op jit(solution)/shard_map/transpose | solution.py:220
  89.8 12.0 %all-to-all-done = bf16[64,2,256]{2,1,0:T(2,128)(2,1)S(1)} async-done(((bf16[64,2,256]{2,1,0:T(2,128)(2,1)}), bf16[64,2,256]{2,1,0:T(2,128)(2,1)S(1)}, u32[]{:S(2)}, u32[]{:S(2)}) %all-to-all-start) | async-done | bytes 65568 | tf_op jit(solution)/shard_map/all_to_all | solution.py:223
  101.9 0.1 reshape.115
  102.1 0.0 collective-permute-done.2.right_other
  102.1 4.1 %copy.28.hidden_hbm = bf16[256,4096]{1,0:T(8,128)(2,1)} copy(bf16[256,4096]{0,1:T(8,128)(2,1)} %bitcast.20) | data formatting | bytes 4194304 | tf_op jit(solution)/shard_map/optimization_barrier | solution.py:226
  106.2 6.5 %shard_map.76 = (bf16[128,896]{1,0:T(8,128)(2,1)S(1)}, bf16[128,896]{1,0:T(8,128)(2,1)S(1)}, f32[32,1,16]{2,1,0:T(1,128)S(1)}) custom-call(s32[2]{0:T(128)S(1)} %pad_add_fusion.place, bf16[32,128,896]{2,1,0:T(8,128)(2,1)} %all-gather.2.cloned.1.call-done.gathered, bf16[256,4096]{1,0:T(8,128)(2,1)} %copy.28.hidden_hbm, ...), custom_call_target="tpu_custom_call" | custom-call | flops 1879048192 | bytes 7340032 | tf_op jit(solution)/shard_map/pallas_call | solution.py:80
  112.7 14.8 %all_to_all.15 = f32[32,1,16]{2,1,0:T(1,128)S(1)} all-to-all(f32[32,1,16]{2,1,0:T(1,128)S(1)} %get-tuple-element.29), channel_id=1, replica_groups=mesh['ylo'=2,'z'=16,'core'=2,'x'=4,'yhi'=2] {'ylo','core','x','yhi'}, dimensions={0} | all-to-all | bytes 4096 | tf_op jit(solution)/shard_map/all_to_all | solution.py:234
  127.5 0.1 broadcast_in_dim.7
  127.6 0.6 broadcast_in_dim.8
  128.2 3.5 %all-to-all-start.2 = ((f32[16,1,32]{2,1,0:T(1,128)}), f32[16,1,32]{2,1,0:T(1,128)S(1)}, u32[]{:S(2)}, u32[]{:S(2)}) async-start(f32[16,1,32]{2,1,0:T(1,128)} %broadcast_in_dim.8), calls=%async_computation.2 | async-start | bytes 16384 | tf_op jit(solution)/shard_map/all_to_all | solution.py:236
  131.7 2.2 %collective-permute-start.6 = (bf16[128,896]{1,0:T(8,128)(2,1)S(1)}, bf16[128,896]{1,0:T(8,128)(2,1)S(1)}, u32[]{:S(2)}, u32[]{:S(2)}) collective-permute-start(bf16[128,896]{1,0:T(8,128)(2,1)S(1)} %get-tuple-element.28), channel_id=1, source_target_pairs={{0,256},{256,0},{1,257},{257,1},{2,258},{258,2},{3,259},{259,3},{4... | collective-permute-start | bytes 688136 | tf_op jit(solution)/shard_map/ppermute | solution.py:237
  133.9 8.9 %all-to-all-done.2.reward = f32[16,1,32]{2,1,0:T(1,128)S(1)} async-done(((f32[16,1,32]{2,1,0:T(1,128)}), f32[16,1,32]{2,1,0:T(1,128)S(1)}, u32[]{:S(2)}, u32[]{:S(2)}) %all-to-all-start.2) | async-done | bytes 2080 | tf_op jit(solution)/shard_map/all_to_all | solution.py:236
  142.8 2.2 %shard_map.77 = (f32[64,1792]{1,0:T(8,128)}, f32[1,8]{1,0:T(1,128)}) custom-call(s32[2]{0:T(128)S(1)} %pad_add_fusion.place, f32[16,1,32]{2,1,0:T(1,128)S(1)} %all-to-all-done.2.reward, bf16[512,64]{1,0:T(8,128)(2,1)S(1)} %bitcast.19, bf16[256,1792]{1,0:T(8,128)(2,1)S(1)} %all_gather.8.right_own, bf16[256,1792]{1,0:T(8,128)(2,1)S(1)} %collective-permute-done.2.right_other), custom_call_target="tpu_custom_call" | custom-call | flops 7516192768 | bytes 4128768 | tf_op jit(solution)/shard_map/pallas_call | solution.py:153
  145.0 0.0 collective-permute-done.6
  145.0 0.9 maximum_select_fusion
  (10 shorter events, 0.1 us)
Async XLA Ops:
  7.2 13.1 %copy-start.2 = (bf16[8,1792]{1,0:T(8,128)(2,1)S(1)}, bf16[8,1792]{1,0:T(8,128)(2,1)}, u32[]{:S(2)}) copy-start(bf16[8,1792]{1,0:T(8,128)(2,1)} %param.8) | copy-start | bytes 86020
  7.2 15.1 %copy-start.1 = (bf16[128,1792]{1,0:T(8,128)(2,1)S(1)}, bf16[128,1792]{1,0:T(8,128)(2,1)}, u32[]{:S(2)}) copy-start(bf16[128,1792]{1,0:T(8,128)(2,1)} %param.9) | copy-start | bytes 1376260
  7.2 99.0 %all-gather.2.cloned.1.call-start = ((), (), s32[]{:S(2)}) async-start(), calls=%async_computation.3 | async-start | bytes 7569408 | tf_op jit(solution)/shard_map/all_gather | solution.py:194
  7.2 19.1 %copy-start = (bf16[128,4096]{1,0:T(8,128)(2,1)S(1)}, bf16[128,4096]{1,0:T(8,128)(2,1)}, u32[]{:S(2)}) copy-start(bf16[128,4096]{1,0:T(8,128)(2,1)} %param.5) | copy-start | bytes 3145732
  7.3 19.1 %copy-start.3 = (bf16[8,4096]{1,0:T(8,128)(2,1)S(1)}, bf16[8,4096]{1,0:T(8,128)(2,1)}, u32[]{:S(2)}) copy-start(bf16[8,4096]{1,0:T(8,128)(2,1)} %param.7) | copy-start | bytes 196612
  8.4 6.2 %collective-permute-start = (bf16[64,896]{1,0:T(8,128)(2,1)S(1)}, bf16[64,896]{1,0:T(8,128)(2,1)S(1)}, u32[]{:S(2)}, u32[]{:S(2)}) collective-permute-start(bf16[64,896]{1,0:T(8,128)(2,1)S(1)} %get-tuple-element.38), channel_id=1, source_target_pairs={{0,256},{256,0},{1,257},{257,1},{2,258},{258,2},{3,259},{259,3},{4... | collective-permute-start | bytes 344072 | tf_op jit(solution)/shard_map/ppermute | solution.py:192
  16.9 56.0 %collective-permute-start.1 = (bf16[128,4096]{0,1:T(8,128)(2,1)S(1)}, bf16[128,4096]{0,1:T(8,128)(2,1)}, u32[]{:S(2)}, u32[]{:S(2)}) collective-permute-start(bf16[128,4096]{0,1:T(8,128)(2,1)S(1)} %copy.25), channel_id=1, source_target_pairs={{0,256},{256,0},{1,257},{257,1},{2,258},{258,2},{3,259},{259,3},{4... | collective-permute-start | bytes 3145736 | tf_op jit(solution)/shard_map/ppermute | solution.py:202
  20.3 55.7 %collective-permute-start.4 = (bf16[8,896]{1,0:T(8,128)(2,1)S(1)}, bf16[8,896]{1,0:T(8,128)(2,1)S(1)}, u32[]{:S(2)}, u32[]{:S(2)}) collective-permute-start(bf16[8,896]{1,0:T(8,128)(2,1)S(1)} %get-tuple-element.40), channel_id=1, source_target_pairs={{0,256},{256,0},{1,257},{257,1},{2,258},{258,2},{3,259},{259,3},{4... | collective-permute-start | bytes 43016 | tf_op jit(solution)/shard_map/ppermute | solution.py:200
  23.0 53.0 %collective-permute-start.3 = (bf16[128,896]{1,0:T(8,128)(2,1)}, bf16[128,896]{1,0:T(8,128)(2,1)S(1)}, u32[]{:S(2)}, u32[]{:S(2)}) collective-permute-start(bf16[128,896]{1,0:T(8,128)(2,1)} %get-tuple-element.36), channel_id=1, source_target_pairs={{0,256},{256,0},{1,257},{257,1},{2,258},{258,2},{3,259},{259,3},{4... | collective-permute-start | bytes 688136 | tf_op jit(solution)/shard_map/ppermute | solution.py:205
  27.0 45.8 %collective-permute-start.5 = (f32[128,1]{0,1:T(1,128)S(1)}, f32[128,1]{0,1:T(1,128)S(1)}, u32[]{:S(2)}, u32[]{:S(2)}) collective-permute-start(f32[128,1]{0,1:T(1,128)S(1)} %mul.28), channel_id=1, source_target_pairs={{0,256},{256,0},{1,257},{257,1},{2,258},{258,2},{3,259},{259,3},{4... | collective-permute-start | bytes 1544 | tf_op jit(solution)/shard_map/ppermute | solution.py:215
  72.9 29.2 %collective-permute-start.2 = (bf16[256,1792]{1,0:T(8,128)(2,1)S(1)}, bf16[256,1792]{1,0:T(8,128)(2,1)S(1)}, u32[]{:S(2)}, u32[]{:S(2)}) collective-permute-start(bf16[256,1792]{1,0:T(8,128)(2,1)S(1)} %all_gather.8.right_own), channel_id=1, source_target_pairs={{0,256},{256,0},{1,257},{257,1},{2,258},{258,2},{3,259},{259,3},{4... | collective-permute-start | bytes 2752520 | tf_op jit(solution)/shard_map/ppermute | solution.py:204
  78.8 23.1 %all-to-all-start = ((bf16[64,2,256]{2,1,0:T(2,128)(2,1)}), bf16[64,2,256]{2,1,0:T(2,128)(2,1)S(1)}, u32[]{:S(2)}, u32[]{:S(2)}) async-start(bf16[64,2,256]{2,1,0:T(2,128)(2,1)} %reshape.114), calls=%async_computation | async-start | bytes 131072 | tf_op jit(solution)/shard_map/all_to_all | solution.py:223
  128.2 14.6 %all-to-all-start.2 = ((f32[16,1,32]{2,1,0:T(1,128)}), f32[16,1,32]{2,1,0:T(1,128)S(1)}, u32[]{:S(2)}, u32[]{:S(2)}) async-start(f32[16,1,32]{2,1,0:T(1,128)} %broadcast_in_dim.8), calls=%async_computation.2 | async-start | bytes 16384 | tf_op jit(solution)/shard_map/all_to_all | solution.py:236
  131.7 13.4 %collective-permute-start.6 = (bf16[128,896]{1,0:T(8,128)(2,1)S(1)}, bf16[128,896]{1,0:T(8,128)(2,1)S(1)}, u32[]{:S(2)}, u32[]{:S(2)}) collective-permute-start(bf16[128,896]{1,0:T(8,128)(2,1)S(1)} %get-tuple-element.28), channel_id=1, source_target_pairs={{0,256},{256,0},{1,257},{257,1},{2,258},{258,2},{3,259},{259,3},{4... | collective-permute-start | bytes 688136 | tf_op jit(solution)/shard_map/ppermute | solution.py:237
Sparse Core Ops, SparseCore 0:
  15.4 88.1 all-gather.1

commit v10 on v8

--- a/solution.py
+++ b/solution.py
@@ -76,7 +76,7 @@
     rows, features = hidden.shape
     members = right.shape[0]
     width = features // blocks
-    slabs = blocks // 8
+    slabs = blocks // 4
     return pl.pallas_call(
         project_kernel,
         in_specs=[SMEM, ANY, ANY, ANY, VMEM, VMEM],

time: 153 us -> 152 us (level)
  no operation moved by 1% of the time
where the time goes in v10:
time: 152 us
  blocking collectives  51.3 us (34%)
  starting transfers between devices  45.3 us (30%)
  waiting for transfers between devices  15.7 us (10%)
  between operations  14.3 us (9%)
  local copies, waits for them, and re-layouts  9.28 us (6%)
  Pallas kernels  8.37 us (6%)
  other arithmetic  6.82 us (4%)
    all_gather x1, blocking collectives, local(): right_own = lax.all_gather(right_b, ('z', 'core'), axis=0, tiled=True)  36.4 us
    all_to_all x1, starting transfers between devices, local(): lax.all_to_all(left_split, ('ylo', 'z', 'core'), 0, 0, tiled=True)  18.7 us
    all_to_all x1, blocking collectives, local(): near = lax.all_to_all(part, ('ylo', 'core', 'x', 'yhi'), 0, 0, tiled=True)  14.9 us
    all_to_all x1, waiting for transfers between devices, local(): lax.all_to_all(jnp.broadcast_to(near, (16, 1, 4 * members)), 'z', 0, 0, t...  8.99 us
    all_to_all x1, starting transfers between devices, local(): lax.all_to_all(jnp.broadcast_to(near, (16, 1, 4 * members)), 'z', 0, 0, t...  6.33 us
    pallas_call x1, Pallas kernels, project(): pl.pallas_call(project_kernel, in_specs=[SMEM, ANY, ANY, ANY, VMEM, VMEM]...  6.15 us
    all_gather x1, waiting for transfers between devices, local(): gathered = lax.all_gather(packed, ('z', 'core'), axis=0, tiled=False)  4.47 us
    optimization_barrier x1, local copies, waits for them, and re-layouts, local(): lax.optimization_barrier((hidden_all, left_all, right_own))  4.14 us
  transfers between devices with their start and end apart: 10, of which 3 were waited for; matrix products, arithmetic and copies ran while one was open for 9% of the time, Pallas kernels for 6%

profile of v10, /device:TPU:1, one launch (start us, length us, event | category | flops | bytes accessed | tf_op | source)
XLA Modules:
  0.0 151.5 jit_solution(14549162030664310886)
XLA Ops:
  7.2 0.0 copy-start
  7.2 0.0 copy-start.2
  7.2 0.0 copy-start.1
  7.2 0.0 all-gather.2.cloned.1.call-start
  7.2 1.1 select_bitcast_fusion
  8.3 4.0 %collective-permute-start = (bf16[64,896]{1,0:T(8,128)(2,1)S(1)}, bf16[64,896]{1,0:T(8,128)(2,1)S(1)}, u32[]{:S(2)}, u32[]{:S(2)}) collective-permute-start(bf16[64,896]{1,0:T(8,128)(2,1)S(1)} %get-tuple-element.30), channel_id=1, source_target_pairs={{0,256},{256,0},{1,257},{257,1},{2,258},{258,2},{3,259},{259,3},{4... | collective-permute-start | bytes 344072 | tf_op jit(solution)/shard_map/ppermute | solution.py:192
  12.4 2.2 %collective-permute-done = bf16[64,896]{1,0:T(8,128)(2,1)S(1)} collective-permute-done((bf16[64,896]{1,0:T(8,128)(2,1)S(1)}, bf16[64,896]{1,0:T(8,128)(2,1)S(1)}, u32[]{:S(2)}, u32[]{:S(2)}) %collective-permute-start) | collective-permute-done | bytes 114720 | tf_op jit(solution)/shard_map/ppermute | solution.py:192
  14.5 0.7 maximum_select_fusion.1
  15.3 0.0 all-gather.2.cloned.1.call-update
  15.3 1.1 reshape.106
  16.4 0.1 copy.27
  16.5 0.8 reshape.114
  17.3 18.7 %all-to-all-start = ((bf16[64,2,256]{2,1,0:T(2,128)(2,1)}), bf16[64,2,256]{2,1,0:T(2,128)(2,1)S(1)}, u32[]{:S(2)}, u32[]{:S(2)}) async-start(bf16[64,2,256]{2,1,0:T(2,128)(2,1)} %reshape.114), calls=%async_computation | async-start | bytes 131072 | tf_op jit(solution)/shard_map/all_to_all | solution.py:222
  36.0 0.0 copy-done
  36.0 0.7 copy.25
  36.7 3.4 %collective-permute-start.1 = (bf16[128,4096]{0,1:T(8,128)(2,1)S(1)}, bf16[128,4096]{0,1:T(8,128)(2,1)}, u32[]{:S(2)}, u32[]{:S(2)}) collective-permute-start(bf16[128,4096]{0,1:T(8,128)(2,1)S(1)} %copy.25), channel_id=1, source_target_pairs={{0,256},{256,0},{1,257},{257,1},{2,258},{258,2},{3,259},{259,3},{4... | collective-permute-start | bytes 3145736 | tf_op jit(solution)/shard_map/ppermute | solution.py:203
  40.1 1.9 %collective-permute-start.3 = (bf16[8,896]{1,0:T(8,128)(2,1)S(1)}, bf16[8,896]{1,0:T(8,128)(2,1)S(1)}, u32[]{:S(2)}, u32[]{:S(2)}) collective-permute-start(bf16[8,896]{1,0:T(8,128)(2,1)S(1)} %get-tuple-element.32), channel_id=1, source_target_pairs={{0,256},{256,0},{1,257},{257,1},{2,258},{258,2},{3,259},{259,3},{4... | collective-permute-start | bytes 43016 | tf_op jit(solution)/shard_map/ppermute | solution.py:201
  42.1 0.7 broadcast_select_fusion.1
  42.8 3.4 %collective-permute-start.2 = (bf16[128,896]{1,0:T(8,128)(2,1)}, bf16[128,896]{1,0:T(8,128)(2,1)}, u32[]{:S(2)}, u32[]{:S(2)}) collective-permute-start(bf16[128,896]{1,0:T(8,128)(2,1)} %get-tuple-element.28), channel_id=1, source_target_pairs={{0,256},{256,0},{1,257},{257,1},{2,258},{258,2},{3,259},{259,3},{4... | collective-permute-start | bytes 688136 | tf_op jit(solution)/shard_map/ppermute | solution.py:204
  46.2 0.5 fusion
  46.7 0.1 mul.28
  46.7 1.9 %collective-permute-start.4 = (f32[128,1]{0,1:T(1,128)S(1)}, f32[128,1]{0,1:T(1,128)S(1)}, u32[]{:S(2)}, u32[]{:S(2)}) collective-permute-start(f32[128,1]{0,1:T(1,128)S(1)} %mul.28), channel_id=1, source_target_pairs={{0,256},{256,0},{1,257},{257,1},{2,258},{258,2},{3,259},{259,3},{4... | collective-permute-start | bytes 1544 | tf_op jit(solution)/shard_map/ppermute | solution.py:214
  48.7 36.4 %all_gather.8.right_own = bf16[256,1792]{1,0:T(8,128)(2,1)S(1)} all-gather(bf16[8,1792]{1,0:T(8,128)(2,1)S(1)} %copy-done.2), channel_id=1, replica_groups=mesh['ylo'=2,'z'=16,'core'=2,'x'=4,'yhi'=2] {'z','core'}, dimensions={0}, use_global_device_ids=true | all-gather | bytes 946176 | tf_op jit(solution)/shard_map/all_gather | solution.py:199
  85.0 3.4 %collective-permute-start.6 = (bf16[256,1792]{1,0:T(8,128)(2,1)S(1)}, bf16[256,1792]{1,0:T(8,128)(2,1)S(1)}, u32[]{:S(2)}, u32[]{:S(2)}) collective-permute-start(bf16[256,1792]{1,0:T(8,128)(2,1)S(1)} %all_gather.8.right_own), channel_id=1, source_target_pairs={{0,256},{256,0},{1,257},{257,1},{2,258},{258,2},{3,259},{259,3},{4... | collective-permute-start | bytes 2752520 | tf_op jit(solution)/shard_map/ppermute | solution.py:200
  88.5 0.1 pad_add_fusion.place
  88.5 0.0 collective-permute-done.4
  88.5 0.1 copy.29.projected
  88.7 0.0 collective-permute-done.3
  88.7 0.0 collective-permute-done.2
  88.7 1.8 %pad_maximum_fusion.1.target_hbm = bf16[256,896]{1,0:T(8,128)(2,1)} fusion(bf16[128,896]{1,0:T(8,128)(2,1)} %collective-permute-done.2, bf16[128,896]{1,0:T(8,128)(2,1)S(1)} %get-tuple-element.27), kind=kLoop, calls=%fused_computation.1 | loop fusion | flops 917504 | bytes 917504 | tf_op jit(solution)/shard_map/concatenate | solution.py:216
  90.5 0.0 all-to-all-done
  90.5 0.1 reshape.115
  90.7 0.0 collective-permute-done.1
  90.7 1.5 pad_maximum_fusion
  92.2 1.4 copy.26
  93.6 4.1 %copy.28.hidden_hbm = bf16[256,4096]{1,0:T(8,128)(2,1)} copy(bf16[256,4096]{0,1:T(8,128)(2,1)} %bitcast.21) | data formatting | bytes 4194304 | tf_op jit(solution)/shard_map/optimization_barrier | solution.py:225
  97.7 4.5 %all-gather.2.cloned.1.call-done.gathered = bf16[32,128,896]{2,1,0:T(8,128)(2,1)} async-done(((bf16[1,128,896]{2,1,0:T(8,128)(2,1)}), bf16[32,128,896]{2,1,0:T(8,128)(2,1)}) %all-gather.2.cloned.1.call-update) | async-done | bytes 7340048 | tf_op jit(solution)/shard_map/all_gather | solution.py:194
  102.2 6.2 %shard_map.76 = (bf16[128,896]{1,0:T(8,128)(2,1)S(1)}, bf16[128,896]{1,0:T(8,128)(2,1)S(1)}, f32[32,1,16]{2,1,0:T(1,128)S(1)}) custom-call(s32[2]{0:T(128)S(1)} %pad_add_fusion.place, bf16[32,128,896]{2,1,0:T(8,128)(2,1)} %all-gather.2.cloned.1.call-done.gathered, bf16[256,4096]{1,0:T(8,128)(2,1)} %copy.28.hidden_hbm, ...), custom_call_target="tpu_custom_call" | custom-call | flops 1879048192 | bytes 7340032 | tf_op jit(solution)/shard_map/pallas_call | solution.py:80
  108.4 14.9 %all_to_all.15 = f32[32,1,16]{2,1,0:T(1,128)S(1)} all-to-all(f32[32,1,16]{2,1,0:T(1,128)S(1)} %get-tuple-element.22), channel_id=1, replica_groups=mesh['ylo'=2,'z'=16,'core'=2,'x'=4,'yhi'=2] {'ylo','core','x','yhi'}, dimensions={0} | all-to-all | bytes 4096 | tf_op jit(solution)/shard_map/all_to_all | solution.py:231
  123.3 0.1 broadcast_in_dim.7
  123.4 0.6 broadcast_in_dim.8
  124.0 6.3 %all-to-all-start.2 = ((f32[16,1,32]{2,1,0:T(1,128)}), f32[16,1,32]{2,1,0:T(1,128)S(1)}, u32[]{:S(2)}, u32[]{:S(2)}) async-start(f32[16,1,32]{2,1,0:T(1,128)} %broadcast_in_dim.8), calls=%async_computation.2 | async-start | bytes 16384 | tf_op jit(solution)/shard_map/all_to_all | solution.py:233
  130.4 2.2 %collective-permute-start.5 = (bf16[128,896]{1,0:T(8,128)(2,1)S(1)}, bf16[128,896]{1,0:T(8,128)(2,1)S(1)}, u32[]{:S(2)}, u32[]{:S(2)}) collective-permute-start(bf16[128,896]{1,0:T(8,128)(2,1)S(1)} %get-tuple-element.21), channel_id=1, source_target_pairs={{0,256},{256,0},{1,257},{257,1},{2,258},{258,2},{3,259},{259,3},{4... | collective-permute-start | bytes 688136 | tf_op jit(solution)/shard_map/ppermute | solution.py:234
  132.6 0.0 collective-permute-done.6.right_other
  132.6 9.0 %all-to-all-done.2.reward = f32[16,1,32]{2,1,0:T(1,128)S(1)} async-done(((f32[16,1,32]{2,1,0:T(1,128)}), f32[16,1,32]{2,1,0:T(1,128)S(1)}, u32[]{:S(2)}, u32[]{:S(2)}) %all-to-all-start.2) | async-done | bytes 2080 | tf_op jit(solution)/shard_map/all_to_all | solution.py:233
  141.6 2.2 %shard_map.77 = (f32[64,1792]{1,0:T(8,128)}, f32[1,8]{1,0:T(1,128)}) custom-call(s32[2]{0:T(128)S(1)} %pad_add_fusion.place, f32[16,1,32]{2,1,0:T(1,128)S(1)} %all-to-all-done.2.reward, bf16[512,64]{1,0:T(8,128)(2,1)S(1)} %bitcast.19, bf16[256,1792]{1,0:T(8,128)(2,1)S(1)} %all_gather.8.right_own, bf16[256,1792]{1,0:T(8,128)(2,1)S(1)} %collective-permute-done.6.right_other), custom_call_target="tpu_custom_call" | custom-call | flops 7516192768 | bytes 4128768 | tf_op jit(solution)/shard_map/pallas_call | solution.py:153
  143.8 0.0 collective-permute-done.5
  143.8 0.9 maximum_select_fusion
  (10 shorter events, 0.1 us)
Async XLA Ops:
  7.2 28.9 %copy-start = (bf16[128,4096]{1,0:T(8,128)(2,1)S(1)}, bf16[128,4096]{1,0:T(8,128)(2,1)}, u32[]{:S(2)}) copy-start(bf16[128,4096]{1,0:T(8,128)(2,1)} %param.5) | copy-start | bytes 3145732
  7.2 32.9 %copy-start.2 = (bf16[8,1792]{1,0:T(8,128)(2,1)S(1)}, bf16[8,1792]{1,0:T(8,128)(2,1)}, u32[]{:S(2)}) copy-start(bf16[8,1792]{1,0:T(8,128)(2,1)} %param.8) | copy-start | bytes 86020
  7.2 34.9 %copy-start.1 = (bf16[128,1792]{1,0:T(8,128)(2,1)S(1)}, bf16[128,1792]{1,0:T(8,128)(2,1)}, u32[]{:S(2)}) copy-start(bf16[128,1792]{1,0:T(8,128)(2,1)} %param.9) | copy-start | bytes 1376260
  7.2 95.0 %all-gather.2.cloned.1.call-start = ((), (), s32[]{:S(2)}) async-start(), calls=%async_computation.3 | async-start | bytes 7569408 | tf_op jit(solution)/shard_map/all_gather | solution.py:194
  8.3 6.2 %collective-permute-start = (bf16[64,896]{1,0:T(8,128)(2,1)S(1)}, bf16[64,896]{1,0:T(8,128)(2,1)S(1)}, u32[]{:S(2)}, u32[]{:S(2)}) collective-permute-start(bf16[64,896]{1,0:T(8,128)(2,1)S(1)} %get-tuple-element.30), channel_id=1, source_target_pairs={{0,256},{256,0},{1,257},{257,1},{2,258},{258,2},{3,259},{259,3},{4... | collective-permute-start | bytes 344072 | tf_op jit(solution)/shard_map/ppermute | solution.py:192
  15.3 30.9 %copy-start.3 = (bf16[8,4096]{1,0:T(8,128)(2,1)S(1)}, bf16[8,4096]{1,0:T(8,128)(2,1)}, u32[]{:S(2)}) copy-start(bf16[8,4096]{1,0:T(8,128)(2,1)} %param.7) | copy-start | bytes 196612
  17.3 73.2 %all-to-all-start = ((bf16[64,2,256]{2,1,0:T(2,128)(2,1)}), bf16[64,2,256]{2,1,0:T(2,128)(2,1)S(1)}, u32[]{:S(2)}, u32[]{:S(2)}) async-start(bf16[64,2,256]{2,1,0:T(2,128)(2,1)} %reshape.114), calls=%async_computation | async-start | bytes 131072 | tf_op jit(solution)/shard_map/all_to_all | solution.py:222
  36.7 54.0 %collective-permute-start.1 = (bf16[128,4096]{0,1:T(8,128)(2,1)S(1)}, bf16[128,4096]{0,1:T(8,128)(2,1)}, u32[]{:S(2)}, u32[]{:S(2)}) collective-permute-start(bf16[128,4096]{0,1:T(8,128)(2,1)S(1)} %copy.25), channel_id=1, source_target_pairs={{0,256},{256,0},{1,257},{257,1},{2,258},{258,2},{3,259},{259,3},{4... | collective-permute-start | bytes 3145736 | tf_op jit(solution)/shard_map/ppermute | solution.py:203
  40.1 48.6 %collective-permute-start.3 = (bf16[8,896]{1,0:T(8,128)(2,1)S(1)}, bf16[8,896]{1,0:T(8,128)(2,1)S(1)}, u32[]{:S(2)}, u32[]{:S(2)}) collective-permute-start(bf16[8,896]{1,0:T(8,128)(2,1)S(1)} %get-tuple-element.32), channel_id=1, source_target_pairs={{0,256},{256,0},{1,257},{257,1},{2,258},{258,2},{3,259},{259,3},{4... | collective-permute-start | bytes 43016 | tf_op jit(solution)/shard_map/ppermute | solution.py:201
  42.8 45.9 %collective-permute-start.2 = (bf16[128,896]{1,0:T(8,128)(2,1)}, bf16[128,896]{1,0:T(8,128)(2,1)}, u32[]{:S(2)}, u32[]{:S(2)}) collective-permute-start(bf16[128,896]{1,0:T(8,128)(2,1)} %get-tuple-element.28), channel_id=1, source_target_pairs={{0,256},{256,0},{1,257},{257,1},{2,258},{258,2},{3,259},{259,3},{4... | collective-permute-start | bytes 688136 | tf_op jit(solution)/shard_map/ppermute | solution.py:204
  46.7 41.8 %collective-permute-start.4 = (f32[128,1]{0,1:T(1,128)S(1)}, f32[128,1]{0,1:T(1,128)S(1)}, u32[]{:S(2)}, u32[]{:S(2)}) collective-permute-start(f32[128,1]{0,1:T(1,128)S(1)} %mul.28), channel_id=1, source_target_pairs={{0,256},{256,0},{1,257},{257,1},{2,258},{258,2},{3,259},{259,3},{4... | collective-permute-start | bytes 1544 | tf_op jit(solution)/shard_map/ppermute | solution.py:214
  85.0 47.5 %collective-permute-start.6 = (bf16[256,1792]{1,0:T(8,128)(2,1)S(1)}, bf16[256,1792]{1,0:T(8,128)(2,1)S(1)}, u32[]{:S(2)}, u32[]{:S(2)}) collective-permute-start(bf16[256,1792]{1,0:T(8,128)(2,1)S(1)} %all_gather.8.right_own), channel_id=1, source_target_pairs={{0,256},{256,0},{1,257},{257,1},{2,258},{258,2},{3,259},{259,3},{4... | collective-permute-start | bytes 2752520 | tf_op jit(solution)/shard_map/ppermute | solution.py:200
  124.0 17.6 %all-to-all-start.2 = ((f32[16,1,32]{2,1,0:T(1,128)}), f32[16,1,32]{2,1,0:T(1,128)S(1)}, u32[]{:S(2)}, u32[]{:S(2)}) async-start(f32[16,1,32]{2,1,0:T(1,128)} %broadcast_in_dim.8), calls=%async_computation.2 | async-start | bytes 16384 | tf_op jit(solution)/shard_map/all_to_all | solution.py:233
  130.4 13.4 %collective-permute-start.5 = (bf16[128,896]{1,0:T(8,128)(2,1)S(1)}, bf16[128,896]{1,0:T(8,128)(2,1)S(1)}, u32[]{:S(2)}, u32[]{:S(2)}) collective-permute-start(bf16[128,896]{1,0:T(8,128)(2,1)S(1)} %get-tuple-element.21), channel_id=1, source_target_pairs={{0,256},{256,0},{1,257},{257,1},{2,258},{258,2},{3,259},{259,3},{4... | collective-permute-start | bytes 688136 | tf_op jit(solution)/shard_map/ppermute | solution.py:234
Sparse Core Ops, SparseCore 0:
  15.4 86.7 all-gather.1
